TPU v7x, 32 devices: a whole 2x2x4 slice. The times are simulated.
32 devices in a mesh: dp: 8 (over z, core), fsdp: 4 (over y, x).
Axes of the slice: x: 2, y: 2, z: 4, core: 2. Of those that a mesh axis runs over, the one named last changes fastest.
Arguments:
- layer_input: bfloat16 [8192, 2048], P(('dp', 'fsdp')), may hold values from -6 to 6
- first_gain: bfloat16 [2048], P(('dp', 'fsdp')), may hold values from 0.099609375 to 1.8984375
- first_shift: bfloat16 [2048], P(('dp', 'fsdp')), may hold values from -1.75 to 1.75
- query_weight: bfloat16 [2048, 2048], P(('dp', 'fsdp')), may hold values from -0.125 to 0.125
- key_weight: bfloat16 [2048, 2048], P(('dp', 'fsdp')), may hold values from -0.125 to 0.125
- value_weight: bfloat16 [2048, 2048], P(('dp', 'fsdp')), may hold values from -0.125 to 0.125
- output_weight: bfloat16 [2048, 2048], P(('dp', 'fsdp')), may hold values from -1.5 to 1.5
- query_bias: bfloat16 [2048], P(('dp', 'fsdp')), may hold values from -1.75 to 1.75
- value_bias: bfloat16 [2048], P(('dp', 'fsdp')), may hold values from -0.3125 to 0.3125
- output_bias: bfloat16 [2048], P(('dp', 'fsdp')), may hold values from -1.75 to 1.75
- second_gain: bfloat16 [2048], P(('dp', 'fsdp')), may hold values from 0.099609375 to 1.8984375
- second_shift: bfloat16 [2048], P(('dp', 'fsdp')), may hold values from -1.75 to 1.75
- up_weight: bfloat16 [2048, 8192], P(('dp', 'fsdp')), may hold values from -0.125 to 0.125
- up_bias: bfloat16 [8192], P(('dp', 'fsdp')), may hold values from -3 to 3
- down_weight: bfloat16 [8192, 2048], P(('dp', 'fsdp')), may hold values from -0.0625 to 0.0625
- down_bias: bfloat16 [2048], P(('dp', 'fsdp')), may hold values from -1.75 to 1.75
- segment_counts: int32 [2], replicated, may hold values from 1 to 4, as said below
- out_grad: bfloat16 [8192, 2048], P(('dp', 'fsdp')), may hold values from -6 to 6
Outputs:
- layer_output: bfloat16 [8192, 2048], P(('dp', 'fsdp'))
- input_grad: float32 [8192, 2048], P(('dp', 'fsdp'))
- grad_first_gain: float32 [2048], P(('dp', 'fsdp'))
- grad_first_shift: float32 [2048], P(('dp', 'fsdp'))
- grad_query_weight: float32 [2048, 2048], P(('dp', 'fsdp'))
- grad_key_weight: float32 [2048, 2048], P(('dp', 'fsdp'))
- grad_value_weight: float32 [2048, 2048], P(('dp', 'fsdp'))
- grad_output_weight: float32 [2048, 2048], P(('dp', 'fsdp'))
- grad_query_bias: float32 [2048], P(('dp', 'fsdp'))
- grad_value_bias: float32 [2048], P(('dp', 'fsdp'))
- grad_output_bias: float32 [2048], P(('dp', 'fsdp'))
- grad_second_gain: float32 [2048], P(('dp', 'fsdp'))
- grad_second_shift: float32 [2048], P(('dp', 'fsdp'))
- grad_up_weight: float32 [2048, 8192], P(('dp', 'fsdp'))
- grad_up_bias: float32 [8192], P(('dp', 'fsdp'))
- grad_down_weight: float32 [8192, 2048], P(('dp', 'fsdp'))
- grad_down_bias: float32 [2048], P(('dp', 'fsdp'))
Inputs may be any that keep to these rules, and one draw needn't show every extreme that they name: `segment_counts`: every document has 1 to 4 segments; in every draw some document has 4.
All inputs are finite; a program needn't handle non-finite values.
Results may differ from a plain program's by a relative error of at most 0.02.
Values may be sent and summed in bfloat16 or wider, within the bound.
A program may use at most 384 MiB of HBM per device.

v0:
```python
import math

import jax
import jax.numpy as jnp
from jax import lax
from jax.sharding import PartitionSpec as P

HEADS = 32
HEAD = 64
SUMM = 50
PREV = 3
MAXSEG = 4
PRE = 150


epsilon = 1e-05
masked = -1e30


def matmul(left_side, right_side):
    return jnp.dot(left_side, right_side, preferred_element_type=jnp.float32)


def contract_rows(left_side, right_side):
    return lax.dot_general(
        left_side, right_side, (((0,), (0,)), ((), ())), preferred_element_type=jnp.float32
    )


def times_transpose(left_side, right_side):
    return lax.dot_general(
        left_side, right_side, (((1,), (1,)), ((), ())), preferred_element_type=jnp.float32
    )


def widen(value):
    return value.astype(jnp.float32)


def gauss_cdf(value):
    return 0.5 * (1.0 + jax.scipy.special.erf(value * 0.7071067811865476))


def gelu_slope(value, cdf_value):
    return cdf_value + value * jnp.exp(-0.5 * value * value) * 0.3989422804014327


def normalize(values, norm_gain, norm_shift):
    center = values - jnp.mean(values, axis=-1, keepdims=True)
    inverse_std = lax.rsqrt(jnp.mean(center * center, axis=-1, keepdims=True) + epsilon)
    unit_rows = center * inverse_std
    return (unit_rows * norm_gain + norm_shift, unit_rows, inverse_std)


def normalize_back(grad_rows, unit_rows, inverse_std, norm_gain):
    scaled = grad_rows * norm_gain
    centered_grad = scaled - jnp.mean(scaled, axis=-1, keepdims=True)
    centered_grad = centered_grad - unit_rows * jnp.mean(scaled * unit_rows, axis=-1, keepdims=True)
    return (
        centered_grad * inverse_std,
        jnp.sum(grad_rows * unit_rows, axis=0),
        jnp.sum(grad_rows, axis=0),
    )


def key_allowed(query_pos, key_pos, place_in_doc, present):
    slot_live = (key_pos >= PRE) | (place_in_doc >= PREV - key_pos // SUMM)
    key_live = present & slot_live
    same_row = key_pos[None, :] == query_pos[:, None]
    return (key_pos[None, :] <= query_pos[:, None]) & (key_live[None, :] | same_row)


def attend_piece(carry_state, pieces, query_heads, query_pos, place_in_doc, present):
    key_rows, value_rows = pieces
    piece_rows = key_rows.shape[0]
    block_width = math.gcd(piece_rows, 512)
    blocks = piece_rows // block_width
    scale_factor = HEAD ** (-0.5)
    key_blocks = key_rows.reshape(blocks, block_width, HEADS, HEAD)
    value_blocks = value_rows.reshape(blocks, block_width, HEADS, HEAD)

    def attend_one_block(fold_state, block_item):
        running_max, row_total, accumulated = fold_state
        key_block, value_block, block_index = block_item
        key_pos = block_index * block_width + jnp.arange(block_width, dtype=jnp.int32)
        scores = (
            jnp.einsum("qhd,khd->hqk", query_heads, key_block, preferred_element_type=jnp.float32)
            * scale_factor
        )
        allowed = key_allowed(query_pos, key_pos, place_in_doc, present)
        scores = jnp.where(allowed[None], scores, masked)
        new_max = jnp.maximum(running_max, jnp.max(scores, axis=-1))
        rescale = jnp.exp(running_max - new_max)
        exp_scores = jnp.exp(scores - new_max[..., None])
        row_total = row_total * rescale + jnp.sum(exp_scores, axis=-1)
        accumulated = accumulated * rescale[..., None] + jnp.einsum(
            "hqk,khd->hqd",
            exp_scores.astype(jnp.bfloat16),
            value_block,
            preferred_element_type=jnp.float32,
        )
        return ((new_max, row_total, accumulated), None)

    fold_state, _ = lax.scan(
        attend_one_block,
        carry_state,
        (key_blocks, value_blocks, jnp.arange(blocks, dtype=jnp.int32)),
    )
    return fold_state


def backward_piece(
    carry_state,
    pieces,
    query_heads,
    grad_heads,
    log_total,
    delta_rows,
    query_pos,
    place_in_doc,
    present,
):
    key_rows, value_rows = pieces
    piece_rows = key_rows.shape[0]
    width_all = key_rows.shape[1]
    block_width = math.gcd(piece_rows, 512)
    blocks = piece_rows // block_width
    scale_factor = HEAD ** (-0.5)
    key_blocks = key_rows.reshape(blocks, block_width, HEADS, HEAD)
    value_blocks = value_rows.reshape(blocks, block_width, HEADS, HEAD)

    def backward_one_block(fold_state, block_item):
        grad_query = fold_state[0]
        key_block, value_block, block_index = block_item
        first_row = block_index * block_width
        key_pos = first_row + jnp.arange(block_width, dtype=jnp.int32)
        scores = (
            jnp.einsum("qhd,khd->hqk", query_heads, key_block, preferred_element_type=jnp.float32)
            * scale_factor
        )
        allowed = key_allowed(query_pos, key_pos, place_in_doc, present)
        scores = jnp.where(allowed[None], scores, masked)
        probabilities = jnp.exp(scores - log_total[..., None])
        grad_prob = jnp.einsum(
            "qhd,khd->hqk", grad_heads, value_block, preferred_element_type=jnp.float32
        )
        grad_scores = (probabilities * (grad_prob - delta_rows[..., None])).astype(jnp.bfloat16)
        grad_query = grad_query + jnp.einsum(
            "hqk,khd->qhd", grad_scores, key_block, preferred_element_type=jnp.float32
        )
        grad_pairs = fold_state[1]
        prob_low = probabilities.astype(jnp.bfloat16)
        grad_key = (
            jnp.einsum("hqk,qhd->khd", grad_scores, query_heads, preferred_element_type=jnp.float32)
            * scale_factor
        )
        grad_value = jnp.einsum(
            "hqk,qhd->khd", prob_low, grad_heads, preferred_element_type=jnp.float32
        )
        update = jnp.stack((grad_key, grad_value), axis=1).reshape(block_width, 2, width_all)
        current = lax.dynamic_slice_in_dim(grad_pairs, first_row, block_width, 0)
        grad_pairs = lax.dynamic_update_slice_in_dim(grad_pairs, current + update, first_row, 0)
        return ((grad_query, grad_pairs), None)

    fold_state, _ = lax.scan(
        backward_one_block,
        carry_state,
        (key_blocks, value_blocks, jnp.arange(blocks, dtype=jnp.int32)),
    )
    return fold_state


def body(
    layer_input,
    first_gain,
    first_shift,
    query_weight,
    key_weight,
    value_weight,
    output_weight,
    query_bias,
    value_bias,
    output_bias,
    second_gain,
    second_shift,
    up_weight,
    up_bias,
    down_weight,
    down_bias,
    segment_counts,
    out_grad,
):
    rows_here = layer_input.shape[0]
    width_all = layer_input.shape[1]
    group_size = lax.axis_size("fsdp")
    segment_rows = rows_here * group_size
    outer_index = lax.axis_index("dp")
    inner_index = lax.axis_index("fsdp")
    place_in_doc = outer_index % MAXSEG
    present = place_in_doc < segment_counts[outer_index // MAXSEG]
    query_pos = inner_index * rows_here + jnp.arange(rows_here, dtype=jnp.int32)
    slot_here = (query_pos >= PRE) | (place_in_doc >= PREV - query_pos // SUMM)
    row_live = (present & slot_here).astype(jnp.float32)
    scale_factor = HEAD ** (-0.5)
    (
        query_full,
        key_full,
        value_full,
        output_full,
        first_gain_low,
        first_shift_low,
        query_bias_low,
        value_bias_low,
        output_bias_low,
    ) = (
        lax.all_gather(query_weight, ("dp", "fsdp"), axis=0, tiled=True),
        lax.all_gather(key_weight, ("dp", "fsdp"), axis=0, tiled=True),
        lax.all_gather(value_weight, ("dp", "fsdp"), axis=0, tiled=True),
        lax.all_gather(output_weight, ("dp", "fsdp"), axis=0, tiled=True),
        lax.all_gather(first_gain, ("dp", "fsdp"), axis=0, tiled=True),
        lax.all_gather(first_shift, ("dp", "fsdp"), axis=0, tiled=True),
        lax.all_gather(query_bias, ("dp", "fsdp"), axis=0, tiled=True),
        lax.all_gather(value_bias, ("dp", "fsdp"), axis=0, tiled=True),
        lax.all_gather(output_bias, ("dp", "fsdp"), axis=0, tiled=True),
    )
    first_gain_full = widen(first_gain_low)
    first_shift_full = widen(first_shift_low)
    query_bias_full = widen(query_bias_low)
    value_bias_full = widen(value_bias_low)
    output_bias_full = widen(output_bias_low)
    layer_rows = layer_input.astype(jnp.float32)
    normed_one, unit_one, inverse_one = normalize(layer_rows, first_gain_full, first_shift_full)
    normed_low = normed_one.astype(jnp.bfloat16)
    query_low = (matmul(normed_low, query_full) + query_bias_full).astype(jnp.bfloat16)
    key_low = matmul(normed_low, key_full).astype(jnp.bfloat16)
    value_low = (matmul(normed_low, value_full) + value_bias_full).astype(jnp.bfloat16)
    query_heads = query_low.reshape(rows_here, HEADS, HEAD)
    start_state = (
        jnp.full((HEADS, rows_here), masked, jnp.float32),
        jnp.zeros((HEADS, rows_here), jnp.float32),
        jnp.zeros((HEADS, rows_here, HEAD), jnp.float32),
    )
    running_max, row_total, accumulated = attend_piece(
        start_state,
        (
            lax.all_gather(key_low, "fsdp", axis=0, tiled=True),
            lax.all_gather(value_low, "fsdp", axis=0, tiled=True),
        ),
        query_heads,
        query_pos,
        place_in_doc,
        present,
    )
    mixed_float = (accumulated / row_total[..., None]).transpose(1, 0, 2)
    log_total = running_max + jnp.log(row_total)
    mixed_low = mixed_float.reshape(rows_here, width_all).astype(jnp.bfloat16)
    after_attention = layer_rows + matmul(mixed_low, output_full) + output_bias_full
    up_full, down_full, second_gain_low, second_shift_low, up_bias_low, down_bias_low = (
        lax.all_gather(up_weight, ("dp", "fsdp"), axis=0, tiled=True),
        lax.all_gather(down_weight, ("dp", "fsdp"), axis=0, tiled=True),
        lax.all_gather(second_gain, ("dp", "fsdp"), axis=0, tiled=True),
        lax.all_gather(second_shift, ("dp", "fsdp"), axis=0, tiled=True),
        lax.all_gather(up_bias, ("dp", "fsdp"), axis=0, tiled=True),
        lax.all_gather(down_bias, ("dp", "fsdp"), axis=0, tiled=True),
    )
    second_gain_full = widen(second_gain_low)
    second_shift_full = widen(second_shift_low)
    up_bias_full = widen(up_bias_low)
    down_bias_full = widen(down_bias_low)
    normed_two, unit_two, inverse_two = normalize(
        after_attention, second_gain_full, second_shift_full
    )
    second_low = normed_two.astype(jnp.bfloat16)
    pre_act = matmul(second_low, up_full) + up_bias_full
    cdf_values = gauss_cdf(pre_act)
    activated = (pre_act * cdf_values).astype(jnp.bfloat16)
    layer_output = (after_attention + matmul(activated, down_full) + down_bias_full).astype(
        jnp.bfloat16
    )
    up_back, down_back, second_gain_again = (
        lax.all_gather(up_weight, ("dp", "fsdp"), axis=0, tiled=True),
        lax.all_gather(down_weight, ("dp", "fsdp"), axis=0, tiled=True),
        lax.all_gather(second_gain, ("dp", "fsdp"), axis=0, tiled=True),
    )
    second_gain_back = widen(second_gain_again)
    grad_out_low = (out_grad.astype(jnp.float32) * row_live[:, None]).astype(jnp.bfloat16)
    grad_down_weight = contract_rows(activated, grad_out_low)
    grad_down_bias = jnp.sum(grad_out_low.astype(jnp.float32), axis=0)
    grad_activated = times_transpose(grad_out_low, down_back)
    grad_pre = (grad_activated * gelu_slope(pre_act, cdf_values)).astype(jnp.bfloat16)
    grad_up_weight = contract_rows(second_low, grad_pre)
    grad_up_bias = jnp.sum(grad_pre.astype(jnp.float32), axis=0)
    grad_second_in = times_transpose(grad_pre, up_back)
    grad_norm_two, grad_second_gain, grad_second_shift = normalize_back(
        grad_second_in, unit_two, inverse_two, second_gain_back
    )
    grad_after = grad_out_low.astype(jnp.float32) + grad_norm_two
    owned_up, owned_up_bias, owned_down, owned_down_bias, owned_second_gain, owned_second_shift = (
        lax.psum_scatter(grad_up_weight, ("dp", "fsdp"), scatter_dimension=0, tiled=True),
        lax.psum_scatter(grad_up_bias, ("dp", "fsdp"), scatter_dimension=0, tiled=True),
        lax.psum_scatter(grad_down_weight, ("dp", "fsdp"), scatter_dimension=0, tiled=True),
        lax.psum_scatter(grad_down_bias, ("dp", "fsdp"), scatter_dimension=0, tiled=True),
        lax.psum_scatter(grad_second_gain, ("dp", "fsdp"), scatter_dimension=0, tiled=True),
        lax.psum_scatter(grad_second_shift, ("dp", "fsdp"), scatter_dimension=0, tiled=True),
    )
    query_back, key_back, value_back, output_back, first_gain_again = (
        lax.all_gather(query_weight, ("dp", "fsdp"), axis=0, tiled=True),
        lax.all_gather(key_weight, ("dp", "fsdp"), axis=0, tiled=True),
        lax.all_gather(value_weight, ("dp", "fsdp"), axis=0, tiled=True),
        lax.all_gather(output_weight, ("dp", "fsdp"), axis=0, tiled=True),
        lax.all_gather(first_gain, ("dp", "fsdp"), axis=0, tiled=True),
    )
    first_gain_back = widen(first_gain_again)
    grad_after_low = grad_after.astype(jnp.bfloat16)
    grad_output_weight = contract_rows(mixed_low, grad_after_low)
    grad_output_bias = jnp.sum(grad_after_low.astype(jnp.float32), axis=0)
    grad_mixed = times_transpose(grad_after_low, output_back).astype(jnp.bfloat16)
    grad_heads = grad_mixed.reshape(rows_here, HEADS, HEAD)
    delta_rows = jnp.sum(grad_heads.astype(jnp.float32) * mixed_float, axis=-1).T
    back_state = (
        jnp.zeros((rows_here, HEADS, HEAD), jnp.float32),
        jnp.zeros((segment_rows, 2, width_all), jnp.float32),
    )
    back_result = backward_piece(
        back_state,
        (
            lax.all_gather(key_low, "fsdp", axis=0, tiled=True),
            lax.all_gather(value_low, "fsdp", axis=0, tiled=True),
        ),
        query_heads,
        grad_heads,
        log_total,
        delta_rows,
        query_pos,
        place_in_doc,
        present,
    )
    grad_query_sum = back_result[0]
    own_pairs = lax.psum_scatter(
        back_result[1].astype(jnp.bfloat16), "fsdp", scatter_dimension=0, tiled=True
    ).astype(jnp.float32)
    grad_key_low = own_pairs[:, 0].astype(jnp.bfloat16)
    grad_value_low = own_pairs[:, 1].astype(jnp.bfloat16)
    grad_query_low = (
        (grad_query_sum * scale_factor).astype(jnp.bfloat16).reshape(rows_here, width_all)
    )
    grad_query_weight = contract_rows(normed_low, grad_query_low)
    grad_key_weight = contract_rows(normed_low, grad_key_low)
    grad_value_weight = contract_rows(normed_low, grad_value_low)
    grad_query_bias = jnp.sum(grad_query_low.astype(jnp.float32), axis=0)
    grad_value_bias = jnp.sum(grad_value_low.astype(jnp.float32), axis=0)
    grad_first_in = (
        times_transpose(grad_query_low, query_back)
        + times_transpose(grad_key_low, key_back)
        + times_transpose(grad_value_low, value_back)
    )
    grad_norm_one, grad_first_gain, grad_first_shift = normalize_back(
        grad_first_in, unit_one, inverse_one, first_gain_back
    )
    keep_rows = (query_pos >= SUMM).astype(jnp.float32)
    input_grad = (grad_after + grad_norm_one) * keep_rows[:, None]
    (
        owned_query,
        owned_key,
        owned_value,
        owned_output,
        owned_first_gain,
        owned_first_shift,
        owned_query_bias,
        owned_value_bias,
        owned_output_bias,
    ) = (
        lax.psum_scatter(grad_query_weight, ("dp", "fsdp"), scatter_dimension=0, tiled=True),
        lax.psum_scatter(grad_key_weight, ("dp", "fsdp"), scatter_dimension=0, tiled=True),
        lax.psum_scatter(grad_value_weight, ("dp", "fsdp"), scatter_dimension=0, tiled=True),
        lax.psum_scatter(grad_output_weight, ("dp", "fsdp"), scatter_dimension=0, tiled=True),
        lax.psum_scatter(grad_first_gain, ("dp", "fsdp"), scatter_dimension=0, tiled=True),
        lax.psum_scatter(grad_first_shift, ("dp", "fsdp"), scatter_dimension=0, tiled=True),
        lax.psum_scatter(grad_query_bias, ("dp", "fsdp"), scatter_dimension=0, tiled=True),
        lax.psum_scatter(grad_value_bias, ("dp", "fsdp"), scatter_dimension=0, tiled=True),
        lax.psum_scatter(grad_output_bias, ("dp", "fsdp"), scatter_dimension=0, tiled=True),
    )
    return (
        layer_output,
        input_grad,
        owned_first_gain,
        owned_first_shift,
        owned_query,
        owned_key,
        owned_value,
        owned_output,
        owned_query_bias,
        owned_value_bias,
        owned_output_bias,
        owned_second_gain,
        owned_second_shift,
        owned_up,
        owned_up_bias,
        owned_down,
        owned_down_bias,
    )


def solution(mesh):
    placed = (
        P(("dp", "fsdp"), None),
        P(("dp", "fsdp")),
        P(("dp", "fsdp")),
        P(("dp", "fsdp"), None),
        P(("dp", "fsdp"), None),
        P(("dp", "fsdp"), None),
        P(("dp", "fsdp"), None),
        P(("dp", "fsdp")),
        P(("dp", "fsdp")),
        P(("dp", "fsdp")),
        P(("dp", "fsdp")),
        P(("dp", "fsdp")),
        P(("dp", "fsdp"), None),
        P(("dp", "fsdp")),
        P(("dp", "fsdp"), None),
        P(("dp", "fsdp")),
        P(),
        P(("dp", "fsdp"), None),
    )
    return jax.shard_map(
        body,
        mesh=mesh,
        in_specs=placed,
        out_specs=(
            P(("dp", "fsdp"), None),
            P(("dp", "fsdp"), None),
            P(("dp", "fsdp")),
            P(("dp", "fsdp")),
            P(("dp", "fsdp"), None),
            P(("dp", "fsdp"), None),
            P(("dp", "fsdp"), None),
            P(("dp", "fsdp"), None),
            P(("dp", "fsdp")),
            P(("dp", "fsdp")),
            P(("dp", "fsdp")),
            P(("dp", "fsdp")),
            P(("dp", "fsdp")),
            P(("dp", "fsdp"), None),
            P(("dp", "fsdp")),
            P(("dp", "fsdp"), None),
            P(("dp", "fsdp")),
        ),
        check_vma=False,
    )
```

profile of v0, /device:TPU:0, one launch (start us, length us, event | category | flops | bytes accessed | tf_op | source)
XLA Modules:
  0.0 5504.1 jit_solution(8804623922125856199)
XLA Ops:
  16.3 43.0 all-reduce.18
  61.2 30.1 all-gather.10.cloned.1.call-done
  98.2 72.2 %all-gather.16.cloned.1.call-done = bf16[2048,2048]{1,0:T(8,128)(2,1)} async-done(((bf16[64,2048]{1,0:T(8,128)(2,1)}), bf16[2048,2048]{1,0:T(8,128)(2,1)}) %all-gather.16.cloned.1.call-update) | async-done | bytes 8388624 | tf_op jit(solution)/shard_map/all_gather | solution.py:218
  179.4 66.9 %all-gather = bf16[32,1,256]{2,1,0:T(2,128)(2,1)S(1)} all-gather(bf16[1,1,256]{2,1,0:T(2,128)(2,1)S(1)} %reshape.344), channel_id=1, replica_groups=mesh['dp'=8,'fsdp'=4] {'dp','fsdp'}, dimensions={0}, use_global_device_ids=true | all-gather | bytes 16896 | tf_op jit(solution)/shard_map/all_gather | solution.py:263
  255.8 47.4 all-gather.12.cloned.1.call-done
  303.2 12.9 reshape.347
  325.8 32.4 all-gather.18.cloned.1.call-done
  380.8 66.8 %while.32 = (s32[]{:T(128)}, f32[32,256]{1,0:T(8,128)S(1)}, f32[32,256]{1,0:T(8,128)S(1)}, f32[32,256,64]{1,2,0:T(8,128)}, s32[2]{0:T(128)S(1)}, /*index=5*/pred...) while((s32[]{:T(128)}, f32[32,256]{1,0:T(8,128)S(1)}, ...), condition=%wide.region_5.6_spmd.clone, body=%wide.region_2.5_spmd.clone.sunk | while | flops 1122025216 | bytes 60824772 | solution.py:104
  457.8 177.0 %all-gather.22.cloned.1.call-done = bf16[2048,8192]{1,0:T(8,128)(2,1)} async-done(((bf16[64,8192]{1,0:T(8,128)(2,1)}), bf16[2048,8192]{1,0:T(8,128)(2,1)}) %all-gather.22.cloned.1.call-update) | async-done | bytes 33554448 | tf_op jit(solution)/shard_map/all_gather | solution.py:259
  634.8 18.7 convolution_add_fusion
  653.5 177.2 %all-gather.24.cloned.1.call-done = bf16[8192,2048]{1,0:T(8,128)(2,1)} async-done(((bf16[256,2048]{1,0:T(8,128)(2,1)}), bf16[8192,2048]{1,0:T(8,128)(2,1)}) %all-gather.24.cloned.1.call-update) | async-done | bytes 33554448 | tf_op jit(solution)/shard_map/all_gather | solution.py:260
  830.7 20.4 convert_reduce_fusion
  851.1 18.7 multiply_reduce_fusion
  893.4 104.8 %while.33 = (s32[]{:T(128)}, f32[256,32,64]{0,2,1:T(8,128)S(1)}, f32[1024,2,2048]{0,2,1:T(8,128)}, bf16[2,512,32,64]{1,3,2,0:T(8,128)(2,1)}, s32[2]{0:T(128)S(1)...) while((s32[]{:T(128)}, f32[256,32,64]{0,2,1:T(8,128)S(1)}, ...), condition=%wide.region_12.13_spmd.clone, body=%wide.region_11.12_spmd.clone.sunk | while | flops 2733121280 | bytes 161979728 | solution.py:165
  1014.4 77.7 %reduce-scatter.8.cloned.1.call-done = bf16[256,2,2048]{0,2,1:T(8,128)(2,1)} async-done(((bf16[1024,2,2048]{0,2,1:T(8,128)(2,1)}), bf16[256,2,2048]{0,2,1:T(8,128)(2,1)}) %reduce-scatter.8.cloned.1.call-update) | async-done | bytes 2097168 | tf_op jit(solution)/shard_map/reduce_scatter | solution.py:339
  1148.2 25.5 fusion.91
  1174.4 27.3 fusion.90
  1202.4 22.9 fusion.68
  1245.8 350.1 %reduce-scatter.10.cloned.1.call-done = f32[64,2048]{1,0:T(8,128)} async-done(((f32[2048,2048]{1,0:T(8,128)}), f32[64,2048]{1,0:T(8,128)}) %reduce-scatter.10.cloned.1.call-update) | async-done | bytes 524304 | tf_op jit(solution)/shard_map/reduce_scatter | solution.py:373
  1595.9 361.8 %reduce-scatter.16.cloned.1.call-done = f32[64,2048]{1,0:T(8,128)} async-done(((f32[2048,2048]{1,0:T(8,128)}), f32[64,2048]{1,0:T(8,128)}) %reduce-scatter.16.cloned.1.call-update) | async-done | bytes 524304 | tf_op jit(solution)/shard_map/reduce_scatter | solution.py:376
  1957.7 362.0 %reduce-scatter.12.cloned.1.call-done = f32[64,2048]{1,0:T(8,128)} async-done(((f32[2048,2048]{1,0:T(8,128)}), f32[64,2048]{1,0:T(8,128)}) %reduce-scatter.12.cloned.1.call-update) | async-done | bytes 524304 | tf_op jit(solution)/shard_map/reduce_scatter | solution.py:374
  2319.7 361.8 %reduce-scatter.14.cloned.1.call-done = f32[64,2048]{1,0:T(8,128)} async-done(((f32[2048,2048]{1,0:T(8,128)}), f32[64,2048]{1,0:T(8,128)}) %reduce-scatter.14.cloned.1.call-update) | async-done | bytes 524304 | tf_op jit(solution)/shard_map/reduce_scatter | solution.py:375
  2681.5 1408.5 %reduce-scatter.18.cloned.1.call-done = f32[64,8192]{1,0:T(8,128)} async-done(((f32[2048,8192]{1,0:T(8,128)}), f32[64,8192]{1,0:T(8,128)}) %reduce-scatter.18.cloned.1.call-update) | async-done | bytes 2097168 | tf_op jit(solution)/shard_map/reduce_scatter | solution.py:299
  4090.0 1407.4 %reduce-scatter.20.cloned.1.call-done = f32[256,2048]{1,0:T(8,128)} async-done(((f32[8192,2048]{1,0:T(8,128)}), f32[256,2048]{1,0:T(8,128)}) %reduce-scatter.20.cloned.1.call-update) | async-done | bytes 2097168 | tf_op jit(solution)/shard_map/reduce_scatter | solution.py:301
  (242 shorter events, 363.3 us)
Async XLA Ops:
  7.2 84.1 %all-gather.10.cloned.1.call-start = ((), (), s32[]{:S(2)}) async-start(), calls=%async_computation.7 | async-start | bytes 8650752 | tf_op jit(solution)/shard_map/all_gather | solution.py:217
  7.9 162.5 %all-gather.16.cloned.1.call-start = ((), (), s32[]{:S(2)}) async-start(), calls=%async_computation.10 | async-start | bytes 8650752 | tf_op jit(solution)/shard_map/all_gather | solution.py:218
  8.7 240.8 %all-gather.14.cloned.1.call-start = ((), (), s32[]{:S(2)}) async-start(), calls=%async_computation.9 | async-start | bytes 8650752 | tf_op jit(solution)/shard_map/all_gather | solution.py:216
  9.4 293.8 %all-gather.12.cloned.1.call-start = ((), (), s32[]{:S(2)}) async-start(), calls=%async_computation.8 | async-start | bytes 5242880 | tf_op jit(solution)/shard_map/all_gather | solution.py:246
  59.3 190.2 %copy-start.23 = (f32[2048]{0:T(1024)}, f32[2048]{0:T(1024)S(1)}, u32[]{:S(2)}) copy-start(f32[2048]{0:T(1024)S(1)} %convert_element_type.143) | copy-start | bytes 24580
  59.3 190.2 %copy-start.19 = (f32[2048]{0:T(1024)}, f32[2048]{0:T(1024)S(1)}, u32[]{:S(2)}) copy-start(f32[2048]{0:T(1024)S(1)} %convert_element_type.142) | copy-start | bytes 24580
  98.1 260.1 %all-gather.18.cloned.1.call-start = ((), (), s32[]{:S(2)}) async-start(), calls=%async_computation.11 | async-start | bytes 5242880 | tf_op jit(solution)/shard_map/all_gather | solution.py:247
  177.2 272.7 %all-gather.20.cloned.1.call-start = ((), (), s32[]{:S(2)}) async-start(), calls=%async_computation.12 | async-start | bytes 8650752 | tf_op jit(solution)/shard_map/all_gather | solution.py:219
  177.7 457.1 %all-gather.22.cloned.1.call-start = ((), (), s32[]{:S(2)}) async-start(), calls=%async_computation.13 | async-start | bytes 34603008 | tf_op jit(solution)/shard_map/all_gather | solution.py:259
  178.5 652.2 %all-gather.24.cloned.1.call-start = ((), (), s32[]{:S(2)}) async-start(), calls=%async_computation.14 | async-start | bytes 34603008 | tf_op jit(solution)/shard_map/all_gather | solution.py:260
  179.2 912.8 %reduce-scatter.8.cloned.1.call-start = ((), (), s32[]{:S(2)}) async-start(), calls=%async_computation.15 | async-start | bytes 10485760 | tf_op jit(solution)/shard_map/reduce_scatter | solution.py:339
  246.3 388.5 %copy-start.21 = (f32[2048]{0:T(1024)}, f32[2048]{0:T(1024)S(1)}, u32[]{:S(2)}) copy-start(f32[2048]{0:T(1024)S(1)} %convert_element_type.154) | copy-start | bytes 24580
  246.4 623.4 %copy-start.17 = (f32[2048]{0:T(1024)}, f32[2048]{0:T(1024)S(1)}, u32[]{:S(2)}) copy-start(f32[2048]{0:T(1024)S(1)} %convert_element_type.153) | copy-start | bytes 24580
  247.7 622.1 %copy-start.33 = (f32[256]{0:T(256)}, f32[256]{0:T(256)S(1)}, u32[]{:S(2)}) copy-start(f32[256]{0:T(256)S(1)} %and_convert_fusion) | copy-start | bytes 3076
  456.1 413.7 %copy-start.25 = (f32[256]{0:T(256)}, f32[256]{0:T(256)S(1)}, u32[]{:S(2)}) copy-start(f32[256]{0:T(256)S(1)} %broadcast_multiply_fusion.4) | copy-start | bytes 3076
  457.8 412.0 %copy-start.31 = (f32[256]{0:T(256)}, f32[256]{0:T(256)S(1)}, u32[]{:S(2)}) copy-start(f32[256]{0:T(256)S(1)} %add_rsqrt_fusion) | copy-start | bytes 3076
  653.5 197.6 %copy-start.5 = (f32[256,2048]{1,0:T(8,128)S(1)}, f32[256,2048]{1,0:T(8,128)}, u32[]{:S(2)}) copy-start(f32[256,2048]{1,0:T(8,128)} %copy-done.4) | copy-start | bytes 6291460
  1007.4 227.0 %all-reduce.21.cloned.1.call-start = ((), (), s32[]{:S(2)}) async-start(), calls=%async_computation.22 | async-start | bytes 196608
  1109.0 486.9 %reduce-scatter.10.cloned.1.call-start = ((), (), s32[]{:S(2)}) async-start(), calls=%async_computation.16 | async-start | bytes 17301504 | tf_op jit(solution)/shard_map/reduce_scatter | solution.py:373
  1117.3 840.4 %reduce-scatter.16.cloned.1.call-start = ((), (), s32[]{:S(2)}) async-start(), calls=%async_computation.19 | async-start | bytes 17301504 | tf_op jit(solution)/shard_map/reduce_scatter | solution.py:376
  1128.2 1191.5 %reduce-scatter.12.cloned.1.call-start = ((), (), s32[]{:S(2)}) async-start(), calls=%async_computation.17 | async-start | bytes 17301504 | tf_op jit(solution)/shard_map/reduce_scatter | solution.py:374
  1138.2 1543.3 %reduce-scatter.14.cloned.1.call-start = ((), (), s32[]{:S(2)}) async-start(), calls=%async_computation.18 | async-start | bytes 17301504 | tf_op jit(solution)/shard_map/reduce_scatter | solution.py:375
  1146.6 2943.4 %reduce-scatter.18.cloned.1.call-start = ((), (), s32[]{:S(2)}) async-start(), calls=%async_computation.20 | async-start | bytes 69206016 | tf_op jit(solution)/shard_map/reduce_scatter | solution.py:299
  1173.7 4323.6 %reduce-scatter.20.cloned.1.call-start = ((), (), s32[]{:S(2)}) async-start(), calls=%async_computation.21 | async-start | bytes 69206016 | tf_op jit(solution)/shard_map/reduce_scatter | solution.py:301
  (33 other events, 646.6 us)
Sparse Core Ops, SparseCore 0:
  10.9 80.3 all-gather.9
  94.2 76.1 all-gather.15
  173.3 76.1 all-gather.13
  251.8 51.3 all-gather.11
  305.4 52.6 all-gather.17
  360.9 77.5 all-gather.19
  441.4 193.3 all-gather.21
  637.7 192.9 all-gather.23
  1007.5 84.5 reduce-scatter.7
  1109.1 125.1 all-reduce.20
  1237.2 358.6 reduce-scatter.9
  1598.6 359.0 reduce-scatter.15
  1960.6 359.0 reduce-scatter.11
  2322.4 359.0 reduce-scatter.13
  2684.3 1405.7 reduce-scatter.17
  4092.8 1404.5 reduce-scatter.19
where the time goes:
time: 5510 us; the launch traced here: 5500 us
  waiting for transfers between devices  4880 us (89%)
  matrix products  353 us (6%)
  blocking collectives  110 us (2%)
  local copies, waits for them, and re-layouts  86 us (2%)
  other arithmetic  58.7 us (1%)
    reduce_scatter x1, waiting for transfers between devices, body(): lax.psum_scatter(grad_up_weight, ('dp', 'fsdp'), scatter_dimension=0, til...  1410 us
    reduce_scatter x1, waiting for transfers between devices, body(): lax.psum_scatter(grad_down_weight, ('dp', 'fsdp'), scatter_dimension=0, t...  1410 us
    reduce_scatter x1, waiting for transfers between devices, body(): lax.psum_scatter(grad_key_weight, ('dp', 'fsdp'), scatter_dimension=0, ti...  362 us
    reduce_scatter x1, waiting for transfers between devices, body(): lax.psum_scatter(grad_output_weight, ('dp', 'fsdp'), scatter_dimension=0,...  362 us
    reduce_scatter x1, waiting for transfers between devices, body(): lax.psum_scatter(grad_value_weight, ('dp', 'fsdp'), scatter_dimension=0,...  362 us
    reduce_scatter x1, waiting for transfers between devices, body(): lax.psum_scatter(grad_query_weight, ('dp', 'fsdp'), scatter_dimension=0,...  350 us
    all_gather x1, waiting for transfers between devices, body(): lax.all_gather(down_weight, ('dp', 'fsdp'), axis=0, tiled=True)  177 us
    all_gather x1, waiting for transfers between devices, body(): lax.all_gather(up_weight, ('dp', 'fsdp'), axis=0, tiled=True)  177 us
  transfers between devices with their start and end apart: 16, of which 15 were waited for; matrix products, arithmetic and copies ran while one was open for 5% of the time, Pallas kernels for 0%

commit v1 on v0

v1 whole, which is shorter than its diff:
```python
import jax
import jax.numpy as jnp
from jax import lax
from jax.sharding import Mesh, PartitionSpec as P

HEADS = 32
HEAD = 64
SUMM = 50
PREV = 3
MAXSEG = 4
PRE = 150

epsilon = 1e-05
masked = -1e30

ALL = ("z", "core", "fsdp")
PLANE = ("core", "fsdp")
bf16 = jnp.bfloat16
f32 = jnp.float32


def dot(a, b, ca, cb):
    return lax.dot_general(a, b, (((ca,), (cb,)), ((), ())), preferred_element_type=f32)


def plane_gather(rows):
    return lax.all_gather(rows, PLANE, axis=0, tiled=True)


def plane_sum(partial):
    return lax.psum_scatter(partial.astype(bf16), PLANE, scatter_dimension=0, tiled=True).astype(f32)


def z_gather(rows):
    return lax.all_gather(rows, "z", axis=0, tiled=True)


def z_sum(partial):
    return lax.psum_scatter(partial.astype(bf16), "z", scatter_dimension=0, tiled=True)


def plane_exchange(blocks):
    return lax.all_to_all(blocks, PLANE, 0, 0, tiled=True)


def gauss_cdf(value):
    return 0.5 * (1.0 + lax.erf(value * 0.7071067811865476))


def gelu_slope(value, cdf_value):
    return cdf_value + value * jnp.exp(-0.5 * value * value) * 0.3989422804014327


def unit_norm(values):
    center = values - jnp.mean(values, axis=-1, keepdims=True)
    inverse_std = lax.rsqrt(jnp.mean(center * center, axis=-1, keepdims=True) + epsilon)
    return center * inverse_std, inverse_std


def normalize_back(grad_rows, unit_rows, inverse_std, norm_gain):
    scaled = grad_rows * norm_gain
    centered = scaled - jnp.mean(scaled, axis=-1, keepdims=True)
    centered = centered - unit_rows * jnp.mean(scaled * unit_rows, axis=-1, keepdims=True)
    return (
        centered * inverse_std,
        jnp.sum(grad_rows * unit_rows, axis=0),
        jnp.sum(grad_rows, axis=0),
    )


def attend(q, k, v, live):
    rows = q.shape[1]
    pos = jnp.arange(rows, dtype=jnp.int32)
    scores = jnp.einsum("sqhd,skhd->shqk", q, k, preferred_element_type=f32) * HEAD**-0.5
    diagonal = pos[None, :] == pos[:, None]
    allowed = (pos[None, :] <= pos[:, None]) & (live[:, None, :] | diagonal)
    scores = jnp.where(allowed[:, None], scores, masked)
    top = jnp.max(scores, axis=-1, keepdims=True)
    powers = jnp.exp(scores - top)
    probs = powers / jnp.sum(powers, axis=-1, keepdims=True)
    mixed = jnp.einsum("shqk,skhd->sqhd", probs.astype(bf16), v, preferred_element_type=f32)
    return probs, mixed


def attend_back(q, k, v, probs, mixed, grad):
    delta = jnp.sum(grad.astype(f32) * mixed, axis=-1).transpose(0, 2, 1)
    grad_probs = jnp.einsum("sqhd,skhd->shqk", grad, v, preferred_element_type=f32)
    grad_scores = (probs * (grad_probs - delta[..., None])).astype(bf16)
    grad_q = jnp.einsum("shqk,skhd->sqhd", grad_scores, k, preferred_element_type=f32)
    grad_k = jnp.einsum("shqk,sqhd->skhd", grad_scores, q, preferred_element_type=f32)
    grad_v = jnp.einsum("shqk,sqhd->skhd", probs.astype(bf16), grad, preferred_element_type=f32)
    scale = HEAD**-0.5
    return (grad_q * scale).astype(bf16), (grad_k * scale).astype(bf16), grad_v.astype(bf16)


def body(
    layer_input,
    first_gain,
    first_shift,
    query_weight,
    key_weight,
    value_weight,
    output_weight,
    query_bias,
    value_bias,
    output_bias,
    second_gain,
    second_shift,
    up_weight,
    up_bias,
    down_weight,
    down_bias,
    segment_counts,
    out_grad,
):
    here, width = layer_input.shape
    wide = up_weight.shape[1]
    planes = lax.axis_size("z")
    group = lax.axis_size("fsdp")
    team = 2 * group
    z_at, core_at, inner_at = (lax.axis_index(name) for name in ALL)
    plane_at = core_at * group + inner_at
    seg_rows = here * group
    own_rows = query_weight.shape[0]
    own_wide = down_weight.shape[0]
    cols = width // team
    heads_here = cols // HEAD
    whole_heads = own_rows % HEAD == 0

    def to_columns(weight, unit):
        cut = weight.reshape(weight.shape[0], planes, team, unit)
        return cut.transpose(2, 0, 1, 3).reshape(team, weight.shape[0], planes * unit)

    def from_columns(blocks, unit):
        rows = blocks.shape[1]
        return blocks.reshape(team, rows, planes, unit).transpose(1, 2, 0, 3).reshape(rows, planes * team * unit)

    def head_columns(weight):
        if whole_heads:
            return to_columns(weight, own_rows)
        return weight.reshape(own_rows, team, cols).transpose(1, 0, 2)

    def head_rows(blocks):
        if whole_heads:
            return from_columns(blocks, own_rows)
        return blocks.transpose(1, 0, 2).reshape(own_rows, width)

    attn_blocks = jnp.concatenate([head_columns(w) for w in (query_weight, key_weight, value_weight)], axis=2)
    attn_cols = plane_exchange(attn_blocks).reshape(team * own_rows, 3 * cols)
    up_cols = plane_exchange(to_columns(up_weight, own_wide)).reshape(team * own_rows, wide // team)
    attn_full = z_gather(attn_cols)
    small = jnp.concatenate(
        [first_gain, first_shift, query_bias, value_bias, output_bias, second_gain, second_shift, down_bias, up_bias]
    )
    small_all = lax.all_gather(small, ALL, axis=0, tiled=False).astype(f32)
    gain_one, shift_one, bias_q, bias_v, bias_o, gain_two, shift_two, bias_down = (
        small_all[:, i * own_rows : (i + 1) * own_rows].reshape(width) for i in range(8)
    )
    bias_up = small_all[:, 8 * own_rows :].reshape(planes, team, own_wide)[:, plane_at].reshape(wide // team)

    def own_columns(bias):
        if whole_heads:
            return bias.reshape(planes, team, own_rows)[:, plane_at].reshape(cols)
        return lax.dynamic_slice_in_dim(bias, plane_at * cols, cols)

    bias_q, bias_v = own_columns(bias_q), own_columns(bias_v)
    if whole_heads:
        out_full = z_gather(output_weight)
    else:
        out_full = lax.dynamic_slice_in_dim(
            lax.all_gather(output_weight, ALL, axis=0, tiled=True), plane_at * cols, cols
        )
    up_full = z_gather(up_cols)
    down_full = z_gather(down_weight)

    segment = 2 * z_at + jnp.arange(2, dtype=jnp.int32)
    place = segment % MAXSEG
    present = place < segment_counts[segment // MAXSEG]
    pos = jnp.arange(seg_rows, dtype=jnp.int32)
    live = present[:, None] & ((pos >= PRE)[None] | (place[:, None] >= PREV - pos[None] // SUMM))
    own_pos = inner_at * here + jnp.arange(here, dtype=jnp.int32)
    live_own = lax.dynamic_slice(live, (core_at, inner_at * here), (1, here))[0]

    all_rows = plane_gather(layer_input).astype(f32)
    normed_low = (unit_norm(all_rows)[0] * gain_one + shift_one).astype(bf16)
    rows_own = layer_input.astype(f32)
    unit_one, inverse_one = unit_norm(rows_own)
    heads = lambda a: a.reshape(2, seg_rows, heads_here, HEAD)
    qkv = dot(normed_low, attn_full, 1, 0)
    qkv = (qkv + jnp.concatenate([bias_q, jnp.zeros_like(bias_q), bias_v])).astype(bf16)
    q, k, v = (heads(qkv[:, i * cols : (i + 1) * cols]) for i in range(3))
    probs, mixed = attend(q, k, v, live)
    mixed_low = mixed.astype(bf16).reshape(2 * seg_rows, cols)
    after = rows_own + plane_sum(dot(mixed_low, out_full, 1, 0)) + bias_o
    unit_two, inverse_two = unit_norm(after)
    second_low = plane_gather((unit_two * gain_two + shift_two).astype(bf16))
    pre_act = dot(second_low, up_full, 1, 0) + bias_up
    cdf = gauss_cdf(pre_act)
    activated = (pre_act * cdf).astype(bf16)
    layer_output = (after + plane_sum(dot(activated, down_full, 1, 0)) + bias_down).astype(bf16)

    out_own = jnp.where(live_own[:, None], out_grad, jnp.zeros_like(out_grad))
    out_live = plane_gather(out_own)
    out_own = out_own.astype(f32)
    grad_down = z_sum(dot(activated, out_live, 0, 0)).astype(f32)
    grad_pre = (dot(out_live, down_full, 1, 1) * gelu_slope(pre_act, cdf)).astype(bf16)
    grad_up = z_sum(dot(second_low, grad_pre, 0, 0)).reshape(team, own_rows, wide // team)
    grad_up = from_columns(plane_exchange(grad_up), own_wide).astype(f32)
    grad_up_bias = jnp.sum(grad_pre.astype(f32), axis=0)
    grad_norm, grad_second_gain, grad_second_shift = normalize_back(
        plane_sum(dot(grad_pre, up_full, 1, 1)), unit_two, inverse_two, gain_two
    )
    grad_after = out_own + grad_norm
    after_low_own = grad_after.astype(bf16)
    grad_output_bias = jnp.sum(after_low_own.astype(f32), axis=0)
    after_low = plane_gather(after_low_own)
    grad_output = dot(mixed_low, after_low, 0, 0)
    if whole_heads:
        grad_output = z_sum(grad_output).astype(f32)
    else:
        spread = jnp.zeros((width, width), bf16)
        spread = lax.dynamic_update_slice_in_dim(spread, grad_output.astype(bf16), plane_at * cols, 0)
        grad_output = lax.psum_scatter(spread, ALL, scatter_dimension=0, tiled=True).astype(f32)
    grad_mixed = heads(dot(after_low, out_full, 1, 1).astype(bf16))
    grad_q, grad_k, grad_v = attend_back(q, k, v, probs, mixed, grad_mixed)
    grad_qkv = jnp.concatenate([a.reshape(2 * seg_rows, cols) for a in (grad_q, grad_k, grad_v)], axis=1)
    grad_attn = z_sum(dot(normed_low, grad_qkv, 0, 0)).reshape(team, own_rows, 3 * cols)
    grad_attn = plane_exchange(grad_attn)
    grad_weights = [head_rows(grad_attn[:, :, i * cols : (i + 1) * cols]).astype(f32) for i in range(3)]
    grad_bias = jnp.sum(grad_qkv.astype(f32), axis=0)
    grad_norm, grad_first_gain, grad_first_shift = normalize_back(
        plane_sum(dot(grad_qkv, attn_full, 1, 1)), unit_one, inverse_one, gain_one
    )
    input_grad = jnp.where((own_pos >= SUMM)[:, None], grad_after + grad_norm, 0.0)

    def spread_columns(bias):
        if whole_heads:
            full = jnp.zeros((planes, team, own_rows), f32)
            return lax.dynamic_update_slice(full, bias.reshape(planes, 1, own_rows), (0, plane_at, 0)).reshape(width)
        return lax.dynamic_update_slice(jnp.zeros((width,), f32), bias, (plane_at * cols,))

    sums = [
        grad_first_gain,
        grad_first_shift,
        spread_columns(grad_bias[:cols]),
        spread_columns(grad_bias[2 * cols :]),
        grad_output_bias,
        grad_second_gain,
        grad_second_shift,
        jnp.sum(out_own, axis=0),
    ]
    up_spread = jnp.zeros((planes, team, own_wide), f32)
    up_spread = lax.dynamic_update_slice(up_spread, grad_up_bias.reshape(planes, 1, own_wide), (0, plane_at, 0))
    packed = jnp.concatenate(
        [a.reshape(planes * team, own_rows) for a in sums] + [up_spread.reshape(planes * team, own_wide)], axis=1
    )
    packed = lax.psum_scatter(packed, ALL, scatter_dimension=0, tiled=False)
    small_grads = [packed[i * own_rows : (i + 1) * own_rows] for i in range(8)]
    return (
        layer_output,
        input_grad,
        small_grads[0],
        small_grads[1],
        *grad_weights,
        grad_output,
        small_grads[2],
        small_grads[3],
        small_grads[4],
        small_grads[5],
        small_grads[6],
        grad_up,
        packed[8 * own_rows :],
        grad_down,
        small_grads[7],
    )


def solution(mesh):
    outer, inner = mesh.devices.shape
    fine = Mesh(mesh.devices.reshape(outer // 2, 2, inner), ALL)
    rows, vector = P(ALL, None), P(ALL)
    return jax.shard_map(
        body,
        mesh=fine,
        in_specs=(
            rows, vector, vector, rows, rows, rows, rows, vector, vector, vector, vector, vector,
            rows, vector, rows, vector, P(), rows,
        ),
        out_specs=(
            rows, rows, vector, vector, rows, rows, rows, rows, vector, vector, vector, vector, vector,
            rows, vector, rows, vector,
        ),
        check_vma=False,
    )
```

time: 5510 us -> 1270 us (0.23)
  waiting for transfers between devices: 4880 us -> 784 us
  matrix products: 353 us -> 215 us
    reduce_scatter x7 -> x8, waiting for transfers between devices: 4330 us -> 370 us  [the longest x4 233 us: plane_sum(): lax.psum_scatter(partial.astype(bf16), PLANE, scatter_dimension=0, tiled=...]
    all_gather x8, waiting for transfers between devices: 538 us -> 291 us  [the longest x4 154 us: z_gather(): return lax.all_gather(rows, 'z', axis=0, tiled=True)]
    dot_general x32 -> x17, matrix products: 353 us -> 195 us  [the longest x12 136 us: dot(): lax.dot_general(a, b, (((ca,), (cb,)), ((), ())), preferred_element_type=...]
    unnamed x17 -> x18, waiting for transfers between devices: 8.88 us -> 123 us
  transfers between devices with their start and end apart: 16 -> 19, of which waited for: 15 -> 14; matrix products, arithmetic and copies ran while one was open for 5% -> 23% of each run, Pallas kernels for 0% -> 0%
where the time goes in v1:
time: 1270 us; the launch traced here: 1260 us
  waiting for transfers between devices  784 us (62%)
  matrix products  215 us (17%)
  blocking collectives  112 us (9%)
  local copies, waits for them, and re-layouts  63.1 us (5%)
  other arithmetic  62.6 us (5%)
  between operations  15.2 us (1%)
    reduce_scatter x4, waiting for transfers between devices, plane_sum(): lax.psum_scatter(partial.astype(bf16), PLANE, scatter_dimension=0, tiled=...  233 us
    all_gather x4, waiting for transfers between devices, z_gather(): return lax.all_gather(rows, 'z', axis=0, tiled=True)  154 us
    reduce_scatter x4, waiting for transfers between devices, z_sum(): lax.psum_scatter(partial.astype(bf16), 'z', scatter_dimension=0, tiled=True)  137 us
    all_gather x4, waiting for transfers between devices, plane_gather(): return lax.all_gather(rows, PLANE, axis=0, tiled=True)  137 us
    dot_general x12, matrix products, dot(): lax.dot_general(a, b, (((ca,), (cb,)), ((), ())), preferred_element_type=...  136 us
    unnamed x18, waiting for transfers between devices  123 us
    all_gather x1, blocking collectives, body(): small_all = lax.all_gather(small, ALL, axis=0, tiled=False).astype(f32)  69.1 us
    all_to_all x2, blocking collectives, plane_exchange(): return lax.all_to_all(blocks, PLANE, 0, 0, tiled=True)  42.5 us
  transfers between devices with their start and end apart: 19, of which 14 were waited for; matrix products, arithmetic and copies ran while one was open for 23% of the time, Pallas kernels for 0%

profile of v1, /device:TPU:0, one launch (start us, length us, event | category | flops | bytes accessed | tf_op | source)
XLA Modules:
  0.0 1259.8 jit_solution(11762769625896418298)
XLA Ops:
  13.3 23.8 %all_to_all.20 = bf16[8,64,768]{2,1,0:T(8,128)(2,1)} all-to-all(bf16[8,64,768]{2,1,0:T(8,128)(2,1)S(1)} %pad_maximum_fusion), channel_id=1, replica_groups=mesh['z'=4,'core'=2,'fsdp'=4] {'core','fsdp'}, dimensions={0} | all-to-all | bytes 1572864 | tf_op jit(solution)/shard_map/all_to_all | solution.py:43
  38.8 69.1 %all-gather.1 = bf16[32,1,768]{2,1,0:T(2,128)(2,1)S(1)} all-gather(bf16[1,1,768]{2,1,0:T(2,128)(2,1)S(1)} %reshape.475), channel_id=2, replica_groups=mesh['z'=4,'core'=2,'fsdp'=4] {'z','core','fsdp'}, dimensions={0}, use_global_device_ids=true | all-gather | bytes 50688 | tf_op jit(solution)/shard_map/all_gather | solution.py:155
  158.7 19.7 %fusion.58 = (f32[2,4,1024]{2,1,0:T(4,128)S(1)}, f32[2,4,1024,1024]{2,3,1,0:T(8,128)}) fusion(pred[2,1024,1024]{1,2,0:T(8,128)(4,1)} %or_and_fusion, bf16[2,1024,4,64]{1,3,2,0:T(8,128)(2,1)} %copy.86, bf16[2,1024,4,64]{1,3,2,0:T(8,128)(2,1)S(1)} %copy.87), kind=kOutput, calls=%fused_computation.161 | convolution fusion | flops 1107297280 | bytes 37781504 | tf_op jit(solution)/shard_map/sub | solution.py:79
  178.4 17.8 %fusion.11 = bf16[2,4,1024,1024]{2,3,1,0:T(8,128)(2,1)} fusion(f32[2,4,1024,1024]{2,3,1,0:T(8,128)} %get-tuple-element.58, f32[2,4,1024]{2,1,0:T(4,128)S(1)} %get-tuple-element.57), kind=kLoop, calls=%fused_computation.18 | loop fusion | flops 16777216 | bytes 50364416 | tf_op jit(solution)/shard_map/convert_element_type | solution.py:81
  220.5 18.7 %all_to_all.21 = bf16[8,64,1024]{2,1,0:T(8,128)(2,1)} all-to-all(bf16[8,64,1024]{2,1,0:T(8,128)(2,1)S(1)} %reshape.438), channel_id=1, replica_groups=mesh['z'=4,'core'=2,'fsdp'=4] {'core','fsdp'}, dimensions={0} | all-to-all | bytes 2097152 | tf_op jit(solution)/shard_map/all_to_all | solution.py:43
  239.5 48.5 %reduce-scatter.9.cloned.1.call-done = bf16[256,2048]{1,0:T(8,128)(2,1)} async-done(((bf16[2048,2048]{1,0:T(8,128)(2,1)}), bf16[256,2048]{1,0:T(8,128)(2,1)}) %reduce-scatter.9.cloned.1.call-update) | async-done | bytes 1048592 | tf_op jit(solution)/shard_map/reduce_scatter | solution.py:31
  296.2 74.0 %all-gather.19.cloned.1.call-done = bf16[2048,1024]{1,0:T(8,128)(2,1)} async-done(((bf16[512,1024]{1,0:T(8,128)(2,1)}), bf16[2048,1024]{1,0:T(8,128)(2,1)}) %all-gather.19.cloned.1.call-update) | async-done | bytes 4194320 | tf_op jit(solution)/shard_map/all_gather | solution.py:35
  370.2 55.4 %all-gather.17.cloned.1.call-done = bf16[2048,2048]{1,0:T(8,128)(2,1)} async-done(((bf16[256,2048]{1,0:T(8,128)(2,1)}), bf16[2048,2048]{1,0:T(8,128)(2,1)}) %all-gather.17.cloned.1.call-update) | async-done | bytes 8388624 | tf_op jit(solution)/shard_map/all_gather | solution.py:27
  425.7 15.8 %multiply_convert_fusion.1 = (bf16[2048,1024]{1,0:T(8,128)(2,1)}, f32[2048,1024]{1,0:T(8,128)}) fusion(f32[1024]{0:T(1024)S(1)} %bitcast.174, bf16[2048,2048]{1,0:T(8,128)(2,1)} %all-gather.17.cloned.1.call-done, bf16[2048,1024]{1,0:T(8,128)(2,1)} %all-gather.19.cloned.1.call-done), kind=kOutput, calls=%fused_computation.27 | convolution fusion | flops 8602517504 | bytes 25169920 | tf_op jit(solution)/shard_map/dot_general | solution.py:23
  441.5 66.6 %all-gather.21.cloned.1.call-done = bf16[1024,2048]{1,0:T(8,128)(2,1)} async-done(((bf16[256,2048]{1,0:T(8,128)(2,1)}), bf16[1024,2048]{1,0:T(8,128)(2,1)}) %all-gather.21.cloned.1.call-update) | async-done | bytes 4194320 | tf_op jit(solution)/shard_map/all_gather | solution.py:35
  508.1 55.6 %all-gather.23.cloned.1.call-done = bf16[2048,2048]{1,0:T(8,128)(2,1)} async-done(((bf16[256,2048]{1,0:T(8,128)(2,1)}), bf16[2048,2048]{1,0:T(8,128)(2,1)}) %all-gather.23.cloned.1.call-update) | async-done | bytes 8388624 | tf_op jit(solution)/shard_map/all_gather | solution.py:27
  563.7 17.0 %convert_reduce_fusion.1 = (f32[1024]{0:T(1024)}, bf16[2048,1024]{1,0:T(8,128)(2,1)S(1)}) fusion(f32[2048,1024]{1,0:T(8,128)} %get-tuple-element.62, f32[1024]{0:T(1024)S(1)} %bitcast.175, bf16[2048,2048]{1,0:T(8,128)(2,1)} %all-gather.23.cloned.1.call-done, bf16[1024,2048]{1,0:T(8,128)(2,1)} %all-gather.21.cloned.1.call-done), kind=kOutput, calls=%fused_computation.26 | convolution fusion | flops 8617196544 | bytes 25174016 | tf_op jit(solution)/shard_map/dot_general | solution.py:23
  593.6 14.4 %convolution_convert_fusion.2 = bf16[2048,2048]{1,0:T(8,128)(2,1)} fusion(bf16[2048,1024]{1,0:T(8,128)(2,1)} %get-tuple-element.61, bf16[1024,2048]{1,0:T(8,128)(2,1)} %all-gather.21.cloned.1.call-done), kind=kOutput, calls=%fused_computation.32 | convolution fusion | flops 8594128896 | bytes 16777216 | tf_op jit(solution)/shard_map/dot_general | solution.py:23
  608.8 56.2 %reduce-scatter.13.cloned.1.call-done = bf16[256,2048]{1,0:T(8,128)(2,1)} async-done(((bf16[2048,2048]{1,0:T(8,128)(2,1)}), bf16[256,2048]{1,0:T(8,128)(2,1)}) %reduce-scatter.13.cloned.1.call-update) | async-done | bytes 1048592 | tf_op jit(solution)/shard_map/reduce_scatter | solution.py:31
  667.9 71.7 %reduce-scatter.11.cloned.1.call-done = bf16[256,2048]{1,0:T(8,128)(2,1)} async-done(((bf16[2048,2048]{1,0:T(8,128)(2,1)}), bf16[256,2048]{1,0:T(8,128)(2,1)}) %reduce-scatter.11.cloned.1.call-update) | async-done | bytes 1048592 | tf_op jit(solution)/shard_map/reduce_scatter | solution.py:31
  744.3 14.0 %convolution_convert_fusion.5 = bf16[2048,1024]{1,0:T(8,128)(2,1)} fusion(bf16[2048,2048]{1,0:T(8,128)(2,1)} %all-gather.17.cloned.1.call-done, bf16[2048,1024]{1,0:T(8,128)(2,1)} %copy-done.39), kind=kOutput, calls=%fused_computation.40 | convolution fusion | flops 8592031744 | bytes 16777216 | tf_op jit(solution)/shard_map/dot_general | solution.py:23
  758.4 14.3 %convolution_convert_fusion.4 = bf16[1024,2048]{1,0:T(8,128)(2,1)} fusion(bf16[2048,1024]{1,0:T(8,128)(2,1)} %get-tuple-element.61, bf16[2048,2048]{1,0:T(8,128)(2,1)} %all-gather.23.cloned.1.call-done), kind=kOutput, calls=%fused_computation.39 | convolution fusion | flops 8592031744 | bytes 16777216 | tf_op jit(solution)/shard_map/dot_general | solution.py:23
  772.7 26.0 %all-gather.25.cloned.1.call-done = bf16[2048,2048]{1,0:T(8,128)(2,1)} async-done(((bf16[256,2048]{1,0:T(8,128)(2,1)}), bf16[2048,2048]{1,0:T(8,128)(2,1)}) %all-gather.25.cloned.1.call-update) | async-done | bytes 8388624 | tf_op jit(solution)/shard_map/all_gather | solution.py:27
  823.7 17.6 %multiply_convert_fusion = bf16[2,4,1024,1024]{2,3,1,0:T(8,128)(2,1)} fusion(bf16[2,1024,4,64]{1,3,2,0:T(8,128)(2,1)S(1)} %copy.93, bf16[2,1024,4,64]{1,3,2,0:T(8,128)(2,1)S(1)} %copy-done.15, f32[2,4,1024]{2,1,0:T(4,128)S(1)} %bitcast.172, f32[2,4,1024,1024]{2,3,1,0:T(8,128)} %get-tuple-element.58, f32[2,4,1024]{2,1,0:T(4,128)S(1)} %copy-done.27), kind=kOutput, calls=%fused_computation.2 | convolution fusion | flops 1107296256 | bytes 52494336 | tf_op jit(solution)/shard_map/sqhd,skhd->shqk/dot_general | solution.py:87
  897.5 59.8 %reduce-scatter.23.cloned.1.call-done = bf16[256,2048]{1,0:T(8,128)(2,1)} async-done(((bf16[1024,2048]{1,0:T(8,128)(2,1)}), bf16[256,2048]{1,0:T(8,128)(2,1)}) %reduce-scatter.23.cloned.1.call-update) | async-done | bytes 1048592 | tf_op jit(solution)/shard_map/reduce_scatter | solution.py:39
  966.4 54.1 %reduce-scatter.17.cloned.1.call-done = bf16[512,768]{1,0:T(8,128)(2,1)} async-done(((bf16[2048,768]{1,0:T(8,128)(2,1)}), bf16[512,768]{1,0:T(8,128)(2,1)}) %reduce-scatter.17.cloned.1.call-update) | async-done | bytes 786448 | tf_op jit(solution)/shard_map/reduce_scatter | solution.py:39
  1026.8 23.2 %reduce-scatter.19.cloned.1.call-done = bf16[64,2048]{1,0:T(8,128)(2,1)} async-done(((bf16[256,2048]{1,0:T(8,128)(2,1)}), bf16[64,2048]{1,0:T(8,128)(2,1)}) %reduce-scatter.19.cloned.1.call-update) | async-done | bytes 262160 | tf_op jit(solution)/shard_map/reduce_scatter | solution.py:39
  1066.6 56.6 %reduce-scatter.15.cloned.1.call-done = bf16[256,2048]{1,0:T(8,128)(2,1)} async-done(((bf16[2048,2048]{1,0:T(8,128)(2,1)}), bf16[256,2048]{1,0:T(8,128)(2,1)}) %reduce-scatter.15.cloned.1.call-update) | async-done | bytes 1048592 | tf_op jit(solution)/shard_map/reduce_scatter | solution.py:31
  1129.9 120.3 %all-reduce.3.cloned.1.call-done = f32[32,768]{1,0:T(8,128)} async-done(((f32[32,768]{1,0:T(8,128)}), f32[32,768]{1,0:T(8,128)}) %all-reduce.3.cloned.1.call-update) | async-done | bytes 98320
  (256 shorter events, 234.4 us)
Async XLA Ops:
  7.2 101.7 %copy-start = (s32[2]{0:T(128)S(1)}, s32[2]{0:T(128)}, u32[]{:S(2)}) copy-start(s32[2]{0:T(128)} %param.34) | copy-start | bytes 28
  7.2 105.0 %all-gather.11.cloned.1.call-start = ((), (), s32[]{:S(2)}) async-start(), calls=%async_computation.12 | async-start | bytes 9437184 | tf_op jit(solution)/shard_map/all_gather | solution.py:27
  8.0 131.4 %all-gather.13.cloned.1.call-start = ((), (), s32[]{:S(2)}) async-start(), calls=%async_computation.13 | async-start | bytes 3932160 | tf_op jit(solution)/shard_map/all_gather | solution.py:35
  37.1 173.5 %all-gather.15.cloned.1.call-start = ((), (), s32[]{:S(2)}) async-start(), calls=%async_computation.14 | async-start | bytes 1310720 | tf_op jit(solution)/shard_map/all_gather | solution.py:35
  37.8 250.1 %reduce-scatter.9.cloned.1.call-start = ((), (), s32[]{:S(2)}) async-start(), calls=%async_computation.15 | async-start | bytes 9437184 | tf_op jit(solution)/shard_map/reduce_scatter | solution.py:31
  217.8 152.4 %all-gather.19.cloned.1.call-start = ((), (), s32[]{:S(2)}) async-start(), calls=%async_computation.17 | async-start | bytes 5242880 | tf_op jit(solution)/shard_map/all_gather | solution.py:35
  219.3 68.7 %copy-start.3 = (bf16[256,2048]{1,0:T(8,128)(2,1)S(1)}, bf16[256,2048]{1,0:T(8,128)(2,1)}, u32[]{:S(2)}) copy-start(bf16[256,2048]{1,0:T(8,128)(2,1)} %param.18) | copy-start | bytes 3145732
  239.2 186.5 %all-gather.17.cloned.1.call-start = ((), (), s32[]{:S(2)}) async-start(), calls=%async_computation.16 | async-start | bytes 9437184 | tf_op jit(solution)/shard_map/all_gather | solution.py:27
  293.3 214.8 %all-gather.21.cloned.1.call-start = ((), (), s32[]{:S(2)}) async-start(), calls=%async_computation.18 | async-start | bytes 5242880 | tf_op jit(solution)/shard_map/all_gather | solution.py:35
  294.1 269.6 %all-gather.23.cloned.1.call-start = ((), (), s32[]{:S(2)}) async-start(), calls=%async_computation.20 | async-start | bytes 9437184 | tf_op jit(solution)/shard_map/all_gather | solution.py:27
  296.1 368.9 %reduce-scatter.13.cloned.1.call-start = ((), (), s32[]{:S(2)}) async-start(), calls=%async_computation.21 | async-start | bytes 9437184 | tf_op jit(solution)/shard_map/reduce_scatter | solution.py:31
  593.6 146.0 %reduce-scatter.11.cloned.1.call-start = ((), (), s32[]{:S(2)}) async-start(), calls=%async_computation.19 | async-start | bytes 9437184 | tf_op jit(solution)/shard_map/reduce_scatter | solution.py:31
  608.0 131.6 %copy-start.5 = (bf16[256,2048]{1,0:T(8,128)(2,1)S(1)}, bf16[256,2048]{1,0:T(8,128)(2,1)}, u32[]{:S(2)}) copy-start(bf16[256,2048]{1,0:T(8,128)(2,1)} %get-tuple-element.27) | copy-start | bytes 3145732
  608.0 190.7 %all-gather.25.cloned.1.call-start = ((), (), s32[]{:S(2)}) async-start(), calls=%async_computation.22 | async-start | bytes 9437184 | tf_op jit(solution)/shard_map/all_gather | solution.py:27
  744.2 148.9 %reduce-scatter.21.cloned.1.call-start = ((), (), s32[]{:S(2)}) async-start(), calls=%async_computation.26 | async-start | bytes 5242880 | tf_op jit(solution)/shard_map/reduce_scatter | solution.py:39
  758.3 199.1 %reduce-scatter.23.cloned.1.call-start = ((), (), s32[]{:S(2)}) async-start(), calls=%async_computation.27 | async-start | bytes 5242880 | tf_op jit(solution)/shard_map/reduce_scatter | solution.py:39
  772.7 247.8 %reduce-scatter.17.cloned.1.call-start = ((), (), s32[]{:S(2)}) async-start(), calls=%async_computation.24 | async-start | bytes 3932160 | tf_op jit(solution)/shard_map/reduce_scatter | solution.py:39
  874.6 175.3 %reduce-scatter.19.cloned.1.call-start = ((), (), s32[]{:S(2)}) async-start(), calls=%async_computation.25 | async-start | bytes 1310720 | tf_op jit(solution)/shard_map/reduce_scatter | solution.py:39
  881.5 241.7 %reduce-scatter.15.cloned.1.call-start = ((), (), s32[]{:S(2)}) async-start(), calls=%async_computation.23 | async-start | bytes 9437184 | tf_op jit(solution)/shard_map/reduce_scatter | solution.py:31
  893.1 67.1 %all-to-all-start.3 = ((bf16[8,64,1024]{2,1,0:T(8,128)(2,1)}), bf16[8,64,1024]{2,1,0:T(8,128)(2,1)}, u32[]{:S(2)}, u32[]{:S(2)}) async-start(bf16[8,64,1024]{2,1,0:T(8,128)(2,1)} %bitcast.165), calls=%async_computation.10 | async-start | bytes 2097152 | tf_op jit(solution)/shard_map/all_to_all | solution.py:43
  1020.5 31.3 %all-to-all-start.2 = ((bf16[8,64,768]{2,1,0:T(8,128)(2,1)}), bf16[8,64,768]{2,1,0:T(8,128)(2,1)S(1)}, u32[]{:S(2)}, u32[]{:S(2)}) async-start(bf16[8,64,768]{2,1,0:T(8,128)(2,1)} %bitcast.166), calls=%async_computation.7 | async-start | bytes 1572864 | tf_op jit(solution)/shard_map/all_to_all | solution.py:43
  1024.1 226.1 %all-reduce.3.cloned.1.call-start = ((), (), s32[]{:S(2)}) async-start(), calls=%async_computation.28 | async-start | bytes 196608
  1058.4 68.1 %copy-start.6 = (f32[256,2048]{1,0:T(8,128)S(1)}, f32[256,2048]{1,0:T(8,128)}, u32[]{:S(2)}) copy-start(f32[256,2048]{1,0:T(8,128)} %get-tuple-element.30) | copy-start | bytes 6291460
  1064.0 189.0 %copy-start.1 = (s32[2]{0:T(128)S(1)}, s32[2]{0:T(128)}, u32[]{:S(2)}) copy-start(s32[2]{0:T(128)} %param.34) | copy-start | bytes 28
  (37 other events, 525.7 us)
Sparse Core Ops, SparseCore 0:
  9.9 63.9 all-gather.10
  75.5 63.7 all-gather.12
  140.9 26.6 all-gather.14
  217.9 69.9 reduce-scatter.8
  289.5 80.7 all-gather.18
  372.7 52.9 all-gather.16
  427.3 80.7 all-gather.20
  510.7 52.9 all-gather.22
  593.7 71.2 reduce-scatter.12
  668.3 71.2 reduce-scatter.10
  744.3 54.3 all-gather.24
  801.0 76.7 reduce-scatter.20
  880.1 77.2 reduce-scatter.22
  959.6 60.7 reduce-scatter.16
  1022.7 27.2 reduce-scatter.18
  1053.3 69.9 reduce-scatter.14
  1129.6 120.5 all-reduce.2

commit v2 on v1

v2 whole, which is shorter than its diff:
```python
import functools

import jax
import jax.numpy as jnp
from jax import lax
from jax.experimental import pallas as pl
from jax.experimental.pallas import tpu as pltpu
from jax.sharding import Mesh, PartitionSpec as P

HEADS = 32
HEAD = 64
SUMM = 50
PREV = 3
MAXSEG = 4
PRE = 150

epsilon = 1e-05
masked = -1e30

ALL = ("z", "core", "fsdp")
PLANE = ("core", "fsdp")
bf16 = jnp.bfloat16
f32 = jnp.float32
MESH = pl.DeviceIdType.MESH


def dot(a, b, ca, cb):
    return lax.dot_general(a, b, (((ca,), (cb,)), ((), ())), preferred_element_type=f32)


def z_gather(rows):
    return lax.all_gather(rows, "z", axis=0, tiled=True)


def z_sum(partial):
    return lax.psum_scatter(partial.astype(bf16), "z", scatter_dimension=0, tiled=True)


def after(value, *earlier):
    return lax.optimization_barrier((value, *earlier))[0]


def gauss_cdf(value):
    return 0.5 * (1.0 + lax.erf(value * 0.7071067811865476))


def gelu_slope(value, cdf_value):
    return cdf_value + value * jnp.exp(-0.5 * value * value) * 0.3989422804014327


def unit_norm(values):
    center = values - jnp.mean(values, axis=-1, keepdims=True)
    inverse_std = lax.rsqrt(jnp.mean(center * center, axis=-1, keepdims=True) + epsilon)
    return center * inverse_std, inverse_std


def normalize_back(grad_rows, unit_rows, inverse_std, norm_gain):
    scaled = grad_rows * norm_gain
    centered = scaled - jnp.mean(scaled, axis=-1, keepdims=True)
    centered = centered - unit_rows * jnp.mean(scaled * unit_rows, axis=-1, keepdims=True)
    return (
        centered * inverse_std,
        jnp.sum(grad_rows * unit_rows, axis=0),
        jnp.sum(grad_rows, axis=0),
    )


def head_mask(rows, cols, head):
    lane = lax.broadcasted_iota(jnp.int32, (rows, cols), 1)
    return lane // HEAD == head


def attend_segment(block, heads, seg_rows, seg, qkv_ref, live_ref, mixed_ref, total_ref, bias_ref):
    cols = heads * HEAD
    base = seg * seg_rows
    lane = lax.broadcasted_iota(jnp.int32, (block, 128), 1)
    for at in range(seg_rows // block):
        wide = (at + 1) * block
        rows = pl.ds(pl.multiple_of(base + at * block, block), block)
        keys = pl.ds(pl.multiple_of(base, seg_rows), wide)
        query_pos = at * block + lax.broadcasted_iota(jnp.int32, (block, wide), 0)
        key_pos = lax.broadcasted_iota(jnp.int32, (block, wide), 1)
        open_key = (live_ref[seg, :, :wide] > 0.0) & (key_pos < query_pos) | (key_pos == query_pos)
        bias_ref[:, :wide] = jnp.where(open_key, 0.0, masked)
        query = qkv_ref[rows, :cols] * jnp.asarray(HEAD**-0.5, bf16)
        result = jnp.zeros((block, cols), f32)
        totals = jnp.zeros((block, 128), f32)
        for head in range(heads):
            chosen = head_mask(block, cols, head)
            scores = dot(jnp.where(chosen, query, jnp.zeros_like(query)), qkv_ref[keys, cols : 2 * cols], 1, 1)
            scores = scores + bias_ref[:, :wide]
            top = jnp.max(scores, axis=1, keepdims=True)
            powers = jnp.exp(scores - top)
            total = jnp.sum(powers, axis=1, keepdims=True)
            probs = (powers * (1.0 / total)).astype(bf16)
            value = dot(probs, qkv_ref[keys, 2 * cols :], 1, 0)
            result = jnp.where(chosen, value, result)
            totals = jnp.where(lane == head, top + jnp.log(total), totals)
        mixed_ref[rows, :] = result.astype(bf16)
        total_ref[seg, :, at * block : (at + 1) * block] = totals.T[:8]


def attend_back_rows(
    block, heads, seg_rows, seg, at, qkv_ref, grad_ref, live_ref, total_ref, out_ref, bias_ref, sums_ref
):
    cols = heads * HEAD
    base = seg * seg_rows
    wide = (at + 1) * block
    rows = pl.ds(pl.multiple_of(base + at * block, block), block)
    keys = pl.ds(pl.multiple_of(base, seg_rows), wide)
    key_pos = lax.broadcasted_iota(jnp.int32, (wide, block), 0)
    query_pos = at * block + lax.broadcasted_iota(jnp.int32, (wide, block), 1)
    open_key = (live_ref[keys, :] > 0.0) & (key_pos < query_pos) | (key_pos == query_pos)
    bias_ref[:wide, :] = jnp.where(open_key, 0.0, masked)
    query = qkv_ref[rows, :cols] * jnp.asarray(HEAD**-0.5, bf16)
    grad = grad_ref[rows, :]
    grad_query = jnp.zeros((block, cols), f32)
    for head in range(heads):
        chosen = head_mask(block, cols, head)
        query_one = jnp.where(chosen, query, jnp.zeros_like(query))
        grad_one = jnp.where(chosen, grad, jnp.zeros_like(grad))
        scores = dot(qkv_ref[keys, cols : 2 * cols], query_one, 1, 1)
        total = total_ref[seg, head : head + 1, at * block : (at + 1) * block]
        probs = jnp.exp(scores + bias_ref[:wide, :] - total)
        terms = probs * dot(qkv_ref[keys, 2 * cols :], grad_one, 1, 1)
        delta = jnp.sum(terms, axis=0, keepdims=True)
        grad_scores = (terms - probs * delta).astype(bf16)
        sums_ref[:wide, :cols] += dot(grad_scores, query_one, 1, 0)
        sums_ref[:wide, cols:] += dot(probs.astype(bf16), grad_one, 1, 0)
        value = dot(grad_scores, qkv_ref[keys, cols : 2 * cols], 0, 0)
        grad_query = jnp.where(chosen, value, grad_query)
    out_ref[rows, :cols] = (grad_query * HEAD**-0.5).astype(bf16)


def greet(core_at, inner_at, group):
    barrier = pltpu.get_barrier_semaphore()
    pl.semaphore_signal(barrier, inc=1, device_id={"core": 1 - core_at, "fsdp": inner_at}, device_id_type=MESH)
    for step in range(1, group):
        pl.semaphore_signal(
            barrier,
            inc=1,
            device_id={"core": core_at, "fsdp": lax.rem(inner_at + step, group)},
            device_id_type=MESH,
        )
    pl.semaphore_wait(barrier, group)


def send(source, target, send_sem, recv_sem, core, inner):
    return pltpu.make_async_remote_copy(
        src_ref=source,
        dst_ref=target,
        send_sem=send_sem,
        recv_sem=recv_sem,
        device_id={"core": core, "fsdp": inner},
        device_id_type=MESH,
    )


def beside(inner_at):
    at_x = inner_at + 1 - 2 * lax.rem(inner_at, 2)
    at_y = lax.rem(inner_at + 2, 4)
    return at_x, at_y, lax.rem(at_x + 2, 4)


class PlaneGather:

    @staticmethod
    def scratch(group):
        return [pltpu.SemaphoreType.DMA((2, 2 * group)), pltpu.SemaphoreType.DMA((2, 2 * group)), pltpu.SemaphoreType.DMA]

    def __init__(self, group, source, target, chip_sems, core_sems, own_sem):
        self.group, self.source, self.target = group, source, target
        self.chip_sems, self.core_sems = chip_sems, core_sems
        self.core, self.inner = lax.axis_index("core"), lax.axis_index("fsdp")
        self.mine = self.core * group + self.inner
        self.own = pltpu.make_async_copy(source, target.at[self.mine], own_sem)
        half = source.shape[0] // 2
        self.low, self.high = pl.ds(0, half), pl.ds(half, half)
        self.sent = []

    def to_chip(self, at, source, target, inner):
        return send(source, target, self.chip_sems.at[0, at], self.chip_sems.at[1, at], self.core, inner)

    def to_core(self, at, source, target):
        return send(source, target, self.core_sems.at[0, at], self.core_sems.at[1, at], 1 - self.core, self.inner)

    def block(self, core, inner, part=None):
        at = core * self.group + inner
        return self.target.at[at] if part is None else self.target.at[at, part]

    def go(self, copy):
        copy.start()
        self.sent.append(copy)

    def start(self):
        own = self.target.at[self.mine]
        if self.group == 4:
            at_x, at_y, _ = beside(self.inner)
            self.go(self.to_chip(0, self.source, own, at_x))
            self.go(self.to_chip(1, self.source, own, at_y))
        else:
            for step in range(1, self.group):
                self.go(self.to_chip(step, self.source, own, lax.rem(self.inner + step, self.group)))
        self.go(self.to_core(0, self.source, own))
        self.own.start()

    def relay(self):
        if self.group == 4:
            at_x, at_y, _ = beside(self.inner)
            block = self.block(self.core, at_x)
            self.to_chip(0, block, block, at_x).wait_recv()
            part = self.block(self.core, at_x, self.low)
            self.go(self.to_chip(2, part, part, at_y))
            self.go(self.to_core(1, block, block))
            block = self.block(self.core, at_y)
            self.to_chip(1, block, block, at_y).wait_recv()
            part = self.block(self.core, at_y, self.high)
            self.go(self.to_chip(3, part, part, at_x))
            self.go(self.to_core(2, block, block))
        else:
            for step in range(1, self.group):
                inner = lax.rem(self.inner - step + self.group, self.group)
                block = self.block(self.core, inner)
                self.to_chip(step, block, block, inner).wait_recv()
                self.go(self.to_core(step, block, block))

    def finish(self):
        other = 1 - self.core
        if self.group == 4:
            at_x, at_y, across = beside(self.inner)
            for at, part in ((2, self.low), (3, self.high)):
                block = self.block(self.core, across, part)
                self.to_chip(at, block, block, at_x).wait_recv()
                self.go(self.to_core(at + 1, block, block))
            arriving = [
                self.block(other, self.inner),
                self.block(other, at_x),
                self.block(other, at_y),
                self.block(other, across, self.low),
                self.block(other, across, self.high),
            ]
        else:
            arriving = [
                self.block(other, lax.rem(self.inner - step + self.group, self.group)) for step in range(self.group)
            ]
        for at, block in enumerate(arriving):
            self.to_core(at, block, block).wait_recv()
        for copy in self.sent:
            copy.wait_send()
        self.own.wait()


class PlaneSum:

    @staticmethod
    def scratch(group, here, width):
        blocks = pltpu.VMEM((group, here, width), bf16)
        return [blocks, blocks, blocks, blocks, pltpu.SemaphoreType.DMA((2, 2 * group)), pltpu.SemaphoreType.DMA((2, group))]

    def __init__(self, group, product, out_ref, to_core, from_core, pair, land, chip_sems, core_sems):
        self.group, self.product, self.out_ref = group, product, out_ref
        self.to_core_ref, self.from_core_ref, self.pair, self.land = to_core, from_core, pair, land
        self.chip_sems, self.core_sems = chip_sems, core_sems
        self.core, self.inner = lax.axis_index("core"), lax.axis_index("fsdp")
        self.here, self.width = out_ref.shape
        half = self.here // 2
        self.low, self.high = pl.ds(0, half), pl.ds(half, half)
        self.tile = 512
        if group == 4:
            self.across_x, self.across_y, across = beside(self.inner)
            self.targets = [across, self.across_x, self.across_y, self.inner]
        else:
            self.targets = [lax.rem(self.inner + step, group) for step in range(1, group)] + [self.inner]
        self.sent = []

    def to_chip(self, at, source, target, inner):
        return send(source, target, self.chip_sems.at[0, at], self.chip_sems.at[1, at], self.core, inner)

    def go(self, copy):
        copy.start()
        self.sent.append(copy)

    def core_copy(self, i):
        return send(
            self.to_core_ref.at[i],
            self.from_core_ref.at[i],
            self.core_sems.at[0, i],
            self.core_sems.at[1, i],
            1 - self.core,
            self.inner,
        )

    def part_core(self, i):
        @pl.loop(0, self.width // self.tile)
        def _(at):
            columns = pl.ds(pl.multiple_of(at * self.tile, self.tile), self.tile)
            self.to_core_ref[i, :, columns] = self.product(1 - self.core, self.targets[i], columns).astype(bf16)

        self.go(self.core_copy(i))

    def part_chip(self, i):
        self.core_copy(i).wait_recv()
        last = i == self.group - 1

        @pl.loop(0, self.width // self.tile)
        def _(at):
            columns = pl.ds(pl.multiple_of(at * self.tile, self.tile), self.tile)
            value = self.product(self.core, self.targets[i], columns) + self.from_core_ref[i, :, columns].astype(f32)
            if last:
                self.out_ref[:, columns] = value
            else:
                self.pair[i, :, columns] = value.astype(bf16)

        if last:
            return
        pair, land = self.pair, self.land
        if self.group != 4:
            self.go(self.to_chip(i, pair.at[i], land.at[i], self.targets[i]))
        elif i == 0:
            self.go(self.to_chip(0, pair.at[0, self.low], land.at[0, self.low], self.across_x))
            self.go(self.to_chip(1, pair.at[0, self.high], land.at[1, self.low], self.across_y))
        elif i == 1:
            self.go(self.to_chip(2, pair.at[1, self.low], land.at[0, self.high], self.across_x))
        else:
            self.go(self.to_chip(3, pair.at[2, self.high], land.at[1, self.high], self.across_y))

    def arrive(self, at, place, part):
        self.to_chip(at, self.pair.at[0, part], self.land.at[place, part], self.across_x).wait_recv()
        return self.land[place, part, :].astype(f32)

    def relay(self):
        if self.group != 4:
            return
        pair, land = self.pair, self.land
        value = self.arrive(0, 0, self.low) + pair[2, self.low, :].astype(f32)
        pair[3, self.low, :] = value.astype(bf16)
        self.go(self.to_chip(4, pair.at[3, self.low], land.at[2, self.low], self.across_y))
        value = self.arrive(1, 1, self.low) + pair[1, self.high, :].astype(f32)
        pair[3, self.high, :] = value.astype(bf16)
        self.go(self.to_chip(5, pair.at[3, self.high], land.at[2, self.high], self.across_x))

    def finish(self):
        out_ref = self.out_ref
        if self.group == 4:
            out_ref[self.low, :] += self.arrive(2, 0, self.high)
            out_ref[self.high, :] += self.arrive(3, 1, self.high)
            out_ref[self.low, :] += self.arrive(4, 2, self.low)
            out_ref[self.high, :] += self.arrive(5, 2, self.high)
        else:
            for i in range(self.group - 1):
                self.to_chip(i, self.pair.at[i], self.land.at[i], self.inner).wait_recv()
                out_ref[...] += self.land[i].astype(f32)
        for copy in self.sent:
            copy.wait_send()

    def run(self):
        self.part_core(0)
        for i in range(self.group):
            if i + 1 < self.group:
                self.part_core(i + 1)
            self.part_chip(i)
        self.relay()
        self.finish()


def row_product(group, here, flip, a_ref, w_ref):
    def product(core, inner, columns):
        rows = a_ref[pl.ds(pl.multiple_of((core * group + inner) * here, here), here), :]
        if flip:
            return dot(rows, w_ref[columns, :], 1, 1)
        return dot(rows, w_ref[:, columns], 1, 0)

    return product


def other_device(core_at, inner_at, group, step):
    return lax.rem(core_at + step // group, 2), lax.rem(inner_at + step % group, group)


def gather_kernel(planes, group, *refs):
    gather_refs = 3
    if not planes:
        source, target = refs[:2]
        gather = PlaneGather(group, source, target, *refs[2:])
        greet(gather.core, gather.inner, group)
        gather.start()
        gather.relay()
        gather.finish()
        return
    source, small_ref, target, all_ref = refs[:4]
    gather = PlaneGather(group, source, target, *refs[4 : 4 + gather_refs])
    line_sems, face_sems = refs[4 + gather_refs :]
    z_at, core_at, inner_at = lax.axis_index("z"), gather.core, gather.inner
    mine, team = gather.mine, 2 * group
    barrier = pltpu.get_barrier_semaphore()
    for step in range(1, team):
        core, inner = other_device(core_at, inner_at, group, step)
        pl.semaphore_signal(barrier, inc=1, device_id={"core": core, "fsdp": inner}, device_id_type=MESH)
    for step in range(1, planes):
        to = lax.rem(z_at + step, planes)
        pl.semaphore_signal(barrier, inc=1, device_id={"z": to}, device_id_type=MESH)
    pl.semaphore_wait(barrier, team + planes - 2)
    lines, faces = [], []
    for step in range(1, planes):
        copy = pltpu.make_async_remote_copy(
            src_ref=small_ref,
            dst_ref=all_ref.at[mine, z_at],
            send_sem=line_sems.at[0, step],
            recv_sem=line_sems.at[1, step],
            device_id={"z": lax.rem(z_at + step, planes)},
            device_id_type=MESH,
        )
        copy.start()
        lines.append(copy)
    gather.start()
    all_ref[mine, z_at] = small_ref[...]
    for copy in lines:
        copy.wait()
    face = all_ref.at[mine]
    for step in range(1, team):
        copy = send(
            face, face, face_sems.at[0, step], face_sems.at[1, step], *other_device(core_at, inner_at, group, step)
        )
        copy.start()
        faces.append(copy)
    gather.relay()
    gather.finish()
    for step in range(1, team):
        core = lax.rem(core_at + step // group, 2)
        face = all_ref.at[core * group + lax.rem(inner_at - step % group + group, group)]
        send(face, face, face_sems.at[0, step], face_sems.at[1, step], core_at, inner_at).wait_recv()
    for copy in faces:
        copy.wait_send()


def plane_gather(array, group, collective_id, planes=0, small=None):
    anywhere = pl.BlockSpec(memory_space=pl.ANY)
    local = pl.BlockSpec(memory_space=pltpu.VMEM)
    shapes = [jax.ShapeDtypeStruct((2 * group, *array.shape), array.dtype)]
    scratch = PlaneGather.scratch(group)
    extra = []
    if planes:
        extra = [small]
        shapes.append(jax.ShapeDtypeStruct((2 * group, planes, *small.shape), small.dtype))
        scratch += [pltpu.SemaphoreType.DMA((2, planes)), pltpu.SemaphoreType.DMA((2, 2 * group))]
    results = pl.pallas_call(
        functools.partial(gather_kernel, planes, group),
        out_shape=shapes,
        in_specs=[anywhere] + [local] * len(extra),
        out_specs=[anywhere] + [local] * len(extra),
        scratch_shapes=scratch,
        compiler_params=pltpu.CompilerParams(collective_id=collective_id, has_side_effects=True),
        cost_estimate=pl.CostEstimate(flops=0, bytes_accessed=100 * array.size * 2, transcendentals=0),
    )(array, *extra)
    return [results[0].reshape(-1, array.shape[-1]), *results[1:]]


def product_sum_kernel(group, flip, a_ref, w_ref, out_ref, *refs):
    total = PlaneSum(group, row_product(group, out_ref.shape[0], flip, a_ref, w_ref), out_ref, *refs)
    greet(total.core, total.inner, group)
    total.run()


def product_sum(a, w, flip, group, collective_id):
    here = a.shape[0] // (2 * group)
    width = w.shape[0 if flip else 1]
    local = pl.BlockSpec(memory_space=pltpu.VMEM)
    return pl.pallas_call(
        functools.partial(product_sum_kernel, group, flip),
        out_shape=jax.ShapeDtypeStruct((here, width), f32),
        in_specs=[local, local],
        out_specs=local,
        scratch_shapes=PlaneSum.scratch(group, here, width),
        compiler_params=pltpu.CompilerParams(
            collective_id=collective_id, has_side_effects=True, vmem_limit_bytes=60 * 2**20
        ),
        cost_estimate=pl.CostEstimate(
            flops=2 * a.shape[0] * a.shape[1] * width, bytes_accessed=100 * a.shape[0] * width, transcendentals=0
        ),
    )(a, w)


def attend_kernel(
    block, group, x_ref, w_ref, gain_ref, shift_ref, qkv_bias_ref, live_ref, source,
    normed_ref, qkv_ref, mixed_ref, total_ref, target, bias_ref, *refs,
):
    seg_rows, heads = x_ref.shape[0] // 2, mixed_ref.shape[1] // HEAD
    gather = PlaneGather(group, source, target, *refs)
    greet(gather.core, gather.inner, group)
    gather.start()

    @pl.loop(0, 2 * seg_rows // block)
    def _(at):
        rows = pl.ds(pl.multiple_of(at * block, block), block)
        normed = (unit_norm(x_ref[rows, :].astype(f32))[0] * gain_ref[...] + shift_ref[...]).astype(bf16)
        normed_ref[rows, :] = normed
        qkv_ref[rows, :] = (dot(normed, w_ref[...], 1, 0) + qkv_bias_ref[...]).astype(bf16)

    for seg in range(2):
        attend_segment(block, heads, seg_rows, seg, qkv_ref, live_ref, mixed_ref, total_ref, bias_ref)
        if seg == 0:
            gather.relay()
    gather.finish()


def attend(x, w, gain, shift, qkv_bias, live, array, group, collective_id):
    rows, width = x.shape
    cols = w.shape[1] // 3
    block = 256
    local = pl.BlockSpec(memory_space=pltpu.VMEM)
    anywhere = pl.BlockSpec(memory_space=pl.ANY)
    results = pl.pallas_call(
        functools.partial(attend_kernel, block, group),
        out_shape=[
            jax.ShapeDtypeStruct((rows, width), bf16),
            jax.ShapeDtypeStruct((rows, 3 * cols), bf16),
            jax.ShapeDtypeStruct((rows, cols), bf16),
            jax.ShapeDtypeStruct((2, 8, rows // 2), f32),
            jax.ShapeDtypeStruct((2 * group, *array.shape), array.dtype),
        ],
        in_specs=[local] * 6 + [anywhere],
        out_specs=[local] * 4 + [anywhere],
        scratch_shapes=[pltpu.VMEM((block, rows // 2), f32), *PlaneGather.scratch(group)],
        compiler_params=pltpu.CompilerParams(
            collective_id=collective_id, has_side_effects=True, vmem_limit_bytes=60 * 2**20
        ),
        cost_estimate=pl.CostEstimate(
            flops=rows * rows * cols + 6 * rows * width * cols, bytes_accessed=10**8, transcendentals=0
        ),
    )(x, w, gain[None], shift[None], qkv_bias[None], live.astype(f32)[:, None], array)
    return [*results[:4], results[4].reshape(-1, array.shape[-1])]


def attend_back_kernel(
    block, group, qkv_ref, grad_ref, live_ref, total_ref, a_ref, w_ref, out_ref, own_ref, bias_ref, sums_ref, *refs
):
    seg_rows, heads = qkv_ref.shape[0] // 2, grad_ref.shape[1] // HEAD
    cols = heads * HEAD
    total = PlaneSum(group, row_product(group, own_ref.shape[0], False, a_ref, w_ref), own_ref, *refs)
    greet(total.core, total.inner, group)
    blocks = seg_rows // block
    for seg in range(2):
        sums_ref[...] = jnp.zeros_like(sums_ref)
        for at in range(blocks):
            step, late = divmod(seg * blocks + at, 2)
            if late:
                total.part_chip(step)
            else:
                total.part_core(step)
            if seg and at == blocks - 1:
                total.relay()
            attend_back_rows(
                block, heads, seg_rows, seg, at, qkv_ref, grad_ref, live_ref, total_ref, out_ref, bias_ref, sums_ref
            )
        out_ref[pl.ds(seg * seg_rows, seg_rows), cols:] = sums_ref[...].astype(bf16)
    total.finish()


def attend_back(qkv, grad, live, totals, a, w, group, collective_id):
    rows, cols = qkv.shape[0], qkv.shape[1] // 3
    here, width = rows // (2 * group), w.shape[1]
    local = pl.BlockSpec(memory_space=pltpu.VMEM)
    block = here
    return pl.pallas_call(
        functools.partial(attend_back_kernel, block, group),
        out_shape=[jax.ShapeDtypeStruct((rows, 3 * cols), bf16), jax.ShapeDtypeStruct((here, width), f32)],
        in_specs=[local] * 6,
        out_specs=[local] * 2,
        scratch_shapes=[
            pltpu.VMEM((rows // 2, block), f32),
            pltpu.VMEM((rows // 2, 2 * cols), f32),
            *PlaneSum.scratch(group, here, width),
        ],
        compiler_params=pltpu.CompilerParams(
            collective_id=collective_id, has_side_effects=True, vmem_limit_bytes=62 * 2**20
        ),
        cost_estimate=pl.CostEstimate(
            flops=2 * rows * rows * cols + 2 * rows * a.shape[1] * width, bytes_accessed=10**8, transcendentals=0
        ),
    )(qkv, grad, live.astype(f32).reshape(rows, 1), totals, a, w)


def exchange_kernel(group, count, *refs):
    ins, outs = refs[:count], refs[count : 2 * count]
    own_sem, out_sem, in_sem = refs[2 * count :]
    team = 2 * group
    core_at, inner_at = lax.axis_index("core"), lax.axis_index("fsdp")
    mine = core_at * group + inner_at

    def other(step):
        return lax.rem(core_at + step // group, 2), lax.rem(inner_at + step % group, group)

    def before(step):
        return lax.rem(core_at + step // group, 2), lax.rem(inner_at - step % group + group, group)

    barrier = pltpu.get_barrier_semaphore()
    for step in range(1, team):
        core, inner = other(step)
        pl.semaphore_signal(barrier, inc=1, device_id={"core": core, "fsdp": inner}, device_id_type=MESH)
    pl.semaphore_wait(barrier, team - 1)
    copies = []
    for i in range(count):
        for step in range(1, team):
            core, inner = other(step)
            copy = send(
                ins[i].at[core * group + inner], outs[i].at[mine], out_sem.at[i, step], in_sem.at[i, step], core, inner
            )
            copy.start()
            copies.append(copy)
        pltpu.make_async_copy(ins[i].at[mine], outs[i].at[mine], own_sem.at[i]).start()
    for i in range(count):
        pltpu.make_async_copy(ins[i].at[mine], outs[i].at[mine], own_sem.at[i]).wait()
        for step in range(1, team):
            core, inner = before(step)
            block = outs[i].at[core * group + inner]
            send(block, block, out_sem.at[i, step], in_sem.at[i, step], core, inner).wait_recv()
    for copy in copies:
        copy.wait_send()


def plane_exchange(arrays, group, collective_id):
    count = len(arrays)
    sems = pltpu.SemaphoreType.DMA((count, 2 * group))
    anywhere = pl.BlockSpec(memory_space=pl.ANY)
    size = sum(a.size * a.dtype.itemsize for a in arrays)
    return pl.pallas_call(
        functools.partial(exchange_kernel, group, count),
        out_shape=[jax.ShapeDtypeStruct(a.shape, a.dtype) for a in arrays],
        in_specs=[anywhere] * count,
        out_specs=[anywhere] * count,
        scratch_shapes=[pltpu.SemaphoreType.DMA((count,)), sems, sems],
        compiler_params=pltpu.CompilerParams(collective_id=collective_id, has_side_effects=True),
        cost_estimate=pl.CostEstimate(flops=0, bytes_accessed=40 * size, transcendentals=0),
    )(*arrays)


def small_sum_kernel(planes, group, in_ref, out_ref, from_plane, summed, from_z, plane_sems, z_sems):
    team = 2 * group
    z_at, core_at, inner_at = (lax.axis_index(name) for name in ALL)
    mine = core_at * group + inner_at

    def other(step):
        return lax.rem(core_at + step // group, 2), lax.rem(inner_at + step % group, group)

    barrier = pltpu.get_barrier_semaphore()
    for step in range(1, team):
        core, inner = other(step)
        pl.semaphore_signal(barrier, inc=1, device_id={"core": core, "fsdp": inner}, device_id_type=MESH)
    for step in range(1, planes):
        pl.semaphore_signal(
            barrier, inc=1, device_id={"z": lax.rem(z_at + step, planes)}, device_id_type=MESH
        )
    pl.semaphore_wait(barrier, team + planes - 2)
    copies = []
    for step in range(1, team):
        core, inner = other(step)
        copy = send(
            in_ref.at[core * group + inner],
            from_plane.at[step],
            plane_sems.at[0, step],
            plane_sems.at[1, step],
            core,
            inner,
        )
        copy.start()
        copies.append(copy)
    summed[...] = in_ref[mine]
    for copy in copies:
        copy.wait_recv()
    for step in range(1, team):
        summed[...] += from_plane[step]
    more = []
    for step in range(1, planes):
        to = lax.rem(z_at + step, planes)
        copy = pltpu.make_async_remote_copy(
            src_ref=summed.at[to],
            dst_ref=from_z.at[step],
            send_sem=z_sems.at[0, step],
            recv_sem=z_sems.at[1, step],
            device_id={"z": to},
            device_id_type=MESH,
        )
        copy.start()
        more.append(copy)
    out_ref[...] = summed[z_at]
    for step, copy in enumerate(more, 1):
        copy.wait_recv()
        out_ref[...] += from_z[step]
    for copy in copies + more:
        copy.wait_send()


def small_sum(terms, planes, group, collective_id):
    lines = terms.shape[2]
    local = pl.BlockSpec(memory_space=pltpu.VMEM)
    return pl.pallas_call(
        functools.partial(small_sum_kernel, planes, group),
        out_shape=jax.ShapeDtypeStruct((lines, 128), f32),
        in_specs=[local],
        out_specs=local,
        scratch_shapes=[
            pltpu.VMEM((2 * group, planes, lines, 128), f32),
            pltpu.VMEM((planes, lines, 128), f32),
            pltpu.VMEM((planes, lines, 128), f32),
            pltpu.SemaphoreType.DMA((2, 2 * group)),
            pltpu.SemaphoreType.DMA((2, planes)),
        ],
        compiler_params=pltpu.CompilerParams(collective_id=collective_id, has_side_effects=True),
        cost_estimate=pl.CostEstimate(flops=0, bytes_accessed=10**7, transcendentals=0),
    )(terms)


def body(
    layer_input,
    first_gain,
    first_shift,
    query_weight,
    key_weight,
    value_weight,
    output_weight,
    query_bias,
    value_bias,
    output_bias,
    second_gain,
    second_shift,
    up_weight,
    up_bias,
    down_weight,
    down_bias,
    segment_counts,
    out_grad,
):
    here, width = layer_input.shape
    wide = up_weight.shape[1]
    planes = lax.axis_size("z")
    group = lax.axis_size("fsdp")
    team = 2 * group
    z_at, core_at, inner_at = (lax.axis_index(name) for name in ALL)
    plane_at = core_at * group + inner_at
    seg_rows = here * group
    own_rows = query_weight.shape[0]
    own_wide = down_weight.shape[0]
    cols = width // team
    heads_here = cols // HEAD
    whole_heads = own_rows % HEAD == 0

    def to_columns(weight, unit):
        cut = weight.reshape(weight.shape[0], planes, team, unit)
        return cut.transpose(2, 0, 1, 3).reshape(team, weight.shape[0], planes * unit)

    def from_columns(blocks, unit):
        rows = blocks.shape[1]
        return blocks.reshape(team, rows, planes, unit).transpose(1, 2, 0, 3).reshape(rows, planes * team * unit)

    def head_columns(weight):
        if whole_heads:
            return to_columns(weight, own_rows)
        return weight.reshape(own_rows, team, cols).transpose(1, 0, 2)

    def head_rows(blocks):
        if whole_heads:
            return from_columns(blocks, own_rows)
        return blocks.transpose(1, 0, 2).reshape(own_rows, width)

    attn_blocks = jnp.concatenate([head_columns(w) for w in (query_weight, key_weight, value_weight)], axis=2)
    (attn_cols,) = plane_exchange([attn_blocks], group, 0)
    attn_cols = attn_cols.reshape(team * own_rows, 3 * cols)
    attn_full = z_gather(attn_cols)
    small = jnp.concatenate(
        [first_gain, first_shift, query_bias, value_bias, output_bias, second_gain, second_shift, down_bias, up_bias]
    )
    length = small.shape[0]
    small = jnp.pad(small.astype(f32), (0, -length % 1024)).reshape(-1, 128)
    all_rows, small_all = plane_gather(after(layer_input, attn_cols), group, 1, planes, small)
    small_all = small_all.swapaxes(0, 1).reshape(planes * team, -1)
    (up_cols,) = plane_exchange([after(to_columns(up_weight, own_wide), all_rows)], group, 10)
    up_cols = up_cols.reshape(team * own_rows, wide // team)
    gain_one, shift_one, bias_q, bias_v, bias_o, gain_two, shift_two, bias_down = (
        small_all[:, i * own_rows : (i + 1) * own_rows].reshape(width) for i in range(8)
    )
    bias_up = small_all[:, 8 * own_rows : length].reshape(planes, team, own_wide)[:, plane_at].reshape(wide // team)

    def own_columns(bias):
        if whole_heads:
            return bias.reshape(planes, team, own_rows)[:, plane_at].reshape(cols)
        return lax.dynamic_slice_in_dim(bias, plane_at * cols, cols)

    bias_q, bias_v = own_columns(bias_q), own_columns(bias_v)
    if whole_heads:
        out_full = z_gather(output_weight)
    else:
        out_full = lax.dynamic_slice_in_dim(
            lax.all_gather(output_weight, ALL, axis=0, tiled=True), plane_at * cols, cols
        )
    up_full = z_gather(up_cols)
    down_full = z_gather(down_weight)

    segment = 2 * z_at + jnp.arange(2, dtype=jnp.int32)
    place = segment % MAXSEG
    present = place < segment_counts[segment // MAXSEG]
    pos = jnp.arange(seg_rows, dtype=jnp.int32)
    live = present[:, None] & ((pos >= PRE)[None] | (place[:, None] >= PREV - pos[None] // SUMM))
    own_pos = inner_at * here + jnp.arange(here, dtype=jnp.int32)
    live_own = lax.dynamic_slice(live, (core_at, inner_at * here), (1, here))[0]

    out_own = jnp.where(live_own[:, None], out_grad, jnp.zeros_like(out_grad))
    rows_own = layer_input.astype(f32)
    unit_one, inverse_one = unit_norm(rows_own)
    normed_low, qkv, mixed_low, totals, out_live = attend(
        all_rows,
        attn_full,
        gain_one,
        shift_one,
        jnp.concatenate([bias_q, jnp.zeros_like(bias_q), bias_v]),
        live,
        out_own,
        group,
        11,
    )
    attended = rows_own + product_sum(mixed_low, out_full, False, group, 2) + bias_o
    unit_two, inverse_two = unit_norm(attended)
    (second_low,) = plane_gather((unit_two * gain_two + shift_two).astype(bf16), group, 3)
    pre_act = dot(second_low, up_full, 1, 0) + bias_up
    cdf = gauss_cdf(pre_act)
    activated = (pre_act * cdf).astype(bf16)

    out_own = out_own.astype(f32)
    grad_down = dot(activated, out_live, 0, 0).astype(bf16)
    out_live = after(out_live, grad_down)
    grad_down = z_sum(grad_down).astype(f32)
    grad_pre = (dot(out_live, down_full, 1, 1) * gelu_slope(pre_act, cdf)).astype(bf16)
    grad_up = dot(second_low, grad_pre, 0, 0).astype(bf16)
    grad_pre = after(grad_pre, grad_up)
    grad_up_bias = jnp.sum(grad_pre.astype(f32), axis=0)
    grad_second_in = product_sum(grad_pre, up_full, True, group, 5)
    grad_up = z_sum(after(grad_up, grad_down, grad_second_in)).reshape(team, own_rows, wide // team)
    grad_norm, grad_second_gain, grad_second_shift = normalize_back(
        grad_second_in, unit_two, inverse_two, gain_two
    )
    grad_after = out_own + grad_norm
    after_low_own = grad_after.astype(bf16)
    grad_output_bias = jnp.sum(after_low_own.astype(f32), axis=0)
    (after_low,) = plane_gather(after_low_own, group, 6)
    grad_output = dot(mixed_low, after_low, 0, 0).astype(bf16)
    after_low = after(after_low, grad_output)
    grad_mixed = dot(after_low, out_full, 1, 1).astype(bf16)
    grad_qkv, added = attend_back(qkv, grad_mixed, live, totals, activated, down_full, group, 4)
    layer_output = (attended + added + bias_down).astype(bf16)
    if whole_heads:
        grad_output = z_sum(after(grad_output, grad_up, grad_qkv)).astype(f32)
    else:
        spread = jnp.zeros((width, width), bf16)
        spread = lax.dynamic_update_slice_in_dim(spread, grad_output.astype(bf16), plane_at * cols, 0)
        grad_output = lax.psum_scatter(spread, ALL, scatter_dimension=0, tiled=True).astype(f32)
    grad_attn = dot(normed_low, grad_qkv, 0, 0).astype(bf16)
    grad_qkv = after(grad_qkv, grad_attn)
    grad_attn = z_sum(after(grad_attn, grad_output)).reshape(team, own_rows, 3 * cols)
    grad_bias = jnp.sum(grad_qkv.astype(f32), axis=0)
    grad_norm, grad_first_gain, grad_first_shift = normalize_back(
        product_sum(grad_qkv, attn_full, True, group, 8), unit_one, inverse_one, gain_one
    )
    input_grad = jnp.where((own_pos >= SUMM)[:, None], grad_after + grad_norm, 0.0)

    def spread_columns(bias):
        if whole_heads:
            full = jnp.zeros((planes, team, own_rows), f32)
            return lax.dynamic_update_slice(full, bias.reshape(planes, 1, own_rows), (0, plane_at, 0)).reshape(width)
        return lax.dynamic_update_slice(jnp.zeros((width,), f32), bias, (plane_at * cols,))

    sums = [
        grad_first_gain,
        grad_first_shift,
        spread_columns(grad_bias[:cols]),
        spread_columns(grad_bias[2 * cols :]),
        grad_output_bias,
        grad_second_gain,
        grad_second_shift,
        jnp.sum(out_own, axis=0),
    ]
    up_spread = jnp.zeros((planes, team, own_wide), f32)
    up_spread = lax.dynamic_update_slice(up_spread, grad_up_bias.reshape(planes, 1, own_wide), (0, plane_at, 0))
    packed = jnp.concatenate(
        [a.reshape(planes * team, own_rows) for a in sums] + [up_spread.reshape(planes * team, own_wide)], axis=1
    )
    packed = jnp.pad(packed, ((0, 0), (0, -length % 1024))).reshape(planes, team, -1, 128).swapaxes(0, 1)
    packed = small_sum(packed, planes, group, 9).reshape(-1)
    (grad_up,) = plane_exchange([after(grad_up, packed)], group, 12)
    grad_up = from_columns(grad_up, own_wide).astype(f32)
    (grad_attn,) = plane_exchange([after(grad_attn, grad_up)], group, 7)
    grad_weights = [head_rows(grad_attn[:, :, i * cols : (i + 1) * cols]).astype(f32) for i in range(3)]
    small_grads = [packed[i * own_rows : (i + 1) * own_rows] for i in range(8)]
    return (
        layer_output,
        input_grad,
        small_grads[0],
        small_grads[1],
        *grad_weights,
        grad_output,
        small_grads[2],
        small_grads[3],
        small_grads[4],
        small_grads[5],
        small_grads[6],
        grad_up,
        packed[8 * own_rows : length],
        grad_down,
        small_grads[7],
    )


def solution(mesh):
    outer, inner = mesh.devices.shape
    fine = Mesh(mesh.devices.reshape(outer // 2, 2, inner), ALL)
    rows, vector = P(ALL, None), P(ALL)
    return jax.shard_map(
        body,
        mesh=fine,
        in_specs=(
            rows, vector, vector, rows, rows, rows, rows, vector, vector, vector, vector, vector,
            rows, vector, rows, vector, P(), rows,
        ),
        out_specs=(
            rows, rows, vector, vector, rows, rows, rows, rows, vector, vector, vector, vector, vector,
            rows, vector, rows, vector,
        ),
        check_vma=False,
    )
```

time: 1270 us -> 645 us (0.51)
  waiting for transfers between devices: 784 us -> 27.1 us
  Pallas kernels: 0 us -> 449 us
  matrix products: 215 us -> 82.4 us
  blocking collectives: 112 us -> 0 us
  local copies, waits for them, and re-layouts: 63.1 us -> 32.1 us
  other arithmetic: 62.6 us -> 32.8 us
    pallas_call x0 -> x13, Pallas kernels: none -> 449 us  [the longest x3 142 us: product_sum(): pl.pallas_call(functools.partial(product_sum_kernel, group, flip), out_sh...]
    reduce_scatter x4 -> x0, waiting for transfers between devices: 233 us -> none  [plane_sum(): lax.psum_scatter(partial.astype(bf16), PLANE, scatter_dimension=0, tiled=...]
    all_gather x4, waiting for transfers between devices: 154 us -> 12.3 us  [z_gather(): return lax.all_gather(rows, 'z', axis=0, tiled=True)]
    all_gather x4 -> x0, waiting for transfers between devices: 137 us -> none  [plane_gather(): return lax.all_gather(rows, PLANE, axis=0, tiled=True)]
    reduce_scatter x4, waiting for transfers between devices: 137 us -> 13.5 us  [z_sum(): lax.psum_scatter(partial.astype(bf16), 'z', scatter_dimension=0, tiled=True)]
    unnamed x18 -> x8, waiting for transfers between devices: 123 us -> 1.32 us
    all_gather x1 -> x0, blocking collectives: 69.1 us -> none  [body(): small_all = lax.all_gather(small, ALL, axis=0, tiled=False).astype(f32)]
    dot_general x5 -> x0, matrix products: 59.1 us -> none  [the longest x1 17.6 us: attend_back(): jnp.einsum('sqhd,skhd->shqk', grad, v, preferred_element_type=f32)]
  transfers between devices with their start and end apart: 19 -> 8, of which waited for: 14 -> 2; matrix products, arithmetic and copies ran while one was open for 23% -> 20% of each run, Pallas kernels for 0% -> 66%
where the time goes in v2:
time: 645 us; the launch traced here: 639 us
  Pallas kernels  449 us (70%)
  matrix products  82.4 us (13%)
  other arithmetic  32.8 us (5%)
  local copies, waits for them, and re-layouts  32.1 us (5%)
  waiting for transfers between devices  27.1 us (4%)
  between operations  15.4 us (2%)
    pallas_call x3, Pallas kernels, product_sum(): pl.pallas_call(functools.partial(product_sum_kernel, group, flip), out_sh...  142 us
    pallas_call x3, Pallas kernels, plane_gather(): pl.pallas_call(functools.partial(gather_kernel, planes, group), out_shape...  129 us
    dot_general x7, matrix products, dot(): lax.dot_general(a, b, (((ca,), (cb,)), ((), ())), preferred_element_type=...  82.4 us
    pallas_call x1, Pallas kernels, attend_back(): pl.pallas_call(functools.partial(attend_back_kernel, block, group), out_s...  59.2 us
    pallas_call x4, Pallas kernels, plane_exchange(): pl.pallas_call(functools.partial(exchange_kernel, group, count), out_shap...  56.5 us
    pallas_call x1, Pallas kernels, attend(): pl.pallas_call(functools.partial(attend_kernel, block, group), out_shape=...  51.2 us
    reduce_scatter x4, waiting for transfers between devices, z_sum(): lax.psum_scatter(partial.astype(bf16), 'z', scatter_dimension=0, tiled=True)  13.5 us
  transfers between devices with their start and end apart: 8, of which 2 were waited for; matrix products, arithmetic and copies ran while one was open for 20% of the time, Pallas kernels for 66%

profile of v2, /device:TPU:0, one launch (start us, length us, event | category | flops | bytes accessed | tf_op | source)
XLA Modules:
  0.0 638.6 jit_solution(5734757154993648977)
XLA Ops:
  12.4 14.3 %shard_map.305 = bf16[8,64,768]{2,1,0:T(8,128)(2,1)} custom-call(bf16[8,64,768]{2,1,0:T(8,128)(2,1)} %pad_maximum_fusion.refs_0_), custom_call_target="tpu_custom_call" | custom-call | bytes 31457280 | tf_op jit(solution)/shard_map/pallas_call | solution.py:626
  30.7 46.2 %shard_map.306 = (bf16[8,256,2048]{2,1,0:T(8,128)(2,1)}, f32[8,4,8,128]{3,2,1,0:T(8,128)}) custom-call(bf16[256,2048]{1,0:T(8,128)(2,1)} %refs_0_, f32[8,128]{1,0:T(8,128)} %bitcast_convert_fusion.refs_1_), custom_call_target="tpu_custom_call" | custom-call | bytes 104857600 | tf_op jit(solution)/shard_map/pallas_call | solution.py:446
  76.9 14.5 %shard_map.310 = bf16[8,64,1024]{2,1,0:T(8,128)(2,1)} custom-call(bf16[8,64,1024]{2,1,0:T(8,128)(2,1)} %reshape.482.refs_0_), custom_call_target="tpu_custom_call" | custom-call | bytes 41943040 | tf_op jit(solution)/shard_map/pallas_call | solution.py:626
  97.8 51.2 %shard_map.307 = (bf16[2048,2048]{1,0:T(8,128)(2,1)}, bf16[2048,768]{1,0:T(8,128)(2,1)}, bf16[2048,256]{1,0:T(8,128)(2,1)}, f32[2,8,1024]{2,1,0:T(8,128)}, bf16[8,256,2048]{2,1,0:T(8,128)(2,1)}) custom-call(bf16[2048,2048]{1,0:T(8,128)(2,1)} %bitcast.122, bf16[2048,768]{1,0:T(8,128)(2,1)} %all-gather.5.cloned.1.call-done.w_ref, ...), custom_call_target="tpu_custom_call" | custom-call | flops 7516192768 | bytes 100000000 | tf_op jit(solution)/shard_map/pallas_call | solution.py:512
  149.0 45.3 %shard_map.308 = f32[256,2048]{1,0:T(8,128)} custom-call(bf16[2048,256]{1,0:T(8,128)(2,1)} %get-tuple-element.40.a_ref, bf16[256,2048]{1,0:T(8,128)(2,1)} %all-gather.7.cloned.1.call-done.w_ref), custom_call_target="tpu_custom_call" | custom-call | flops 2147483648 | bytes 419430400 | tf_op jit(solution)/shard_map/pallas_call | solution.py:468
  198.5 41.2 %shard_map.309 = bf16[8,256,2048]{2,1,0:T(8,128)(2,1)} custom-call(bf16[256,2048]{1,0:T(8,128)(2,1)} %add_convert_fusion.1.refs_0_), custom_call_target="tpu_custom_call" | custom-call | bytes 104857600 | tf_op jit(solution)/shard_map/pallas_call | solution.py:446
  239.7 15.0 %multiply_convert_fusion = (bf16[2048,1024]{1,0:T(8,128)(2,1)S(1)}, f32[2048,1024]{1,0:T(8,128)}) fusion(f32[1024]{0:T(1024)S(1)} %bitcast.120, bf16[2048,2048]{1,0:T(8,128)(2,1)} %bitcast.93, bf16[2048,1024]{1,0:T(8,128)(2,1)} %all-gather.9.cloned.1.call-done.w_ref), kind=kOutput, calls=%fused_computation.9 | convolution fusion | flops 8602517504 | bytes 25169920 | tf_op jit(solution)/shard_map/dot_general | solution.py:28
  256.6 13.1 %convolution_convert_fusion = bf16[1024,2048]{1,0:T(8,128)(2,1)} fusion(bf16[2048,1024]{1,0:T(8,128)(2,1)S(1)} %get-tuple-element.96.a_ref, bf16[2048,2048]{1,0:T(8,128)(2,1)} %bitcast.123), kind=kOutput, calls=%fused_computation.12 | convolution fusion | flops 8592031744 | bytes 16777216 | tf_op jit(solution)/shard_map/dot_general | solution.py:28
  269.8 12.2 %all-gather.11.cloned.1.call-done.w_ref = bf16[1024,2048]{1,0:T(8,128)(2,1)} async-done(((bf16[256,2048]{1,0:T(8,128)(2,1)}), bf16[1024,2048]{1,0:T(8,128)(2,1)}) %all-gather.11.cloned.1.call-update) | async-done | bytes 4194320 | tf_op jit(solution)/shard_map/all_gather | solution.py:32
  282.0 16.1 %fusion.5.a_ref = bf16[2048,1024]{1,0:T(8,128)(2,1)S(1)} fusion(f32[2048,1024]{1,0:T(8,128)} %get-tuple-element.97, bf16[2048,2048]{1,0:T(8,128)(2,1)} %bitcast.124, bf16[1024,2048]{1,0:T(8,128)(2,1)} %all-gather.11.cloned.1.call-done.w_ref, f32[1024]{0:T(1024)S(1)} %bitcast.121), kind=kOutput, calls=%fused_computation.7 | convolution fusion | flops 8613003264 | bytes 25169920 | tf_op jit(solution)/shard_map/dot_general | solution.py:28
  300.1 12.8 %convolution_convert_fusion.1 = bf16[2048,1024]{1,0:T(8,128)(2,1)} fusion(bf16[2048,2048]{1,0:T(8,128)(2,1)} %bitcast.94, bf16[2048,1024]{1,0:T(8,128)(2,1)S(1)} %fusion.5.a_ref), kind=kOutput, calls=%fused_computation.13 | convolution fusion | flops 8592031744 | bytes 16777216 | tf_op jit(solution)/shard_map/dot_general | solution.py:28
  312.9 49.1 %shard_map.311 = f32[256,2048]{1,0:T(8,128)} custom-call(bf16[2048,1024]{1,0:T(8,128)(2,1)} %copy-done.8, bf16[2048,1024]{1,0:T(8,128)(2,1)} %all-gather.9.cloned.1.call-done.w_ref), custom_call_target="tpu_custom_call" | custom-call | flops 8589934592 | bytes 419430400 | tf_op jit(solution)/shard_map/pallas_call | solution.py:468
  371.8 41.6 %shard_map.312 = bf16[8,256,2048]{2,1,0:T(8,128)(2,1)} custom-call(bf16[256,2048]{1,0:T(8,128)(2,1)} %get-tuple-element.68.refs_0_), custom_call_target="tpu_custom_call" | custom-call | bytes 104857600 | tf_op jit(solution)/shard_map/pallas_call | solution.py:446
  413.4 6.9 %convolution_convert_fusion.4 = bf16[256,2048]{1,0:T(8,128)(2,1)} fusion(bf16[2048,256]{1,0:T(8,128)(2,1)S(1)} %copy-done.10, bf16[2048,2048]{1,0:T(8,128)(2,1)} %bitcast.91), kind=kOutput, calls=%fused_computation.21 | convolution fusion | flops 2148007936 | bytes 10485760 | tf_op jit(solution)/shard_map/dot_general | solution.py:28
  420.3 6.8 %convolution_convert_fusion.3.grad_ref = bf16[2048,256]{1,0:T(8,128)(2,1)} fusion(bf16[2048,2048]{1,0:T(8,128)(2,1)} %bitcast.92, bf16[256,2048]{1,0:T(8,128)(2,1)S(1)} %copy-done.25), kind=kOutput, calls=%fused_computation.20 | convolution fusion | flops 2148007936 | bytes 10485760 | tf_op jit(solution)/shard_map/dot_general | solution.py:28
  427.2 59.2 %shard_map.313 = (bf16[2048,768]{1,0:T(8,128)(2,1)}, f32[256,2048]{1,0:T(8,128)}) custom-call(bf16[2048,768]{1,0:T(8,128)(2,1)} %get-tuple-element.41.qkv_ref, bf16[2048,256]{1,0:T(8,128)(2,1)} %convolution_convert_fusion.3.grad_ref, f32[2048,1]{1,0:T(8,128)} %bitcast.110, f32[2,8,1024]{2,1,0:T(8,128)} %get-tuple-element.47.total_ref, ...), custom_call_target="tpu_custom_call" | custom-call | flops 10737418240 | bytes 100000000 | tf_op jit(solution)/shard_map/pallas_call | solution.py:564
  486.5 11.6 %convolution_convert_fusion.2 = bf16[2048,768]{1,0:T(8,128)(2,1)} fusion(bf16[2048,2048]{1,0:T(8,128)(2,1)} %get-tuple-element.50, bf16[2048,768]{1,0:T(8,128)(2,1)} %get-tuple-element.51.a_ref), kind=kOutput, calls=%fused_computation.14 | convolution fusion | flops 6444023808 | bytes 14680064 | tf_op jit(solution)/shard_map/dot_general | solution.py:28
  498.2 13.5 %reduce-scatter.9.cloned.1.call-done = bf16[64,2048]{1,0:T(8,128)(2,1)} async-done(((bf16[256,2048]{1,0:T(8,128)(2,1)}), bf16[64,2048]{1,0:T(8,128)(2,1)}) %reduce-scatter.9.cloned.1.call-update) | async-done | bytes 262160 | tf_op jit(solution)/shard_map/reduce_scatter | solution.py:36
  513.6 47.4 %shard_map.314 = f32[256,2048]{1,0:T(8,128)} custom-call(bf16[2048,768]{1,0:T(8,128)(2,1)} %get-tuple-element.51.a_ref, bf16[2048,768]{1,0:T(8,128)(2,1)} %all-gather.5.cloned.1.call-done.w_ref), custom_call_target="tpu_custom_call" | custom-call | flops 6442450944 | bytes 419430400 | tf_op jit(solution)/shard_map/pallas_call | solution.py:468
  566.8 3.1 convert_reduce_fusion
  570.7 10.7 %shard_map.315 = f32[8,128]{1,0:T(8,128)} custom-call(f32[8,4,8,128]{3,2,1,0:T(8,128)} %copy_bitcast_fusion.6.in_ref), custom_call_target="tpu_custom_call" | custom-call | bytes 10000000 | tf_op jit(solution)/shard_map/pallas_call | solution.py:696
  584.2 3.2 add_convert_fusion
  589.7 15.5 %shard_map.316 = bf16[8,64,1024]{2,1,0:T(8,128)(2,1)} custom-call(bf16[8,64,1024]{2,1,0:T(8,128)(2,1)} %bitcast.109), custom_call_target="tpu_custom_call" | custom-call | bytes 41943040 | tf_op jit(solution)/shard_map/pallas_call | solution.py:626
  611.2 12.1 %shard_map.317 = bf16[8,64,768]{2,1,0:T(8,128)(2,1)} custom-call(bf16[8,64,768]{2,1,0:T(8,128)(2,1)} %bitcast.111), custom_call_target="tpu_custom_call" | custom-call | bytes 31457280 | tf_op jit(solution)/shard_map/pallas_call | solution.py:626
  (175 shorter events, 60.4 us)
Async XLA Ops:
  7.2 85.0 %copy-start = (s32[2]{0:T(128)S(1)}, s32[2]{0:T(128)}, u32[]{:S(2)}) copy-start(s32[2]{0:T(128)} %param.34) | copy-start | bytes 28
  7.2 2.1 copy-start.13
  7.2 90.5 %all-gather.5.cloned.1.call-start = ((), (), s32[]{:S(2)}) async-start(), calls=%async_computation.4 | async-start | bytes 3932160 | tf_op jit(solution)/shard_map/all_gather | solution.py:32
  11.5 16.1 %copy-start.12 = (bf16[64,8192]{1,0:T(8,128)(2,1)S(1)}, bf16[64,8192]{1,0:T(8,128)(2,1)}, u32[]{:S(2)}) copy-start(bf16[64,8192]{1,0:T(8,128)(2,1)} %param.30) | copy-start | bytes 3145732
  26.8 122.2 %all-gather.7.cloned.1.call-start = ((), (), s32[]{:S(2)}) async-start(), calls=%async_computation.5 | async-start | bytes 1310720 | tf_op jit(solution)/shard_map/all_gather | solution.py:32
  27.5 212.2 %all-gather.9.cloned.1.call-start = ((), (), s32[]{:S(2)}) async-start(), calls=%async_computation.6 | async-start | bytes 5242880 | tf_op jit(solution)/shard_map/all_gather | solution.py:32
  27.8 2.1 copy-start.16
  76.9 16.7 %copy-start.4 = (bf16[256,2048]{1,0:T(8,128)(2,1)S(1)}, bf16[256,2048]{1,0:T(8,128)(2,1)}, u32[]{:S(2)}) copy-start(bf16[256,2048]{1,0:T(8,128)(2,1)} %refs_0_) | copy-start | bytes 3145732
  91.4 2.4 copy-start.15
  91.5 5.0 copy-start.11
  91.5 190.5 %all-gather.11.cloned.1.call-start = ((), (), s32[]{:S(2)}) async-start(), calls=%async_computation.7 | async-start | bytes 5242880 | tf_op jit(solution)/shard_map/all_gather | solution.py:32
  92.1 270.0 %reduce-scatter.5.cloned.1.call-start = ((), (), s32[]{:S(2)}) async-start(), calls=%async_computation.8 | async-start | bytes 5242880 | tf_op jit(solution)/shard_map/reduce_scatter | solution.py:36
  196.7 172.4 %copy-start.2 = (f32[256,2048]{1,0:T(8,128)}, f32[256,2048]{1,0:T(8,128)S(1)}, u32[]{:S(2)}) copy-start(f32[256,2048]{1,0:T(8,128)S(1)} %get-tuple-element.73) | copy-start | bytes 6291460
  269.7 216.7 %reduce-scatter.7.cloned.1.call-start = ((), (), s32[]{:S(2)}) async-start(), calls=%async_computation.9 | async-start | bytes 5242880 | tf_op jit(solution)/shard_map/reduce_scatter | solution.py:36
  364.9 146.7 %reduce-scatter.9.cloned.1.call-start = ((), (), s32[]{:S(2)}) async-start(), calls=%async_computation.10 | async-start | bytes 1310720 | tf_op jit(solution)/shard_map/reduce_scatter | solution.py:36
  366.3 2.7 copy-start.5
  366.3 2.7 copy-start.9
  371.8 41.6 %copy-start.10 = (bf16[2048,256]{1,0:T(8,128)(2,1)S(1)}, bf16[2048,256]{1,0:T(8,128)(2,1)}, u32[]{:S(2)}) copy-start(bf16[2048,256]{1,0:T(8,128)(2,1)} %get-tuple-element.40.a_ref) | copy-start | bytes 3145732
  413.4 7.0 %copy-start.25 = (bf16[256,2048]{1,0:T(8,128)(2,1)S(1)}, bf16[256,2048]{1,0:T(8,128)(2,1)}, u32[]{:S(2)}) copy-start(bf16[256,2048]{1,0:T(8,128)(2,1)} %all-gather.7.cloned.1.call-done.w_ref) | copy-start | bytes 3145732
  486.5 124.7 %reduce-scatter.11.cloned.1.call-start = ((), (), s32[]{:S(2)}) async-start(), calls=%async_computation.11 | async-start | bytes 3932160 | tf_op jit(solution)/shard_map/reduce_scatter | solution.py:36
  566.7 17.5 %copy-start.3 = (f32[256,2048]{1,0:T(8,128)S(1)}, f32[256,2048]{1,0:T(8,128)}, u32[]{:S(2)}) copy-start(f32[256,2048]{1,0:T(8,128)} %copy-done.2) | copy-start | bytes 6291460
  584.2 3.2 copy-start.6
  584.2 3.2 copy-start.7
  629.1 2.2 copy-start.1
  (11 other events, 21.9 us)
Sparse Core Ops, SparseCore 0:
  26.9 64.3 all-gather.4
  92.8 26.5 all-gather.6
  121.0 80.2 all-gather.8
  202.7 79.2 all-gather.10
  284.2 75.2 reduce-scatter.4
  365.0 74.6 reduce-scatter.6
  486.6 24.9 reduce-scatter.8
  514.0 58.8 reduce-scatter.10

commit v3 on v2

v3 whole, which is shorter than its diff:
```python
import functools
import math

import jax
import jax.numpy as jnp
from jax import lax
from jax.experimental import pallas as pl
from jax.experimental.pallas import tpu as pltpu
from jax.sharding import Mesh, PartitionSpec as P

HEADS = 32
HEAD = 64
SUMM = 50
PREV = 3
MAXSEG = 4
PRE = 150

epsilon = 1e-05
masked = -1e30

ALL = ("z", "core", "fsdp")
PLANE = ("core", "fsdp")
bf16 = jnp.bfloat16
f32 = jnp.float32
MESH = pl.DeviceIdType.MESH


def dot(a, b, ca, cb):
    return lax.dot_general(a, b, (((ca,), (cb,)), ((), ())), preferred_element_type=f32)


def z_gather(rows):
    return lax.all_gather(rows, "z", axis=0, tiled=True)


def z_sum(partial):
    return lax.psum_scatter(partial.astype(bf16), "z", scatter_dimension=0, tiled=True)


def after(value, *earlier):
    return lax.optimization_barrier((value, *earlier))[0]


def unit_norm(values):
    center = values - jnp.mean(values, axis=-1, keepdims=True)
    inverse_std = lax.rsqrt(jnp.mean(center * center, axis=-1, keepdims=True) + epsilon)
    return center * inverse_std, inverse_std


def normalize_back(grad_rows, unit_rows, inverse_std, norm_gain):
    scaled = grad_rows * norm_gain
    centered = scaled - jnp.mean(scaled, axis=-1, keepdims=True)
    centered = centered - unit_rows * jnp.mean(scaled * unit_rows, axis=-1, keepdims=True)
    return centered * inverse_std


def head_mask(rows, cols, head):
    lane = lax.broadcasted_iota(jnp.int32, (rows, cols), 1)
    return lane // HEAD == head


def attend_segment(block, heads, seg_rows, seg, qkv_ref, live_ref, mixed_ref, total_ref, bias_ref):
    cols = heads * HEAD
    base = seg * seg_rows
    lane = lax.broadcasted_iota(jnp.int32, (block, 128), 1)
    for at in range(seg_rows // block):
        wide = (at + 1) * block
        rows = pl.ds(pl.multiple_of(base + at * block, block), block)
        keys = pl.ds(pl.multiple_of(base, seg_rows), wide)
        query_pos = at * block + lax.broadcasted_iota(jnp.int32, (block, wide), 0)
        key_pos = lax.broadcasted_iota(jnp.int32, (block, wide), 1)
        open_key = (live_ref[seg, :, :wide] > 0.0) & (key_pos < query_pos) | (key_pos == query_pos)
        bias_ref[:, :wide] = jnp.where(open_key, 0.0, masked)
        query = qkv_ref[rows, :cols] * jnp.asarray(HEAD**-0.5, bf16)
        result = jnp.zeros((block, cols), f32)
        totals = jnp.zeros((block, 128), f32)
        for head in range(heads):
            chosen = head_mask(block, cols, head)
            scores = dot(jnp.where(chosen, query, jnp.zeros_like(query)), qkv_ref[keys, cols : 2 * cols], 1, 1)
            scores = scores + bias_ref[:, :wide]
            top = jnp.max(scores, axis=1, keepdims=True)
            powers = jnp.exp(scores - top)
            total = jnp.sum(powers, axis=1, keepdims=True)
            probs = (powers * (1.0 / total)).astype(bf16)
            value = dot(probs, qkv_ref[keys, 2 * cols :], 1, 0)
            result = jnp.where(chosen, value, result)
            totals = jnp.where(lane == head, top + jnp.log(total), totals)
        mixed_ref[rows, :] = result.astype(bf16)
        total_ref[seg, :, at * block : (at + 1) * block] = totals.T[:8]


def attend_back_rows(
    block, heads, seg_rows, seg, at, qkv_ref, grad_ref, live_ref, total_ref, out_ref, bias_ref, sums_ref
):
    cols = heads * HEAD
    base = seg * seg_rows
    wide = (at + 1) * block
    rows = pl.ds(pl.multiple_of(base + at * block, block), block)
    keys = pl.ds(pl.multiple_of(base, seg_rows), wide)
    key_pos = lax.broadcasted_iota(jnp.int32, (wide, block), 0)
    query_pos = at * block + lax.broadcasted_iota(jnp.int32, (wide, block), 1)
    open_key = (live_ref[keys, :] > 0.0) & (key_pos < query_pos) | (key_pos == query_pos)
    bias_ref[:wide, :] = jnp.where(open_key, 0.0, masked)
    query = qkv_ref[rows, :cols] * jnp.asarray(HEAD**-0.5, bf16)
    half = block // 2
    part = pl.ds(pl.multiple_of((base + at * block) // 2, half), half)
    grad = jnp.concatenate([one[part, :] for one in grad_ref], axis=0)
    grad_query = jnp.zeros((block, cols), f32)
    for head in range(heads):
        chosen = head_mask(block, cols, head)
        query_one = jnp.where(chosen, query, jnp.zeros_like(query))
        grad_one = jnp.where(chosen, grad, jnp.zeros_like(grad))
        scores = dot(qkv_ref[keys, cols : 2 * cols], query_one, 1, 1)
        total = total_ref[seg, head : head + 1, at * block : (at + 1) * block]
        probs = jnp.exp(scores + bias_ref[:wide, :] - total)
        terms = probs * dot(qkv_ref[keys, 2 * cols :], grad_one, 1, 1)
        delta = jnp.sum(terms, axis=0, keepdims=True)
        grad_scores = (terms - probs * delta).astype(bf16)
        sums_ref[:wide, :cols] += dot(grad_scores, query_one, 1, 0)
        sums_ref[:wide, cols:] += dot(probs.astype(bf16), grad_one, 1, 0)
        value = dot(grad_scores, qkv_ref[keys, cols : 2 * cols], 0, 0)
        grad_query = jnp.where(chosen, value, grad_query)
    out_ref[rows, :cols] = (grad_query * HEAD**-0.5).astype(bf16)


def other_device(core_at, inner_at, group, step):
    return lax.rem(core_at + step // group, 2), lax.rem(inner_at + step % group, group)


def signal(**place):
    pl.semaphore_signal(pltpu.get_barrier_semaphore(), inc=1, device_id=place, device_id_type=MESH)


def greet(core_at, inner_at, group):
    signal(core=1 - core_at, fsdp=inner_at)
    for step in range(1, group):
        signal(core=core_at, fsdp=lax.rem(inner_at + step, group))
    pl.semaphore_wait(pltpu.get_barrier_semaphore(), group)


def greet_all(core_at, inner_at, group, planes):
    z_at = lax.axis_index("z")
    for step in range(1, 2 * group):
        core, inner = other_device(core_at, inner_at, group, step)
        signal(core=core, fsdp=inner)
    for step in range(1, planes):
        signal(z=lax.rem(z_at + step, planes))
    pl.semaphore_wait(pltpu.get_barrier_semaphore(), 2 * group + planes - 2)


def send(source, target, send_sem, recv_sem, core, inner):
    return pltpu.make_async_remote_copy(
        src_ref=source,
        dst_ref=target,
        send_sem=send_sem,
        recv_sem=recv_sem,
        device_id={"core": core, "fsdp": inner},
        device_id_type=MESH,
    )


def beside(inner_at):
    at_x = inner_at + 1 - 2 * lax.rem(inner_at, 2)
    at_y = lax.rem(inner_at + 2, 4)
    return at_x, at_y, lax.rem(at_x + 2, 4)


class PlaneGather:

    @staticmethod
    def scratch(group):
        return [pltpu.SemaphoreType.DMA((2, 2 * group)), pltpu.SemaphoreType.DMA((2, 2 * group)), pltpu.SemaphoreType.DMA]

    def __init__(self, group, source, target, chip_sems, core_sems, own_sem):
        self.group, self.source, self.target = group, source, target
        self.chip_sems, self.core_sems = chip_sems, core_sems
        self.core, self.inner = lax.axis_index("core"), lax.axis_index("fsdp")
        self.mine = self.core * group + self.inner
        self.own = pltpu.make_async_copy(source, target.at[self.mine], own_sem)
        half = source.shape[0] // 2
        self.low, self.high = pl.ds(0, half), pl.ds(half, half)
        self.sent = []

    def to_chip(self, at, source, target, inner):
        return send(source, target, self.chip_sems.at[0, at], self.chip_sems.at[1, at], self.core, inner)

    def to_core(self, at, source, target):
        return send(source, target, self.core_sems.at[0, at], self.core_sems.at[1, at], 1 - self.core, self.inner)

    def block(self, core, inner, part=None):
        at = core * self.group + inner
        return self.target.at[at] if part is None else self.target.at[at, part]

    def go(self, copy):
        copy.start()
        self.sent.append(copy)

    def start(self):
        own = self.target.at[self.mine]
        if self.group == 4:
            at_x, at_y, _ = beside(self.inner)
            self.go(self.to_chip(0, self.source, own, at_x))
            self.go(self.to_chip(1, self.source, own, at_y))
        else:
            for step in range(1, self.group):
                self.go(self.to_chip(step, self.source, own, lax.rem(self.inner + step, self.group)))
        self.go(self.to_core(0, self.source, own))
        self.own.start()

    def wait_core(self, at):
        other, low, high = 1 - self.core, self.low, self.high
        if self.group == 4:
            at_x, at_y, across = beside(self.inner)
            inner, part = ((self.inner, None), (at_x, None), (at_y, None), (across, low), (across, high))[at]
        else:
            inner, part = lax.rem(self.inner - at + self.group, self.group), None
        block = self.block(other, inner, part)
        self.to_core(at, block, block).wait_recv()

    def across(self):
        if self.group == 4:
            at_x, at_y, across = beside(self.inner)
            for at, part in ((2, self.low), (3, self.high)):
                block = self.block(self.core, across, part)
                self.to_chip(at, block, block, at_x).wait_recv()
                self.go(self.to_core(at + 1, block, block))

    def run(self, use):
        core, inner, other = self.core, self.inner, 1 - self.core
        self.start()
        self.own.wait()
        use(core, inner)
        self.wait_core(0)
        use(other, inner)
        self.relay()
        if self.group == 4:
            at_x, at_y, across = beside(inner)
            use(core, at_x)
            use(core, at_y)
            self.wait_core(1)
            use(other, at_x)
            self.wait_core(2)
            use(other, at_y)
            self.across()
            use(core, across)
            self.wait_core(3)
            self.wait_core(4)
            use(other, across)
        else:
            for step in range(1, self.group):
                use(core, lax.rem(inner - step + self.group, self.group))
            for step in range(1, self.group):
                self.wait_core(step)
                use(other, lax.rem(inner - step + self.group, self.group))
        for copy in self.sent:
            copy.wait_send()

    def relay(self):
        if self.group == 4:
            at_x, at_y, _ = beside(self.inner)
            block = self.block(self.core, at_x)
            self.to_chip(0, block, block, at_x).wait_recv()
            part = self.block(self.core, at_x, self.low)
            self.go(self.to_chip(2, part, part, at_y))
            self.go(self.to_core(1, block, block))
            block = self.block(self.core, at_y)
            self.to_chip(1, block, block, at_y).wait_recv()
            part = self.block(self.core, at_y, self.high)
            self.go(self.to_chip(3, part, part, at_x))
            self.go(self.to_core(2, block, block))
        else:
            for step in range(1, self.group):
                inner = lax.rem(self.inner - step + self.group, self.group)
                block = self.block(self.core, inner)
                self.to_chip(step, block, block, inner).wait_recv()
                self.go(self.to_core(step, block, block))

    def finish(self):
        self.across()
        for at in range(5 if self.group == 4 else self.group):
            self.wait_core(at)
        for copy in self.sent:
            copy.wait_send()
        self.own.wait()


class PlaneSum:

    @staticmethod
    def scratch(group, here, width):
        blocks, fewer = (pltpu.VMEM((count, here, width), bf16) for count in (group, group - 1))
        sems = [pltpu.SemaphoreType.DMA((2, 2 * group)), pltpu.SemaphoreType.DMA((2, group))]
        return [blocks, blocks, blocks if group == 4 else fewer, fewer, *sems]

    def __init__(self, group, product, out_ref, to_core, from_core, pair, land, chip_sems, core_sems, prepare=None):
        self.group, self.product, self.out_ref, self.prepare = group, product, out_ref, prepare
        self.to_core_ref, self.from_core_ref, self.pair, self.land = to_core, from_core, pair, land
        self.chip_sems, self.core_sems = chip_sems, core_sems
        self.core, self.inner = lax.axis_index("core"), lax.axis_index("fsdp")
        self.here, self.width = out_ref.shape
        half = self.here // 2
        self.low, self.high = pl.ds(0, half), pl.ds(half, half)
        self.tile = math.gcd(self.width, 8192 // group)
        if group == 4:
            self.across_x, self.across_y, across = beside(self.inner)
            self.targets = [across, self.across_x, self.across_y, self.inner]
        else:
            self.targets = [lax.rem(self.inner + step, group) for step in range(1, group)] + [self.inner]
        self.sent = []

    def to_chip(self, at, source, target, inner):
        return send(source, target, self.chip_sems.at[0, at], self.chip_sems.at[1, at], self.core, inner)

    def go(self, copy):
        copy.start()
        self.sent.append(copy)

    def core_copy(self, i):
        return send(
            self.to_core_ref.at[i],
            self.from_core_ref.at[i],
            self.core_sems.at[0, i],
            self.core_sems.at[1, i],
            1 - self.core,
            self.inner,
        )

    def part_core(self, i):
        if self.prepare:
            self.prepare(1 - self.core, self.targets[i], 2 * i)

        @pl.loop(0, self.width // self.tile)
        def _(at):
            columns = pl.ds(pl.multiple_of(at * self.tile, self.tile), self.tile)
            self.to_core_ref[i, :, columns] = self.product(1 - self.core, self.targets[i], columns).astype(bf16)

        self.go(self.core_copy(i))

    def part_chip(self, i):
        if self.prepare:
            self.prepare(self.core, self.targets[i], 2 * i + 1)
        self.core_copy(i).wait_recv()
        last = i == self.group - 1

        @pl.loop(0, self.width // self.tile)
        def _(at):
            columns = pl.ds(pl.multiple_of(at * self.tile, self.tile), self.tile)
            value = self.product(self.core, self.targets[i], columns) + self.from_core_ref[i, :, columns].astype(f32)
            if last:
                self.out_ref[:, columns] = value
            else:
                self.pair[i, :, columns] = value.astype(bf16)

        if last:
            return
        pair, land = self.pair, self.land
        if self.group != 4:
            self.go(self.to_chip(i, pair.at[i], land.at[i], self.targets[i]))
        elif i == 0:
            self.go(self.to_chip(0, pair.at[0, self.low], land.at[0, self.low], self.across_x))
            self.go(self.to_chip(1, pair.at[0, self.high], land.at[1, self.low], self.across_y))
        elif i == 1:
            self.go(self.to_chip(2, pair.at[1, self.low], land.at[0, self.high], self.across_x))
        else:
            self.go(self.to_chip(3, pair.at[2, self.high], land.at[1, self.high], self.across_y))

    def arrive(self, at, place, part):
        self.to_chip(at, self.pair.at[0, part], self.land.at[place, part], self.across_x).wait_recv()
        return self.land[place, part, :].astype(f32)

    def relay(self):
        if self.group != 4:
            return
        pair, land = self.pair, self.land
        value = self.arrive(0, 0, self.low) + pair[2, self.low, :].astype(f32)
        pair[3, self.low, :] = value.astype(bf16)
        self.go(self.to_chip(4, pair.at[3, self.low], land.at[2, self.low], self.across_y))
        value = self.arrive(1, 1, self.low) + pair[1, self.high, :].astype(f32)
        pair[3, self.high, :] = value.astype(bf16)
        self.go(self.to_chip(5, pair.at[3, self.high], land.at[2, self.high], self.across_x))

    def finish(self):
        out_ref = self.out_ref
        if self.group == 4:
            out_ref[self.low, :] += self.arrive(2, 0, self.high)
            out_ref[self.high, :] += self.arrive(3, 1, self.high)
            out_ref[self.low, :] += self.arrive(4, 2, self.low)
            out_ref[self.high, :] += self.arrive(5, 2, self.high)
        else:
            for i in range(self.group - 1):
                self.to_chip(i, self.pair.at[i], self.land.at[i], self.inner).wait_recv()
                out_ref[...] += self.land[i].astype(f32)
        for copy in self.sent:
            copy.wait_send()

    @staticmethod
    def order(group, eager=False):
        if eager:
            return list(range(2 * group))
        parts = [0]
        for i in range(group):
            parts += ([2 * i + 2] if i + 1 < group else []) + [2 * i + 1]
        return parts

    def part(self, at):
        (self.part_chip if at % 2 else self.part_core)(at // 2)

    def run(self, eager=False, meanwhile=None):
        for at in self.order(self.group, eager):
            self.part(at)
        self.relay()
        if meanwhile:
            meanwhile()
        self.finish()


class PlanesSum:

    @staticmethod
    def scratch(planes, rows, width):
        return [pltpu.VMEM((planes, rows, width), bf16), pltpu.SemaphoreType.DMA((2, planes))]

    def __init__(self, planes, source, out_ref, land, sems):
        self.planes, self.source, self.out_ref, self.land, self.sems = planes, source, out_ref, land, sems
        self.z = lax.axis_index("z")
        self.sent = []

    def rows(self, z):
        count = self.out_ref.shape[0]
        return pl.ds(pl.multiple_of(z * count, count), count)

    def start(self):
        for step in range(1, self.planes):
            to = lax.rem(self.z + step, self.planes)
            copy = pltpu.make_async_remote_copy(
                src_ref=self.source.at[self.rows(to)],
                dst_ref=self.land.at[step],
                send_sem=self.sems.at[0, step],
                recv_sem=self.sems.at[1, step],
                device_id={"z": to},
                device_id_type=MESH,
            )
            copy.start()
            self.sent.append(copy)

    def finish(self):
        self.out_ref[...] = self.source[self.rows(self.z), :].astype(f32)
        for step, copy in enumerate(self.sent, 1):
            copy.wait()
            self.out_ref[...] += self.land[step].astype(f32)


def place_columns(out_ref, blocks, base, unit, planes, team):
    several = max(1, 128 // unit)
    for z in range(planes):
        for p in range(0, team, several):
            parts = [blocks[p + i, :, base + z * unit : base + (z + 1) * unit] for i in range(several)]
            value = parts[0] if several == 1 else jnp.concatenate(parts, axis=1)
            start = (z * team + p) * unit
            out_ref[:, start : start + unit * several] = value


def row_product(group, here, flip, a_ref, w_ref):
    def product(core, inner, columns):
        rows = a_ref[pl.ds(pl.multiple_of((core * group + inner) * here, here), here), :]
        if flip:
            return dot(rows, w_ref[columns, :], 1, 1)
        return dot(rows, w_ref[:, columns], 1, 0)

    return product


class PlaneExchange:

    @staticmethod
    def scratch(group):
        return [pltpu.SemaphoreType.DMA((2, 2 * group)), pltpu.SemaphoreType.DMA]

    def __init__(self, group, source, target, sems, own_sem):
        self.group, self.source, self.target, self.sems = group, source, target, sems
        self.core, self.inner = lax.axis_index("core"), lax.axis_index("fsdp")
        self.mine = self.core * group + self.inner
        self.own = pltpu.make_async_copy(source.at[self.mine], target.at[self.mine], own_sem)
        self.sent = []

    def start(self):
        for step in range(1, 2 * self.group):
            core, inner = other_device(self.core, self.inner, self.group, step)
            copy = send(
                self.source.at[core * self.group + inner],
                self.target.at[self.mine],
                self.sems.at[0, step],
                self.sems.at[1, step],
                core,
                inner,
            )
            copy.start()
            self.sent.append(copy)
        self.own.start()

    def start_cut(self, whole, unit, repeats):
        team = 2 * self.group
        for p in range(team):
            for r in range(repeats):
                start = (r * team + p) * unit
                self.source[p, :, r * unit : (r + 1) * unit] = whole[:, start : start + unit]
        self.start()

    def finish(self):
        group = self.group
        for step in range(1, 2 * group):
            core = lax.rem(self.core + step // group, 2)
            inner = lax.rem(self.inner - step % group + group, group)
            block = self.target.at[core * group + inner]
            send(block, block, self.sems.at[0, step], self.sems.at[1, step], core, inner).wait_recv()
        for copy in self.sent:
            copy.wait_send()
        self.own.wait()


ANY = pl.BlockSpec(memory_space=pl.ANY)
LOCAL = pl.BlockSpec(memory_space=pltpu.VMEM)


def talk(collective_id, megabytes):
    return pltpu.CompilerParams(
        collective_id=collective_id, has_side_effects=True, vmem_limit_bytes=megabytes * 2**20
    )


def cost(flops, bytes_accessed):
    return pl.CostEstimate(flops=flops, bytes_accessed=bytes_accessed, transcendentals=0)


def swap_kernel(group, unit, repeats, attn, up, attn_all, up_all, up_blocks, *refs):
    first = PlaneExchange(group, attn, attn_all, *refs[:2])
    second = PlaneExchange(group, up_blocks, up_all, *refs[2:])
    greet_all(first.core, first.inner, group, 1)
    first.start()
    second.start_cut(up, unit, repeats)
    first.finish()
    second.finish()


def plane_exchange(attn, up, unit, repeats, group, collective_id):
    team = 2 * group
    blocks = jax.ShapeDtypeStruct((team, up.shape[0], unit * repeats), up.dtype)
    return pl.pallas_call(
        functools.partial(swap_kernel, group, unit, repeats),
        out_shape=[jax.ShapeDtypeStruct(attn.shape, attn.dtype), blocks],
        in_specs=[ANY, LOCAL],
        out_specs=[ANY, ANY],
        scratch_shapes=[
            pltpu.VMEM(blocks.shape, blocks.dtype),
            *PlaneExchange.scratch(group),
            *PlaneExchange.scratch(group),
        ],
        compiler_params=talk(collective_id, 60),
        cost_estimate=cost(0, 80 * (attn.size + up.size)),
    )(attn, up)


def halves(ref, first):
    half = ref.shape[-2] // 2
    part = pl.ds(0 if first else half, half)
    return ref.at[part] if len(ref.shape) == 2 else ref.at[:, part]


def entry_kernel(planes, group, x_ref, small_ref, out_ref, x_all, small_all, out_all, *refs):
    rows = PlaneGather(group, x_ref, x_all, *refs[:3])
    first = PlaneGather(group, halves(out_ref, True), halves(out_all, True), *refs[3:6])
    line_sems, face_sems = refs[6:]
    z_at, core_at, inner_at, mine = lax.axis_index("z"), rows.core, rows.inner, rows.mine
    greet_all(core_at, inner_at, group, planes)
    lines, faces = [], []
    for step in range(1, planes):
        copy = pltpu.make_async_remote_copy(
            src_ref=small_ref,
            dst_ref=small_all.at[mine, z_at],
            send_sem=line_sems.at[0, step],
            recv_sem=line_sems.at[1, step],
            device_id={"z": lax.rem(z_at + step, planes)},
            device_id_type=MESH,
        )
        copy.start()
        lines.append(copy)
    rows.start()
    small_all[mine, z_at] = small_ref[...]
    for copy in lines:
        copy.wait()
    face = small_all.at[mine]
    for step in range(1, 2 * group):
        core, inner = other_device(core_at, inner_at, group, step)
        copy = send(face, face, face_sems.at[0, step], face_sems.at[1, step], core, inner)
        copy.start()
        faces.append(copy)
    rows.relay()
    first.start()
    rows.finish()
    first.relay()
    first.finish()
    for step in range(1, 2 * group):
        core = lax.rem(core_at + step // group, 2)
        face = small_all.at[core * group + lax.rem(inner_at - step % group + group, group)]
        send(face, face, face_sems.at[0, step], face_sems.at[1, step], core_at, inner_at).wait_recv()
    for copy in faces:
        copy.wait_send()


def entry(x, small, out_own, planes, group, collective_id):
    team = 2 * group
    return pl.pallas_call(
        functools.partial(entry_kernel, planes, group),
        out_shape=[
            jax.ShapeDtypeStruct((team, *x.shape), x.dtype),
            jax.ShapeDtypeStruct((team, planes, *small.shape), small.dtype),
            jax.ShapeDtypeStruct((team, *out_own.shape), out_own.dtype),
        ],
        in_specs=[ANY, LOCAL, ANY],
        out_specs=[ANY, LOCAL, ANY],
        scratch_shapes=[
            *PlaneGather.scratch(group),
            *PlaneGather.scratch(group),
            pltpu.SemaphoreType.DMA((2, planes)),
            pltpu.SemaphoreType.DMA((2, team)),
        ],
        compiler_params=talk(collective_id, 60),
        cost_estimate=cost(0, 400 * x.size),
    )(x, small, out_own)


def chunks(ref, do):
    rows = math.gcd(ref.shape[0], 64)

    @pl.loop(0, ref.shape[0] // rows)
    def _(at):
        do(pl.ds(pl.multiple_of(at * rows, rows), rows))


GAIN_ONE, SHIFT_ONE, BIAS_Q, BIAS_V, BIAS_O, GAIN_TWO, SHIFT_TWO, BIAS_DOWN = range(8)


def line(params_ref, at):
    return params_ref[at : at + 1, :]


def close_attention(inner_at, own_ref, ins, outs):
    x_ref, params_ref = ins
    attended_ref, low_ref = outs

    def do(rows):
        value = x_ref[rows, :].astype(f32) + own_ref[rows, :] + line(params_ref, BIAS_O)
        attended_ref[rows, :] = value
        normed = unit_norm(value)[0] * line(params_ref, GAIN_TWO) + line(params_ref, SHIFT_TWO)
        low_ref[rows, :] = normed.astype(bf16)

    chunks(own_ref, do)


def add_sums(sums_ref, *terms):
    for i, term in enumerate(terms):
        sums_ref[i : i + 1, :] += jnp.sum(term, axis=0, keepdims=True)


def close_second(inner_at, own_ref, ins, outs):
    attended_ref, out_ref, params_ref = ins
    after_ref, low_ref, sums_ref = outs
    sums_ref[...] = jnp.zeros_like(sums_ref)

    def do(rows):
        unit, inverse = unit_norm(attended_ref[rows, :])
        grad = own_ref[rows, :]
        value = out_ref[rows, :].astype(f32) + normalize_back(
            grad, unit, inverse, line(params_ref, GAIN_TWO)
        )
        low = value.astype(bf16)
        after_ref[rows, :] = value
        low_ref[rows, :] = low
        add_sums(sums_ref, grad * unit, grad, low.astype(f32), out_ref[rows, :].astype(f32))

    chunks(own_ref, do)


def close_first(inner_at, own_ref, ins, outs):
    x_ref, params_ref, after_ref = ins
    grad_ref, sums_ref = outs
    sums_ref[...] = jnp.zeros_like(sums_ref)

    def do(rows):
        unit, inverse = unit_norm(x_ref[rows, :].astype(f32))
        grad = own_ref[rows, :]
        grad_ref[rows, :] = after_ref[rows, :] + normalize_back(grad, unit, inverse, line(params_ref, GAIN_ONE))
        add_sums(sums_ref, grad * unit, grad)

    chunks(own_ref, do)


def product_sum_kernel(group, planes, flip, close, ins, outs, swap, extra, a_ref, w_ref, *refs):
    in_refs, refs = refs[:ins], refs[ins:]
    ahead, refs = refs[: swap + extra], refs[swap + extra :]
    out_refs, refs = refs[:outs], refs[outs:]
    placed, refs = refs[: swap + extra], refs[swap + extra :]
    own_ref, *refs = refs
    sums, refs = refs[:6], refs[6:]
    total = PlaneSum(group, row_product(group, own_ref.shape[0], flip, a_ref, w_ref), own_ref, *sums)
    if swap:
        arrived, *refs = refs
        exchange = PlaneExchange(group, ahead[0], arrived, *refs[:2])
        lines = PlanesSum(planes, ahead[1], placed[1], *refs[2:]) if extra else None
        greet_all(total.core, total.inner, group, planes)
        if extra:
            lines.start()
        exchange.start()
    else:
        greet(total.core, total.inner, group)
    total.run()
    close(total.inner, own_ref, in_refs, out_refs)
    if swap:
        exchange.finish()
        place_columns(placed[0], arrived, 0, arrived.shape[2] // planes, planes, 2 * group)
        if extra:
            lines.finish()


def product_sum(a, w, flip, close, ins, outs, group, collective_id, planes=1, swap=None, terms=None):
    here = a.shape[0] // (2 * group)
    width = w.shape[0 if flip else 1]
    shapes = [jax.ShapeDtypeStruct((rows, width), kind) for rows, kind in outs]
    scratch = [pltpu.VMEM((here, width), f32), *PlaneSum.scratch(group, here, width)]
    ahead, places = [], []
    if swap is not None:
        ahead, places = [swap], [ANY]
        shapes.append(jax.ShapeDtypeStruct((swap.shape[1], swap.shape[0] * swap.shape[2]), swap.dtype))
        scratch += [pltpu.VMEM(swap.shape, swap.dtype), *PlaneExchange.scratch(group)]
    if terms is not None:
        ahead, places = ahead + [terms], places + [LOCAL]
        rows = terms.shape[0] // planes
        shapes.append(jax.ShapeDtypeStruct((rows, width), f32))
        scratch += PlanesSum.scratch(planes, rows, width)
    extra = terms is not None
    return pl.pallas_call(
        functools.partial(
            product_sum_kernel, group, planes, flip, close, len(ins), len(outs), len(ahead) - extra, int(extra)
        ),
        out_shape=shapes,
        in_specs=[LOCAL] * (2 + len(ins)) + places,
        out_specs=[LOCAL] * len(shapes),
        scratch_shapes=scratch,
        compiler_params=talk(collective_id, 60),
        cost_estimate=cost(2 * a.shape[0] * a.shape[1] * width, 100 * a.shape[0] * width),
    )(a, w, *ins, *ahead)


def attend_kernel(
    block, group, x_ref, w_ref, params_ref, qkv_bias_ref, live_ref, source, _,
    normed_ref, qkv_ref, mixed_ref, total_ref, target, bias_ref, *refs,
):
    seg_rows, heads = x_ref.shape[0] // 2, mixed_ref.shape[1] // HEAD
    gather = PlaneGather(group, halves(source, False), halves(target, False), *refs)
    greet(gather.core, gather.inner, group)
    gather.start()

    @pl.loop(0, 2 * seg_rows // block)
    def _(at):
        rows = pl.ds(pl.multiple_of(at * block, block), block)
        normed = unit_norm(x_ref[rows, :].astype(f32))[0] * line(params_ref, GAIN_ONE)
        normed = (normed + line(params_ref, SHIFT_ONE)).astype(bf16)
        normed_ref[rows, :] = normed
        qkv_ref[rows, :] = (dot(normed, w_ref[...], 1, 0) + qkv_bias_ref[...]).astype(bf16)

    for seg in range(2):
        attend_segment(block, heads, seg_rows, seg, qkv_ref, live_ref, mixed_ref, total_ref, bias_ref)
        if seg == 0:
            gather.relay()
    gather.finish()


def attend(x, w, params, qkv_bias, live, array, gathered, group, collective_id):
    rows, width = x.shape
    cols = w.shape[1] // 3
    block = 256
    local = pl.BlockSpec(memory_space=pltpu.VMEM)
    anywhere = pl.BlockSpec(memory_space=pl.ANY)
    results = pl.pallas_call(
        functools.partial(attend_kernel, block, group),
        out_shape=[
            jax.ShapeDtypeStruct((rows, width), bf16),
            jax.ShapeDtypeStruct((rows, 3 * cols), bf16),
            jax.ShapeDtypeStruct((rows, cols), bf16),
            jax.ShapeDtypeStruct((2, 8, rows // 2), f32),
            jax.ShapeDtypeStruct((2 * group, *array.shape), array.dtype),
        ],
        in_specs=[local] * 5 + [anywhere] * 2,
        out_specs=[local] * 4 + [anywhere],
        input_output_aliases={6: 4},
        scratch_shapes=[pltpu.VMEM((block, rows // 2), f32), *PlaneGather.scratch(group)],
        compiler_params=pltpu.CompilerParams(
            collective_id=collective_id, has_side_effects=True, vmem_limit_bytes=60 * 2**20
        ),
        cost_estimate=pl.CostEstimate(
            flops=rows * rows * cols + 6 * rows * width * cols, bytes_accessed=10**8, transcendentals=0
        ),
    )(x, w, params, qkv_bias[None], live.astype(f32)[:, None], array, gathered)
    return [*results[:4], results[4].reshape(-1, array.shape[-1])]


def attend_back_kernel(
    block, group, qkv_ref, first_ref, second_ref, live_ref, total_ref, params_ref, a, w, attended, normed, *refs
):
    out_ref, layer_ref, column_ref, grad_w, *refs = refs
    own_ref, a_ref, w_ref, attended_ref, load_sems, bias_ref, sums_ref, *refs = refs
    grad_ref = first_ref, second_ref
    seg_rows, heads = qkv_ref.shape[0] // 2, first_ref.shape[1] // HEAD
    cols = heads * HEAD
    loads = [
        pltpu.make_async_copy(whole, held, load_sems.at[i])
        for i, (whole, held) in enumerate(((a, a_ref), (w, w_ref), (attended, attended_ref)))
    ]
    for load in loads:
        load.start()
    strips = Strips(normed, out_ref, grad_w, *refs[:3])
    strips.start()
    total = PlaneSum(group, row_product(group, own_ref.shape[0], False, a_ref, w_ref), own_ref, *refs[3:])
    greet(total.core, total.inner, group)
    column_ref[...] = jnp.zeros_like(column_ref)
    blocks = seg_rows // block
    parts, relayed = total.order(group), False
    for seg in range(2):
        sums_ref[...] = jnp.zeros_like(sums_ref)
        for at in range(blocks):
            turn = seg * blocks + at
            if turn == 0:
                for load in loads:
                    load.wait()
            for part in parts[:2]:
                total.part(part)
            if not parts and not relayed and turn >= group + 1:
                total.relay()
                relayed = True
            parts = parts[2:]
            attend_back_rows(
                block, heads, seg_rows, seg, at, qkv_ref, grad_ref, live_ref, total_ref, out_ref, bias_ref, sums_ref
            )
        low = sums_ref[...].astype(bf16)
        out_ref[pl.ds(seg * seg_rows, seg_rows), cols:] = low
        column_ref[:, cols:] += jnp.sum(low.astype(f32), axis=0, keepdims=True)
    column_ref[:, :cols] = jnp.sum(out_ref[:, :cols].astype(f32), axis=0, keepdims=True)
    strips.run()
    total.finish()

    def do(rows):
        layer_ref[rows, :] = (
            attended_ref[rows, :] + own_ref[rows, :] + line(params_ref, BIAS_DOWN)
        ).astype(bf16)

    chunks(own_ref, do)
    strips.finish()


def attend_back(qkv, grads, live, totals, params, a, w, attended, normed, group, collective_id):
    rows, cols = qkv.shape[0], qkv.shape[1] // 3
    here, width = rows // (2 * group), w.shape[1]
    block = here
    shapes = [
        jax.ShapeDtypeStruct((rows, 3 * cols), bf16),
        jax.ShapeDtypeStruct((here, width), bf16),
        jax.ShapeDtypeStruct((1, 3 * cols), f32),
        jax.ShapeDtypeStruct((width, 3 * cols), bf16),
    ]
    scratch = [
        pltpu.VMEM((here, width), f32),
        pltpu.VMEM(a.shape, bf16),
        pltpu.VMEM(w.shape, bf16),
        pltpu.VMEM(attended.shape, f32),
        pltpu.SemaphoreType.DMA((3,)),
        pltpu.VMEM((rows // 2, block), f32),
        pltpu.VMEM((rows // 2, 2 * cols), f32),
        *Strips.scratch(rows, 3 * cols, 1024 // group),
        *PlaneSum.scratch(group, here, width),
    ]
    return pl.pallas_call(
        functools.partial(attend_back_kernel, block, group),
        out_shape=shapes,
        in_specs=[LOCAL] * 6 + [ANY] * 4,
        out_specs=[LOCAL] * 3 + [ANY],
        scratch_shapes=scratch,
        compiler_params=talk(collective_id, 63),
        cost_estimate=cost(2 * rows * rows * cols + 2 * rows * a.shape[1] * width, 10**8),
    )(qkv, *grads, live.astype(f32).reshape(rows, 1), totals, params, a, w, attended, normed)


def gelu_parts(value):
    cdf = 0.5 * (1.0 + lax.erf(value * 0.7071067811865476))
    return value * cdf, cdf + value * jnp.exp(-0.5 * value * value) * 0.3989422804014327


def gather_up_kernel(group, source, up_ref, bias_ref, all_out, act_ref, slope_ref, all_ref, out_sems, *refs):
    gather = PlaneGather(group, source, all_ref, *refs)
    greet(gather.core, gather.inner, group)
    here = source.shape[0]
    tile = math.gcd(1024, up_ref.shape[1])

    def out_copy(core, inner):
        at = core * group + inner
        return pltpu.make_async_copy(all_ref.at[at], all_out.at[at], out_sems.at[at])

    def use(core, inner):
        at = core * group + inner
        out_copy(core, inner).start()
        rows = pl.ds(pl.multiple_of(at * here, here), here)

        @pl.loop(0, up_ref.shape[1] // tile)
        def _(i):
            columns = pl.ds(pl.multiple_of(i * tile, tile), tile)
            value, slope = gelu_parts(dot(all_ref[at], up_ref[:, columns], 1, 0) + bias_ref[:, columns])
            act_ref[rows, columns] = value.astype(bf16)
            slope_ref[rows, columns] = slope.astype(bf16)

    gather.run(use)
    for at in range(2 * group):
        pltpu.make_async_copy(all_ref.at[at], all_out.at[at], out_sems.at[at]).wait()


def gather_up(array, up, bias, group, collective_id):
    here, width = array.shape
    rows, wide = 2 * group * here, up.shape[1]
    local = pl.BlockSpec(memory_space=pltpu.VMEM)
    anywhere = pl.BlockSpec(memory_space=pl.ANY)
    all_rows, act, slope = pl.pallas_call(
        functools.partial(gather_up_kernel, group),
        out_shape=[
            jax.ShapeDtypeStruct((2 * group, here, width), bf16),
            jax.ShapeDtypeStruct((rows, wide), bf16),
            jax.ShapeDtypeStruct((rows, wide), bf16),
        ],
        in_specs=[anywhere, local, local],
        out_specs=[anywhere, local, local],
        scratch_shapes=[
            pltpu.VMEM((2 * group, here, width), bf16),
            pltpu.SemaphoreType.DMA((2 * group,)),
            *PlaneGather.scratch(group),
        ],
        compiler_params=pltpu.CompilerParams(
            collective_id=collective_id, has_side_effects=True, vmem_limit_bytes=60 * 2**20
        ),
        cost_estimate=pl.CostEstimate(
            flops=2 * rows * width * wide, bytes_accessed=50 * rows * width, transcendentals=0
        ),
    )(array, up, bias[None])
    return all_rows.reshape(rows, width), act, slope


def gather_mixed_kernel(group, last, array, w_ref, mixed_ref, *refs):
    sum_in, refs = (refs[0], refs[1:]) if last else (None, refs)
    grad_mixed_ref, grad_w_ref, all_ref, sum_ref = refs[:4]
    source = halves(array, not last)
    gather = PlaneGather(group, source, all_ref, *refs[4:])
    greet(gather.core, gather.inner, group)
    rows_here = source.shape[0]
    sum_ref[...] = sum_in[...] if last else jnp.zeros_like(sum_ref)

    def use(core, inner):
        at = core * group + inner
        rows = pl.ds(pl.multiple_of(at * rows_here, rows_here), rows_here)
        grad_mixed_ref[rows, :] = dot(all_ref[at], w_ref[...], 1, 1).astype(bf16)
        start = at * 2 * rows_here + last * rows_here
        mixed = mixed_ref[pl.ds(pl.multiple_of(start, rows_here), rows_here), :]
        sum_ref[...] += dot(mixed, all_ref[at], 0, 0)

    gather.run(use)
    grad_w_ref[...] = sum_ref[...].astype(grad_w_ref.dtype)


def gather_mixed(array, w, mixed, group, collective_id, before=None):
    here, width = array.shape
    rows, cols = mixed.shape
    extra = [] if before is None else [before]
    return pl.pallas_call(
        functools.partial(gather_mixed_kernel, group, len(extra)),
        out_shape=[
            jax.ShapeDtypeStruct((rows // 2, cols), bf16),
            jax.ShapeDtypeStruct((cols, width), bf16 if extra else f32),
        ],
        in_specs=[ANY] + [LOCAL] * (2 + len(extra)),
        out_specs=[LOCAL] * 2,
        scratch_shapes=[
            pltpu.VMEM((2 * group, here // 2, width), bf16),
            pltpu.VMEM((cols, width), f32),
            *PlaneGather.scratch(group),
        ],
        compiler_params=talk(collective_id, 60),
        cost_estimate=cost(2 * rows * width * cols, 25 * rows * width),
    )(array, w, mixed, *extra)


class Strips:

    @staticmethod
    def scratch(rows, right, depth):
        return [
            pltpu.VMEM((2, rows, depth), bf16),
            pltpu.VMEM((2, depth, right), bf16),
            pltpu.SemaphoreType.DMA((2, 2)),
        ]

    def __init__(self, whole, right_ref, target, held, done, sems):
        self.whole, self.right_ref, self.target = whole, right_ref, target
        self.held, self.done, self.sems = held, done, sems
        self.depth = held.shape[2]
        self.count = whole.shape[1] // self.depth

    def strip(self, at):
        return pl.ds(pl.multiple_of(at * self.depth, self.depth), self.depth)

    def load(self, at):
        slot = lax.rem(at, 2)
        return pltpu.make_async_copy(self.whole.at[:, self.strip(at)], self.held.at[slot], self.sems.at[0, slot])

    def store(self, at):
        slot = lax.rem(at, 2)
        return pltpu.make_async_copy(self.done.at[slot], self.target.at[self.strip(at)], self.sems.at[1, slot])

    def start(self):
        for at in range(2):
            self.load(at).start()

    def run(self):
        @pl.loop(0, self.count)
        def _(at):
            slot = lax.rem(at, 2)
            self.load(at).wait()

            @pl.when(at >= 2)
            def _():
                self.store(at - 2).wait()

            self.done[slot] = dot(self.held[slot], self.right_ref[...], 0, 0).astype(bf16)
            self.store(at).start()

            @pl.when(at + 2 < self.count)
            def _():
                self.load(at + 2).start()

    def finish(self):
        for at in range(self.count - 2, self.count):
            self.store(at).wait()


def back_sum_kernel(
    group, out_live, slope, down, up, second, attended_ref, out_ref, params_ref, bias_ref,
    after_ref, low_ref, sums_ref, grad_up, grad_pre_ref, own_ref, live_v, slope_v, down_v, up_v, sems, *refs,
):
    here = own_ref.shape[0]
    wide = down.shape[0]
    tile = math.gcd(1024, wide)
    order = PlaneSum.order(group, True)

    def rows_of(core, inner):
        return pl.ds(pl.multiple_of((core * group + inner) * here, here), here)

    slots = live_v.shape[0]

    def loads(turn):
        core = total.core if order[turn] % 2 else 1 - total.core
        rows, slot = rows_of(core, total.targets[order[turn] // 2]), turn % slots
        return (
            pltpu.make_async_copy(out_live.at[rows, :], live_v.at[slot], sems.at[0, slot]),
            pltpu.make_async_copy(slope.at[rows, :], slope_v.at[slot], sems.at[1, slot]),
        )

    def start_loads(turn):
        if turn < 2 * group:
            for load in loads(turn):
                load.start()

    down_load = pltpu.make_async_copy(down, down_v, sems.at[0, slots])
    up_load = pltpu.make_async_copy(up, up_v, sems.at[1, slots])

    def prepare(core, inner, at):
        turn = order.index(at)
        slot = turn % slots
        for load in loads(turn):
            load.wait()
        if turn == 0:
            down_load.wait()
        else:
            start_loads(turn + slots - 1)
        rows = rows_of(core, inner)

        @pl.loop(0, wide // tile)
        def _(i):
            columns = pl.ds(pl.multiple_of(i * tile, tile), tile)
            value = dot(live_v[slot], down_v[columns, :], 1, 1) * slope_v[slot, :, columns].astype(f32)
            value = value.astype(bf16)
            grad_pre_ref[rows, columns] = value
            bias_ref[:, columns] += jnp.sum(value.astype(f32), axis=0, keepdims=True)

        if turn == 0:
            up_load.wait()

    strips = Strips(second, grad_pre_ref, grad_up, *refs[:3])
    total = PlaneSum(group, row_product(group, here, True, grad_pre_ref, up_v), own_ref, *refs[3:], prepare=prepare)
    down_load.start()
    for turn in range(slots):
        start_loads(turn)
        if turn == 0:
            up_load.start()
    bias_ref[...] = jnp.zeros_like(bias_ref)
    strips.start()
    greet(total.core, total.inner, group)
    total.run(True, strips.run)
    close_second(total.inner, own_ref, (attended_ref, out_ref, params_ref), (after_ref, low_ref, sums_ref))
    strips.finish()


def back_sum(out_live, slope, down, up, second, attended, out_own, params, group, collective_id):
    rows, width = out_live.shape
    here, wide = rows // (2 * group), down.shape[0]
    local = pl.BlockSpec(memory_space=pltpu.VMEM)
    anywhere = pl.BlockSpec(memory_space=pl.ANY)
    bias, grad_after, low, sums, grad_up = pl.pallas_call(
        functools.partial(back_sum_kernel, group),
        out_shape=[
            jax.ShapeDtypeStruct((1, wide), f32),
            jax.ShapeDtypeStruct((here, width), f32),
            jax.ShapeDtypeStruct((here, width), bf16),
            jax.ShapeDtypeStruct((8, width), f32),
            jax.ShapeDtypeStruct((width, wide), bf16),
        ],
        in_specs=[anywhere] * 5 + [local] * 3,
        out_specs=[local] * 4 + [anywhere],
        scratch_shapes=[
            pltpu.VMEM((rows, wide), bf16),
            pltpu.VMEM((here, width), f32),
            pltpu.VMEM((4, here, width), bf16),
            pltpu.VMEM((4, here, wide), bf16),
            pltpu.VMEM(down.shape, bf16),
            pltpu.VMEM(up.shape, bf16),
            pltpu.SemaphoreType.DMA((2, 5)),
            *Strips.scratch(rows, wide, 1024 // group),
            *PlaneSum.scratch(group, here, width),
        ],
        compiler_params=pltpu.CompilerParams(
            collective_id=collective_id, has_side_effects=True, vmem_limit_bytes=63 * 2**20
        ),
        cost_estimate=pl.CostEstimate(
            flops=4 * rows * width * wide, bytes_accessed=50 * rows * width, transcendentals=0
        ),
    )(out_live, slope, down, up, second, attended, out_own, params)
    return bias[0], grad_after, low, sums, grad_up


def closing_kernel(
    planes, group, unit, repeats, terms, attn, out_ref, *refs
):
    weight_refs, refs = refs[:3], refs[3:]
    attn_all, from_plane, summed, from_z, plane_sems, z_sems = refs[:6]
    exchange = PlaneExchange(group, attn, attn_all, *refs[6:])
    team = 2 * group
    z_at, core_at, inner_at, mine = lax.axis_index("z"), exchange.core, exchange.inner, exchange.mine
    greet_all(core_at, inner_at, group, planes)
    copies = []
    for step in range(1, team):
        core, inner = other_device(core_at, inner_at, group, step)
        copy = send(
            terms.at[core * group + inner],
            from_plane.at[step],
            plane_sems.at[0, step],
            plane_sems.at[1, step],
            core,
            inner,
        )
        copy.start()
        copies.append(copy)
    exchange.start()
    summed[...] = terms[mine]
    for copy in copies:
        copy.wait_recv()
    for step in range(1, team):
        summed[...] += from_plane[step]
    more = []
    for step in range(1, planes):
        to = lax.rem(z_at + step, planes)
        copy = pltpu.make_async_remote_copy(
            src_ref=summed.at[to],
            dst_ref=from_z.at[step],
            send_sem=z_sems.at[0, step],
            recv_sem=z_sems.at[1, step],
            device_id={"z": to},
            device_id_type=MESH,
        )
        copy.start()
        more.append(copy)
    exchange.finish()
    cols = unit * repeats
    for i in range(3):
        place_columns(weight_refs[i], attn_all, i * cols, unit, repeats, team)
    out_ref[...] = summed[z_at]
    for step, copy in enumerate(more, 1):
        copy.wait_recv()
        out_ref[...] += from_z[step]
    for copy in copies + more:
        copy.wait_send()


def closing(terms, attn, planes, group, unit, collective_id):
    team, _, lines, _ = terms.shape
    rows, cols = attn.shape[1], attn.shape[2] // 3
    weight = jax.ShapeDtypeStruct((rows, cols * team), bf16)
    return pl.pallas_call(
        functools.partial(closing_kernel, planes, group, unit, cols // unit),
        out_shape=[
            jax.ShapeDtypeStruct((lines, 128), f32),
            weight,
            weight,
            weight,
        ],
        in_specs=[LOCAL, ANY],
        out_specs=[LOCAL] * 4,
        scratch_shapes=[
            pltpu.VMEM(attn.shape, bf16),
            pltpu.VMEM((team, planes, lines, 128), f32),
            pltpu.VMEM((planes, lines, 128), f32),
            pltpu.VMEM((planes, lines, 128), f32),
            pltpu.SemaphoreType.DMA((2, team)),
            pltpu.SemaphoreType.DMA((2, planes)),
            *PlaneExchange.scratch(group),
        ],
        compiler_params=talk(collective_id, 40),
        cost_estimate=cost(0, 10**8),
    )(terms, attn)


def body(
    layer_input,
    first_gain,
    first_shift,
    query_weight,
    key_weight,
    value_weight,
    output_weight,
    query_bias,
    value_bias,
    output_bias,
    second_gain,
    second_shift,
    up_weight,
    up_bias,
    down_weight,
    down_bias,
    segment_counts,
    out_grad,
):
    here, width = layer_input.shape
    wide = up_weight.shape[1]
    planes = lax.axis_size("z")
    group = lax.axis_size("fsdp")
    team = 2 * group
    z_at, core_at, inner_at = (lax.axis_index(name) for name in ALL)
    plane_at = core_at * group + inner_at
    seg_rows = here * group
    own_rows = query_weight.shape[0]
    own_wide = down_weight.shape[0]
    cols = width // team
    heads_here = cols // HEAD
    whole_heads = own_rows % HEAD == 0

    def to_columns(weight, unit):
        cut = weight.reshape(weight.shape[0], planes, team, unit)
        return cut.transpose(2, 0, 1, 3).reshape(team, weight.shape[0], planes * unit)

    def head_columns(weight):
        if whole_heads:
            return to_columns(weight, own_rows)
        return weight.reshape(own_rows, team, cols).transpose(1, 0, 2)

    attn_blocks = jnp.concatenate([head_columns(w) for w in (query_weight, key_weight, value_weight)], axis=2)
    out_here = z_gather(output_weight) if whole_heads else lax.all_gather(output_weight, ALL, axis=0, tiled=True)
    attn_cols, up_cols = plane_exchange(attn_blocks, up_weight, own_wide, planes, group, 0)
    attn_cols = attn_cols.reshape(team * own_rows, 3 * cols)
    up_cols = up_cols.reshape(team * own_rows, wide // team)
    attn_full = z_gather(after(attn_cols, out_here))
    small = jnp.concatenate(
        [first_gain, first_shift, query_bias, value_bias, output_bias, second_gain, second_shift, down_bias, up_bias]
    )
    length = small.shape[0]
    small = jnp.pad(small.astype(f32), (0, -length % 1024)).reshape(-1, 128)
    segment = 2 * z_at + jnp.arange(2, dtype=jnp.int32)
    place = segment % MAXSEG
    present = place < segment_counts[segment // MAXSEG]
    pos = jnp.arange(seg_rows, dtype=jnp.int32)
    live = present[:, None] & ((pos >= PRE)[None] | (place[:, None] >= PREV - pos[None] // SUMM))
    live_own = lax.dynamic_slice(live, (core_at, inner_at * here), (1, here))[0]
    out_own = jnp.where(live_own[:, None], out_grad, jnp.zeros_like(out_grad))
    all_rows, small_all, out_live = entry(after(layer_input, up_cols), small, out_own, planes, group, 1)
    all_rows = all_rows.reshape(-1, width)
    small_all = small_all.swapaxes(0, 1).reshape(planes * team, -1)
    params = small_all[:, : 8 * own_rows].reshape(planes * team, 8, own_rows).swapaxes(0, 1).reshape(8, width)
    bias_up = small_all[:, 8 * own_rows : length].reshape(planes, team, own_wide)[:, plane_at].reshape(wide // team)

    def own_columns(bias):
        if whole_heads:
            return bias.reshape(planes, team, own_rows)[:, plane_at].reshape(cols)
        return lax.dynamic_slice_in_dim(bias, plane_at * cols, cols)

    bias_q, bias_v = own_columns(params[BIAS_Q]), own_columns(params[BIAS_V])
    out_full = out_here if whole_heads else lax.dynamic_slice_in_dim(out_here, plane_at * cols, cols)
    up_full = z_gather(up_cols)
    down_full = z_gather(after(down_weight, up_cols))
    normed_low, qkv, mixed_low, totals, out_live = attend(
        all_rows,
        attn_full,
        params,
        jnp.concatenate([bias_q, jnp.zeros_like(bias_q), bias_v]),
        live,
        out_own,
        out_live,
        group,
        11,
    )
    out_live = out_live.reshape(-1, width)
    attended, second_own = product_sum(
        mixed_low,
        out_full,
        False,
        close_attention,
        [layer_input, params],
        [(here, f32), (here, bf16)],
        group,
        2,
    )
    second_low, activated, slope = gather_up(second_own, up_full, bias_up, group, 3)
    grad_down = dot(activated, out_live, 0, 0).astype(bf16)
    out_live = after(out_live, grad_down)
    grad_down = z_sum(grad_down)
    grad_up_bias, grad_after, after_low_own, second_sums, grad_up = back_sum(
        out_live, slope, down_full, up_full, second_low, attended, out_own, params, group, 5
    )
    first_mixed, first_output = gather_mixed(after_low_own, out_full, mixed_low, group, 6)
    grad_up = z_sum(after(grad_up, grad_down, first_mixed)).reshape(team, own_rows, wide // team)
    second_mixed, grad_output = gather_mixed(after_low_own, out_full, mixed_low, group, 7, first_output)
    grad_qkv, layer_output, grad_bias, grad_attn = attend_back(
        qkv, (first_mixed, second_mixed), live, totals, params, activated, down_full, attended, normed_low, group, 4
    )
    grad_bias = grad_bias[0]
    grad_attn = z_sum(after(grad_attn, grad_up)).reshape(team, own_rows, 3 * cols)
    input_grad, first_sums, grad_up, *summed = product_sum(
        grad_qkv,
        attn_full,
        True,
        close_first,
        [layer_input, params, grad_after],
        [(here, f32), (8, f32)],
        group,
        8,
        planes,
        grad_up,
        grad_output if whole_heads else None,
    )
    own_pos = inner_at * here + jnp.arange(here, dtype=jnp.int32)
    input_grad = jnp.where((own_pos >= SUMM)[:, None], input_grad, 0.0)

    if not whole_heads:
        spread = jnp.zeros((width, width), bf16)
        spread = lax.dynamic_update_slice_in_dim(spread, grad_output.astype(bf16), plane_at * cols, 0)
        grad_output = lax.psum_scatter(spread, ALL, scatter_dimension=0, tiled=True)
    else:
        (grad_output,) = summed

    def spread_columns(bias):
        if whole_heads:
            full = jnp.zeros((planes, team, own_rows), f32)
            return lax.dynamic_update_slice(full, bias.reshape(planes, 1, own_rows), (0, plane_at, 0)).reshape(width)
        return lax.dynamic_update_slice(jnp.zeros((width,), f32), bias, (plane_at * cols,))

    sums = [
        first_sums[0],
        first_sums[1],
        spread_columns(grad_bias[:cols]),
        spread_columns(grad_bias[2 * cols :]),
        second_sums[2],
        second_sums[0],
        second_sums[1],
        second_sums[3],
    ]
    up_spread = jnp.zeros((planes, team, own_wide), f32)
    up_spread = lax.dynamic_update_slice(up_spread, grad_up_bias.reshape(planes, 1, own_wide), (0, plane_at, 0))
    packed = jnp.concatenate(
        [a.reshape(planes * team, own_rows) for a in sums] + [up_spread.reshape(planes * team, own_wide)], axis=1
    )
    packed = jnp.pad(packed, ((0, 0), (0, -length % 1024))).reshape(planes, team, -1, 128).swapaxes(0, 1)
    packed, *grad_weights = closing(
        packed, grad_attn, planes, group, own_rows if whole_heads else cols, 9
    )
    packed = packed.reshape(-1)
    small_grads = [packed[i * own_rows : (i + 1) * own_rows] for i in range(8)]
    return (
        layer_output,
        input_grad,
        small_grads[0],
        small_grads[1],
        *[weight.astype(f32) for weight in grad_weights],
        grad_output.astype(f32),
        small_grads[2],
        small_grads[3],
        small_grads[4],
        small_grads[5],
        small_grads[6],
        grad_up.astype(f32),
        packed[8 * own_rows : length],
        grad_down.astype(f32),
        small_grads[7],
    )


def solution(mesh):
    outer, inner = mesh.devices.shape
    fine = Mesh(mesh.devices.reshape(outer // 2, 2, inner), ALL)
    rows, vector = P(ALL, None), P(ALL)
    return jax.shard_map(
        body,
        mesh=fine,
        in_specs=(
            rows, vector, vector, rows, rows, rows, rows, vector, vector, vector, vector, vector,
            rows, vector, rows, vector, P(), rows,
        ),
        out_specs=(
            rows, rows, vector, vector, rows, rows, rows, rows, vector, vector, vector, vector, vector,
            rows, vector, rows, vector,
        ),
        check_vma=False,
    )
```

time: 645 us -> 544 us (0.84)
  matrix products: 82.4 us -> 14.3 us
  other arithmetic: 32.8 us -> 13 us
  local copies, waits for them, and re-layouts: 32.1 us -> 18.6 us
  Pallas kernels: 449 us -> 458 us
  waiting for transfers between devices: 27.1 us -> 18.3 us
    dot_general x7 -> x1, matrix products: 82.4 us -> 14.3 us  [dot(): lax.dot_general(a, b, (((ca,), (cb,)), ((), ())), preferred_element_type=...]
    pallas_call x11 -> x9, Pallas kernels: 338 us -> 367 us  [the longest x2 103 us: product_sum(): pl.pallas_call(functools.partial(product_sum_kernel, group, planes, flip,...]
    reduce_sum x9 -> x0, other arithmetic: 17.7 us -> none  [the longest x2 5.28 us: normalize_back(): jnp.sum(grad_rows * unit_rows, axis=0)]
    pallas_call x1, Pallas kernels: 51.2 us -> 39.9 us  [attend(): pl.pallas_call(functools.partial(attend_kernel, block, group), out_shape=...]
    convert_element_type x11 -> x0, local copies, waits for them, and re-layouts: 10.1 us -> none  [the longest x9 6.65 us: body(): head_rows(grad_attn[:, :, i * cols:(i + 1) * cols]).astype(f32)]
    pallas_call x1, Pallas kernels: 59.2 us -> 51.6 us  [attend_back(): pl.pallas_call(functools.partial(attend_back_kernel, block, group), out_s...]
    reduce_scatter x4 -> x3, waiting for transfers between devices: 13.5 us -> 7.74 us  [z_sum(): lax.psum_scatter(partial.astype(bf16), 'z', scatter_dimension=0, tiled=True)]
  transfers between devices with their start and end apart: 8 -> 7, of which waited for: 2 -> 2; matrix products, arithmetic and copies ran while one was open for 20% -> 7% of each run, Pallas kernels for 66% -> 82%
where the time goes in v3:
time: 544 us; the launch traced here: 538 us
  Pallas kernels  458 us (84%)
  local copies, waits for them, and re-layouts  18.6 us (3%)
  waiting for transfers between devices  18.3 us (3%)
  between operations  14.9 us (3%)
  matrix products  14.3 us (3%)
  other arithmetic  13 us (2%)
    pallas_call x2, Pallas kernels, product_sum(): pl.pallas_call(functools.partial(product_sum_kernel, group, planes, flip,...  103 us
    pallas_call x1, Pallas kernels, entry(): pl.pallas_call(functools.partial(entry_kernel, planes, group), out_shape=...  62.8 us
    pallas_call x2, Pallas kernels, gather_mixed(): pl.pallas_call(functools.partial(gather_mixed_kernel, group, len(extra)),...  55.8 us
    pallas_call x1, Pallas kernels, back_sum(): pl.pallas_call(functools.partial(back_sum_kernel, group), out_shape=[jax....  53.8 us
    pallas_call x1, Pallas kernels, attend_back(): pl.pallas_call(functools.partial(attend_back_kernel, block, group), out_s...  51.6 us
    pallas_call x1, Pallas kernels, gather_up(): pl.pallas_call(functools.partial(gather_up_kernel, group), out_shape=[jax...  47.2 us
    pallas_call x1, Pallas kernels, attend(): pl.pallas_call(functools.partial(attend_kernel, block, group), out_shape=...  39.9 us
    pallas_call x1, Pallas kernels, plane_exchange(): pl.pallas_call(functools.partial(swap_kernel, group, unit, repeats), out_...  26.9 us
  transfers between devices with their start and end apart: 7, of which 2 were waited for; matrix products, arithmetic and copies ran while one was open for 7% of the time, Pallas kernels for 82%

profile of v3, /device:TPU:0, one launch (start us, length us, event | category | flops | bytes accessed | tf_op | source)
XLA Modules:
  0.0 537.9 jit_solution(6306642584556784187)
XLA Ops:
  8.0 1.5 reshape.366
  10.0 1.5 reshape.368
  14.2 26.9 %shard_map.305 = (bf16[8,64,768]{2,1,0:T(8,128)(2,1)}, bf16[8,64,1024]{2,1,0:T(8,128)(2,1)}) custom-call(bf16[8,64,768]{2,1,0:T(8,128)(2,1)} %pad_maximum_fusion.attn, bf16[64,8192]{1,0:T(8,128)(2,1)} %up.1), custom_call_target="tpu_custom_call" | custom-call | bytes 73400320 | tf_op jit(solution)/shard_map/pallas_call | solution.py:548
  44.2 1.1 broadcast_select_fusion.1.out_ref.source
  45.3 62.8 %shard_map.306 = (bf16[8,256,2048]{2,1,0:T(8,128)(2,1)}, f32[8,4,8,128]{3,2,1,0:T(8,128)}, bf16[8,256,2048]{2,1,0:T(8,128)(2,1)}) custom-call(bf16[256,2048]{1,0:T(8,128)(2,1)} %refs_0_.3, f32[8,128]{1,0:T(8,128)} %bitcast_convert_fusion.small_ref, bf16[256,2048]{1,0:T(8,128)(2,1)} %broadcast_select_fusion.1.out_ref.source), custom_call_target="tpu_custom_call" | custom-call | bytes 209715200 | tf_op jit(solution)/shard_map/pallas_call | solution.py:612
  112.1 39.9 %shard_map.307 = (bf16[2048,2048]{1,0:T(8,128)(2,1)}, bf16[2048,768]{1,0:T(8,128)(2,1)}, bf16[2048,256]{1,0:T(8,128)(2,1)}, f32[2,8,1024]{2,1,0:T(8,128)}, bf16[8,256,2048]{2,1,0:T(8,128)(2,1)}) custom-call(bf16[2048,2048]{1,0:T(8,128)(2,1)} %bitcast.82, bf16[2048,768]{1,0:T(8,128)(2,1)} %all-gather.7.cloned.1.call-done.w_ref, ...), custom_call_target="tpu_custom_call", output_to_operand_aliasing={{4}: (6, {})} | custom-call | flops 7516192768 | bytes 100000000 | tf_op jit(solution)/shard_map/pallas_call | solution.py:784
  152.0 45.3 %shard_map.308 = (f32[256,2048]{1,0:T(8,128)}, bf16[256,2048]{1,0:T(8,128)(2,1)}) custom-call(bf16[2048,256]{1,0:T(8,128)(2,1)} %get-tuple-element.68.a_ref.mixed_ref, bf16[256,2048]{1,0:T(8,128)(2,1)} %all-gather.5.cloned.1.call-done.w_ref, bf16[256,2048]{1,0:T(8,128)(2,1)} %refs_0_.3, f32[8,2048]{1,0:T(8,128)} %reshape.379.params_ref.refs_1_), custom_call_target="tpu_custom_call" | custom-call | flops 2147483648 | bytes 419430400 | tf_op jit(solution)/shard_map/pallas_call | solution.py:741
  197.4 47.2 %shard_map.309 = (bf16[8,256,2048]{2,1,0:T(8,128)(2,1)}, bf16[2048,1024]{1,0:T(8,128)(2,1)}, bf16[2048,1024]{1,0:T(8,128)(2,1)}) custom-call(bf16[256,2048]{1,0:T(8,128)(2,1)} %get-tuple-element.69.source, bf16[2048,1024]{1,0:T(8,128)(2,1)} %all-gather.9.cloned.1.call-done.up_ref.up, f32[1,1024]{1,0:T(1,128)} %bitcast.81), custom_call_target="tpu_custom_call" | custom-call | flops 8589934592 | bytes 209715200 | tf_op jit(solution)/shard_map/pallas_call | solution.py:929
  244.6 14.3 %convolution_convert_fusion = bf16[1024,2048]{1,0:T(8,128)(2,1)} fusion(bf16[2048,1024]{1,0:T(8,128)(2,1)} %get-tuple-element.70.a, bf16[2048,2048]{1,0:T(8,128)(2,1)} %bitcast.83), kind=kOutput, calls=%fused_computation.1 | convolution fusion | flops 8592031744 | bytes 16777216 | tf_op jit(solution)/shard_map/dot_general | solution.py:29
  258.9 8.6 %all-gather.11.cloned.1.call-done.down.w = bf16[1024,2048]{1,0:T(8,128)(2,1)} async-done(((bf16[256,2048]{1,0:T(8,128)(2,1)}), bf16[1024,2048]{1,0:T(8,128)(2,1)}) %all-gather.11.cloned.1.call-update) | async-done | bytes 4194320 | tf_op jit(solution)/shard_map/all_gather | solution.py:33
  267.5 53.8 %shard_map.310 = (f32[1,1024]{1,0:T(1,128)}, f32[256,2048]{1,0:T(8,128)}, bf16[256,2048]{1,0:T(8,128)(2,1)}, f32[8,2048]{1,0:T(8,128)}, bf16[2048,1024]{1,0:T(8,128)(2,1)}) custom-call(bf16[2048,2048]{1,0:T(8,128)(2,1)} %bitcast.84, bf16[2048,1024]{1,0:T(8,128)(2,1)} %get-tuple-element.72.slope, bf16[1024,2048]{1,0:T(8,128)(2,1)} %all-gather.11.cloned.1.call-done.down.w, ...), custom_call_target="tpu_custom_call" | custom-call | flops 17179869184 | bytes 209715200 | tf_op jit(solution)/shard_map/pallas_call | solution.py:1121
  321.3 26.7 %shard_map.311 = (bf16[1024,256]{1,0:T(8,128)(2,1)}, f32[256,2048]{1,0:T(8,128)}) custom-call(bf16[256,2048]{1,0:T(8,128)(2,1)} %get-tuple-element.76.array, bf16[256,2048]{1,0:T(8,128)(2,1)} %all-gather.5.cloned.1.call-done.w_ref, bf16[2048,256]{1,0:T(8,128)(2,1)} %get-tuple-element.68.a_ref.mixed_ref), custom_call_target="tpu_custom_call" | custom-call | flops 2147483648 | bytes 104857600 | tf_op jit(solution)/shard_map/pallas_call | solution.py:978
  348.3 1.3 copy.51
  349.6 29.1 %shard_map.312 = (bf16[1024,256]{1,0:T(8,128)(2,1)}, bf16[256,2048]{1,0:T(8,128)(2,1)}) custom-call(bf16[256,2048]{1,0:T(8,128)(2,1)} %get-tuple-element.76.array, bf16[256,2048]{1,0:T(8,128)(2,1)} %all-gather.5.cloned.1.call-done.w_ref, bf16[2048,256]{1,0:T(8,128)(2,1)} %get-tuple-element.68.a_ref.mixed_ref, f32[256,2048]{1,0:T(8,128)} %get-tuple-element.78.refs_0_), custom_call_target="tpu_custom_call" | custom-call | flops 2147483648 | bytes 104857600 | tf_op jit(solution)/shard_map/pallas_call | solution.py:978
  378.7 51.6 %shard_map.313 = (bf16[2048,768]{1,0:T(8,128)(2,1)}, bf16[256,2048]{1,0:T(8,128)(2,1)}, f32[1,768]{1,0:T(1,128)}, bf16[2048,768]{1,0:T(8,128)(2,1)}) custom-call(bf16[2048,768]{1,0:T(8,128)(2,1)} %get-tuple-element.66.qkv_ref, bf16[1024,256]{1,0:T(8,128)(2,1)} %get-tuple-element.77.first_ref, bf16[1024,256]{1,0:T(8,128)(2,1)} %get-tuple-element.79.second_ref, ...), custom_call_target="tpu_custom_call" | custom-call | flops 10737418240 | bytes 100000000 | tf_op jit(solution)/shard_map/pallas_call | solution.py:881
  431.6 2.8 convert_element_type.54
  434.4 57.9 %shard_map.314 = (f32[256,2048]{1,0:T(8,128)}, f32[8,2048]{1,0:T(8,128)}, bf16[64,8192]{1,0:T(8,128)(2,1)}, f32[64,2048]{1,0:T(8,128)}) custom-call(bf16[2048,768]{1,0:T(8,128)(2,1)} %get-tuple-element.83.a_ref, bf16[2048,768]{1,0:T(8,128)(2,1)} %all-gather.7.cloned.1.call-done.w_ref, bf16[256,2048]{1,0:T(8,128)(2,1)} %refs_0_.3, ...), custom_call_target="tpu_custom_call" | custom-call | flops 6442450944 | bytes 419430400 | tf_op jit(solution)/shard_map/pallas_call | solution.py:741
  492.3 1.1 slice_reduce_fusion
  493.9 2.7 convert_element_type.53
  496.7 1.5 broadcast_select_fusion
  498.2 7.7 %reduce-scatter.8.cloned.1.call-done = bf16[512,768]{1,0:T(8,128)(2,1)} async-done(((bf16[2048,768]{1,0:T(8,128)(2,1)}), bf16[512,768]{1,0:T(8,128)(2,1)}) %reduce-scatter.8.cloned.1.call-update) | async-done | bytes 786448 | tf_op jit(solution)/shard_map/reduce_scatter | solution.py:37
  505.9 1.1 copy-done.2
  507.1 17.3 %shard_map.315 = (f32[8,128]{1,0:T(8,128)S(1)}, bf16[64,2048]{1,0:T(8,128)(2,1)S(1)}, bf16[64,2048]{1,0:T(8,128)(2,1)S(1)}, bf16[64,2048]{1,0:T(8,128)(2,1)S(1)}) custom-call(f32[8,4,8,128]{3,2,1,0:T(8,128)S(1)} %copy_bitcast_fusion.5.terms, bf16[8,64,768]{2,1,0:T(8,128)(2,1)S(1)} %bitcast.60), custom_call_target="tpu_custom_call" | custom-call | bytes 100000000 | tf_op jit(solution)/shard_map/pallas_call | solution.py:1210
  529.0 1.9 copy.72
  (116 shorter events, 17.5 us)
Async XLA Ops:
  7.2 35.4 %copy-start = (s32[2]{0:T(128)S(1)}, s32[2]{0:T(128)}, u32[]{:S(2)}) copy-start(s32[2]{0:T(128)} %param.34) | copy-start | bytes 28
  7.2 4.8 copy-start.6
  7.2 33.9 %all-gather.5.cloned.1.call-start = ((), (), s32[]{:S(2)}) async-start(), calls=%async_computation.3 | async-start | bytes 1310720 | tf_op jit(solution)/shard_map/all_gather | solution.py:33
  8.0 104.2 %all-gather.7.cloned.1.call-start = ((), (), s32[]{:S(2)}) async-start(), calls=%async_computation.4 | async-start | bytes 3932160 | tf_op jit(solution)/shard_map/all_gather | solution.py:33
  12.6 30.6 %copy-start.9 = (bf16[64]{0:T(256)(128)(2,1)S(1)}, bf16[64]{0:T(256)(128)(2,1)}, u32[]{:S(2)}) copy-start(bf16[64]{0:T(256)(128)(2,1)} %param.19) | copy-start | bytes 388
  12.6 30.6 %copy-start.10 = (bf16[64]{0:T(256)(128)(2,1)S(1)}, bf16[64]{0:T(256)(128)(2,1)}, u32[]{:S(2)}) copy-start(bf16[64]{0:T(256)(128)(2,1)} %param.20) | copy-start | bytes 388
  12.6 30.6 %copy-start.11 = (bf16[64]{0:T(256)(128)(2,1)S(1)}, bf16[64]{0:T(256)(128)(2,1)}, u32[]{:S(2)}) copy-start(bf16[64]{0:T(256)(128)(2,1)} %param.25) | copy-start | bytes 388
  12.6 30.6 %copy-start.12 = (bf16[64]{0:T(256)(128)(2,1)S(1)}, bf16[64]{0:T(256)(128)(2,1)}, u32[]{:S(2)}) copy-start(bf16[64]{0:T(256)(128)(2,1)} %param.26) | copy-start | bytes 388
  12.6 30.6 %copy-start.13 = (bf16[64]{0:T(256)(128)(2,1)S(1)}, bf16[64]{0:T(256)(128)(2,1)}, u32[]{:S(2)}) copy-start(bf16[64]{0:T(256)(128)(2,1)} %param.27) | copy-start | bytes 388
  12.6 30.6 %copy-start.14 = (bf16[64]{0:T(256)(128)(2,1)S(1)}, bf16[64]{0:T(256)(128)(2,1)}, u32[]{:S(2)}) copy-start(bf16[64]{0:T(256)(128)(2,1)} %param.28) | copy-start | bytes 388
  12.7 30.6 %copy-start.15 = (bf16[64]{0:T(256)(128)(2,1)S(1)}, bf16[64]{0:T(256)(128)(2,1)}, u32[]{:S(2)}) copy-start(bf16[64]{0:T(256)(128)(2,1)} %param.29) | copy-start | bytes 388
  12.7 30.6 %copy-start.16 = (bf16[64]{0:T(256)(128)(2,1)S(1)}, bf16[64]{0:T(256)(128)(2,1)}, u32[]{:S(2)}) copy-start(bf16[64]{0:T(256)(128)(2,1)} %param.33) | copy-start | bytes 388
  12.7 30.6 %copy-start.17 = (bf16[256]{0:T(256)(128)(2,1)S(1)}, bf16[256]{0:T(256)(128)(2,1)}, u32[]{:S(2)}) copy-start(bf16[256]{0:T(256)(128)(2,1)} %param.31) | copy-start | bytes 1540
  12.7 31.5 %copy-start.4 = (bf16[256,2048]{1,0:T(8,128)(2,1)S(1)}, bf16[256,2048]{1,0:T(8,128)(2,1)}, u32[]{:S(2)}) copy-start(bf16[256,2048]{1,0:T(8,128)(2,1)} %param.35) | copy-start | bytes 3145732
  41.2 156.2 %all-gather.9.cloned.1.call-start = ((), (), s32[]{:S(2)}) async-start(), calls=%async_computation.5 | async-start | bytes 5242880 | tf_op jit(solution)/shard_map/all_gather | solution.py:33
  41.9 225.6 %all-gather.11.cloned.1.call-start = ((), (), s32[]{:S(2)}) async-start(), calls=%async_computation.6 | async-start | bytes 5242880 | tf_op jit(solution)/shard_map/all_gather | solution.py:33
  42.5 305.6 %reduce-scatter.4.cloned.1.call-start = ((), (), s32[]{:S(2)}) async-start(), calls=%async_computation.7 | async-start | bytes 5242880 | tf_op jit(solution)/shard_map/reduce_scatter | solution.py:37
  258.9 171.5 %reduce-scatter.6.cloned.1.call-start = ((), (), s32[]{:S(2)}) async-start(), calls=%async_computation.8 | async-start | bytes 5242880 | tf_op jit(solution)/shard_map/reduce_scatter | solution.py:37
  348.1 157.9 %reduce-scatter.8.cloned.1.call-start = ((), (), s32[]{:S(2)}) async-start(), calls=%async_computation.9 | async-start | bytes 3932160 | tf_op jit(solution)/shard_map/reduce_scatter | solution.py:37
  378.7 52.6 %copy-start.8 = (f32[1,1024]{1,0:T(1,128)S(1)}, f32[1,1024]{1,0:T(1,128)}, u32[]{:S(2)}) copy-start(f32[1,1024]{1,0:T(1,128)} %get-tuple-element.92) | copy-start | bytes 12292
  434.4 57.9 %copy-start.7 = (f32[8,2048]{1,0:T(8,128)S(1)}, f32[8,2048]{1,0:T(8,128)}, u32[]{:S(2)}) copy-start(f32[8,2048]{1,0:T(8,128)} %get-tuple-element.91) | copy-start | bytes 196612
  492.3 4.4 copy-start.3
  496.5 31.5 %copy-start.5 = (bf16[256,2048]{1,0:T(8,128)(2,1)S(1)}, bf16[256,2048]{1,0:T(8,128)(2,1)}, u32[]{:S(2)}) copy-start(bf16[256,2048]{1,0:T(8,128)(2,1)} %get-tuple-element.140) | copy-start | bytes 3145732
  496.7 34.2 %copy-start.1 = (s32[2]{0:T(128)S(1)}, s32[2]{0:T(128)}, u32[]{:S(2)}) copy-start(s32[2]{0:T(128)} %param.34) | copy-start | bytes 28
  (1 other events, 1.1 us)
Sparse Core Ops, SparseCore 0:
  9.6 30.6 all-gather.4
  41.8 63.8 all-gather.6
  107.3 79.4 all-gather.8
  188.2 79.3 all-gather.10
  269.7 75.2 reduce-scatter.3
  348.2 76.3 reduce-scatter.5
  430.5 75.4 reduce-scatter.7

commit v4 on v3

--- a/solution.py
+++ b/solution.py
@@ -420,7 +420,8 @@
     def scratch(planes, rows, width):
         return [pltpu.VMEM((planes, rows, width), bf16), pltpu.SemaphoreType.DMA((2, planes))]
 
-    def __init__(self, planes, source, out_ref, land, sems):
+    def __init__(self, planes, part, source, out_ref, land, sems):
+        self.columns = pl.ds(part * out_ref.shape[1], out_ref.shape[1])
         self.planes, self.source, self.out_ref, self.land, self.sems = planes, source, out_ref, land, sems
         self.z = lax.axis_index("z")
         self.sent = []
@@ -433,7 +434,7 @@
         for step in range(1, self.planes):
             to = lax.rem(self.z + step, self.planes)
             copy = pltpu.make_async_remote_copy(
-                src_ref=self.source.at[self.rows(to)],
+                src_ref=self.source.at[self.rows(to), self.columns],
                 dst_ref=self.land.at[step],
                 send_sem=self.sems.at[0, step],
                 recv_sem=self.sems.at[1, step],
@@ -444,7 +445,7 @@
             self.sent.append(copy)
 
     def finish(self):
-        self.out_ref[...] = self.source[self.rows(self.z), :].astype(f32)
+        self.out_ref[...] = self.source[self.rows(self.z), self.columns].astype(f32)
         for step, copy in enumerate(self.sent, 1):
             copy.wait()
             self.out_ref[...] += self.land[step].astype(f32)
@@ -706,7 +707,7 @@
     if swap:
         arrived, *refs = refs
         exchange = PlaneExchange(group, ahead[0], arrived, *refs[:2])
-        lines = PlanesSum(planes, ahead[1], placed[1], *refs[2:]) if extra else None
+        lines = PlanesSum(planes, 0, ahead[1], placed[1], *refs[2:]) if extra else None
         greet_all(total.core, total.inner, group, planes)
         if extra:
             lines.start()
@@ -735,8 +736,8 @@
     if terms is not None:
         ahead, places = ahead + [terms], places + [LOCAL]
         rows = terms.shape[0] // planes
-        shapes.append(jax.ShapeDtypeStruct((rows, width), f32))
-        scratch += PlanesSum.scratch(planes, rows, width)
+        shapes.append(jax.ShapeDtypeStruct((rows, width // 2), f32))
+        scratch += PlanesSum.scratch(planes, rows, width // 2)
     extra = terms is not None
     return pl.pallas_call(
         functools.partial(
@@ -805,16 +806,16 @@
 
 
 def attend_back_kernel(
-    block, group, qkv_ref, first_ref, second_ref, live_ref, total_ref, params_ref, a, w, attended, normed, *refs
+    block, group, qkv_ref, first_ref, second_ref, live_ref, total_ref, a, w, normed, *refs
 ):
-    out_ref, layer_ref, column_ref, grad_w, *refs = refs
-    own_ref, a_ref, w_ref, attended_ref, load_sems, bias_ref, sums_ref, *refs = refs
+    out_ref, own_ref, column_ref, grad_w, *refs = refs
+    a_ref, w_ref, load_sems, bias_ref, sums_ref, *refs = refs
     grad_ref = first_ref, second_ref
     seg_rows, heads = qkv_ref.shape[0] // 2, first_ref.shape[1] // HEAD
     cols = heads * HEAD
     loads = [
         pltpu.make_async_copy(whole, held, load_sems.at[i])
-        for i, (whole, held) in enumerate(((a, a_ref), (w, w_ref), (attended, attended_ref)))
+        for i, (whole, held) in enumerate(((a, a_ref), (w, w_ref)))
     ]
     for load in loads:
         load.start()
@@ -847,32 +848,23 @@
     column_ref[:, :cols] = jnp.sum(out_ref[:, :cols].astype(f32), axis=0, keepdims=True)
     strips.run()
     total.finish()
-
-    def do(rows):
-        layer_ref[rows, :] = (
-            attended_ref[rows, :] + own_ref[rows, :] + line(params_ref, BIAS_DOWN)
-        ).astype(bf16)
-
-    chunks(own_ref, do)
     strips.finish()
 
 
-def attend_back(qkv, grads, live, totals, params, a, w, attended, normed, group, collective_id):
+def attend_back(qkv, grads, live, totals, a, w, normed, group, collective_id):
     rows, cols = qkv.shape[0], qkv.shape[1] // 3
     here, width = rows // (2 * group), w.shape[1]
     block = here
     shapes = [
         jax.ShapeDtypeStruct((rows, 3 * cols), bf16),
-        jax.ShapeDtypeStruct((here, width), bf16),
+        jax.ShapeDtypeStruct((here, width), f32),
         jax.ShapeDtypeStruct((1, 3 * cols), f32),
         jax.ShapeDtypeStruct((width, 3 * cols), bf16),
     ]
     scratch = [
-        pltpu.VMEM((here, width), f32),
         pltpu.VMEM(a.shape, bf16),
         pltpu.VMEM(w.shape, bf16),
-        pltpu.VMEM(attended.shape, f32),
-        pltpu.SemaphoreType.DMA((3,)),
+        pltpu.SemaphoreType.DMA((2,)),
         pltpu.VMEM((rows // 2, block), f32),
         pltpu.VMEM((rows // 2, 2 * cols), f32),
         *Strips.scratch(rows, 3 * cols, 1024 // group),
@@ -881,12 +873,12 @@
     return pl.pallas_call(
         functools.partial(attend_back_kernel, block, group),
         out_shape=shapes,
-        in_specs=[LOCAL] * 6 + [ANY] * 4,
+        in_specs=[LOCAL] * 5 + [ANY] * 3,
         out_specs=[LOCAL] * 3 + [ANY],
         scratch_shapes=scratch,
         compiler_params=talk(collective_id, 63),
         cost_estimate=cost(2 * rows * rows * cols + 2 * rows * a.shape[1] * width, 10**8),
-    )(qkv, *grads, live.astype(f32).reshape(rows, 1), totals, params, a, w, attended, normed)
+    )(qkv, *grads, live.astype(f32).reshape(rows, 1), totals, a, w, normed)
 
 
 def gelu_parts(value):
@@ -1150,15 +1142,17 @@
     return bias[0], grad_after, low, sums, grad_up
 
 
-def closing_kernel(
-    planes, group, unit, repeats, terms, attn, out_ref, *refs
-):
-    weight_refs, refs = refs[:3], refs[3:]
+def closing_kernel(planes, group, unit, repeats, extra, terms, attn, *refs):
+    source, refs = refs[:extra], refs[extra:]
+    out_ref, weight_refs, line_ref, refs = refs[0], refs[1:4], refs[4 : 4 + extra], refs[4 + extra :]
     attn_all, from_plane, summed, from_z, plane_sems, z_sems = refs[:6]
-    exchange = PlaneExchange(group, attn, attn_all, *refs[6:])
+    exchange = PlaneExchange(group, attn, attn_all, *refs[6:8])
+    sums = [PlanesSum(planes, 1, *source, *line_ref, *refs[8:])] if extra else []
     team = 2 * group
     z_at, core_at, inner_at, mine = lax.axis_index("z"), exchange.core, exchange.inner, exchange.mine
     greet_all(core_at, inner_at, group, planes)
+    for one in sums:
+        one.start()
     copies = []
     for step in range(1, team):
         core, inner = other_device(core_at, inner_at, group, step)
@@ -1201,22 +1195,27 @@
         out_ref[...] += from_z[step]
     for copy in copies + more:
         copy.wait_send()
-
-
-def closing(terms, attn, planes, group, unit, collective_id):
+    for one in sums:
+        one.finish()
+
+
+def closing(terms, attn, planes, group, unit, collective_id, source=None):
     team, _, lines, _ = terms.shape
     rows, cols = attn.shape[1], attn.shape[2] // 3
     weight = jax.ShapeDtypeStruct((rows, cols * team), bf16)
+    extra = [] if source is None else [source]
+    sums = [(one.shape[0] // planes, one.shape[1] // 2) for one in extra]
     return pl.pallas_call(
-        functools.partial(closing_kernel, planes, group, unit, cols // unit),
+        functools.partial(closing_kernel, planes, group, unit, cols // unit, len(extra)),
         out_shape=[
             jax.ShapeDtypeStruct((lines, 128), f32),
             weight,
             weight,
             weight,
+            *[jax.ShapeDtypeStruct(shape, f32) for shape in sums],
         ],
-        in_specs=[LOCAL, ANY],
-        out_specs=[LOCAL] * 4,
+        in_specs=[LOCAL, ANY] + [LOCAL] * len(extra),
+        out_specs=[LOCAL] * (4 + len(extra)),
         scratch_shapes=[
             pltpu.VMEM(attn.shape, bf16),
             pltpu.VMEM((team, planes, lines, 128), f32),
@@ -1225,10 +1224,11 @@
             pltpu.SemaphoreType.DMA((2, team)),
             pltpu.SemaphoreType.DMA((2, planes)),
             *PlaneExchange.scratch(group),
+            *[one for shape in sums for one in PlanesSum.scratch(planes, *shape)],
         ],
         compiler_params=talk(collective_id, 40),
         cost_estimate=cost(0, 10**8),
-    )(terms, attn)
+    )(terms, attn, *extra)
 
 
 def body(
@@ -1339,8 +1339,8 @@
     first_mixed, first_output = gather_mixed(after_low_own, out_full, mixed_low, group, 6)
     grad_up = z_sum(after(grad_up, grad_down, first_mixed)).reshape(team, own_rows, wide // team)
     second_mixed, grad_output = gather_mixed(after_low_own, out_full, mixed_low, group, 7, first_output)
-    grad_qkv, layer_output, grad_bias, grad_attn = attend_back(
-        qkv, (first_mixed, second_mixed), live, totals, params, activated, down_full, attended, normed_low, group, 4
+    grad_qkv, added, grad_bias, grad_attn = attend_back(
+        qkv, (first_mixed, second_mixed), live, totals, activated, down_full, normed_low, group, 4
     )
     grad_bias = grad_bias[0]
     grad_attn = z_sum(after(grad_attn, grad_up)).reshape(team, own_rows, 3 * cols)
@@ -1357,15 +1357,10 @@
         grad_up,
         grad_output if whole_heads else None,
     )
+    grad_down, added = after(grad_down, input_grad), after(added, input_grad)
+    layer_output = (attended + added + params[BIAS_DOWN]).astype(bf16)
     own_pos = inner_at * here + jnp.arange(here, dtype=jnp.int32)
     input_grad = jnp.where((own_pos >= SUMM)[:, None], input_grad, 0.0)
-
-    if not whole_heads:
-        spread = jnp.zeros((width, width), bf16)
-        spread = lax.dynamic_update_slice_in_dim(spread, grad_output.astype(bf16), plane_at * cols, 0)
-        grad_output = lax.psum_scatter(spread, ALL, scatter_dimension=0, tiled=True)
-    else:
-        (grad_output,) = summed
 
     def spread_columns(bias):
         if whole_heads:
@@ -1389,9 +1384,21 @@
         [a.reshape(planes * team, own_rows) for a in sums] + [up_spread.reshape(planes * team, own_wide)], axis=1
     )
     packed = jnp.pad(packed, ((0, 0), (0, -length % 1024))).reshape(planes, team, -1, 128).swapaxes(0, 1)
+    if not whole_heads:
+        spread = jnp.zeros((width, width), bf16)
+        spread = lax.dynamic_update_slice_in_dim(spread, grad_output, plane_at * cols, 0)
+        last_sum = lax.psum_scatter(spread, ALL, scatter_dimension=0, tiled=True).astype(f32)
     packed, *grad_weights = closing(
-        packed, grad_attn, planes, group, own_rows if whole_heads else cols, 9
+        packed,
+        grad_attn,
+        planes,
+        group,
+        own_rows if whole_heads else cols,
+        9,
+        grad_output if whole_heads else None,
     )
+    if whole_heads:
+        last_sum = jnp.concatenate([*summed, grad_weights.pop()], axis=1)
     packed = packed.reshape(-1)
     small_grads = [packed[i * own_rows : (i + 1) * own_rows] for i in range(8)]
     return (
@@ -1400,7 +1407,7 @@
         small_grads[0],
         small_grads[1],
         *[weight.astype(f32) for weight in grad_weights],
-        grad_output.astype(f32),
+        last_sum,
         small_grads[2],
         small_grads[3],
         small_grads[4],

time: 544 us -> 535 us (0.983)
  waiting for transfers between devices: 18.3 us -> 10.6 us
    reduce_scatter x3, waiting for transfers between devices: 7.74 us -> 0.04 us  [z_sum(): lax.psum_scatter(partial.astype(bf16), 'z', scatter_dimension=0, tiled=True)]
  transfers between devices with their start and end apart: 7 -> 7, of which waited for: 2 -> 1; matrix products, arithmetic and copies ran while one was open for 7% -> 7% of each run, Pallas kernels for 82% -> 83%
where the time goes in v4:
time: 535 us; the launch traced here: 529 us
  Pallas kernels  457 us (85%)
  other arithmetic  15.8 us (3%)
  local copies, waits for them, and re-layouts  15.6 us (3%)
  between operations  14.9 us (3%)
  matrix products  14.3 us (3%)
  waiting for transfers between devices  10.6 us (2%)
    pallas_call x2, Pallas kernels, product_sum(): pl.pallas_call(functools.partial(product_sum_kernel, group, planes, flip,...  104 us
    pallas_call x1, Pallas kernels, entry(): pl.pallas_call(functools.partial(entry_kernel, planes, group), out_shape=...  62.8 us
    pallas_call x2, Pallas kernels, gather_mixed(): pl.pallas_call(functools.partial(gather_mixed_kernel, group, len(extra)),...  55.8 us
    pallas_call x1, Pallas kernels, back_sum(): pl.pallas_call(functools.partial(back_sum_kernel, group), out_shape=[jax....  53.8 us
    pallas_call x1, Pallas kernels, attend_back(): pl.pallas_call(functools.partial(attend_back_kernel, block, group), out_s...  51.1 us
    pallas_call x1, Pallas kernels, gather_up(): pl.pallas_call(functools.partial(gather_up_kernel, group), out_shape=[jax...  47.2 us
    pallas_call x1, Pallas kernels, attend(): pl.pallas_call(functools.partial(attend_kernel, block, group), out_shape=...  39.9 us
    pallas_call x1, Pallas kernels, plane_exchange(): pl.pallas_call(functools.partial(swap_kernel, group, unit, repeats), out_...  26.9 us
  transfers between devices with their start and end apart: 7, of which 1 were waited for; matrix products, arithmetic and copies ran while one was open for 7% of the time, Pallas kernels for 83%

profile of v4, /device:TPU:0, one launch (start us, length us, event | category | flops | bytes accessed | tf_op | source)
XLA Modules:
  0.0 528.9 jit_solution(13416033606602963457)
XLA Ops:
  8.0 1.5 reshape.368
  10.0 1.5 reshape.370
  13.2 0.9 pad_maximum_fusion.attn
  14.2 26.9 %shard_map.305 = (bf16[8,64,768]{2,1,0:T(8,128)(2,1)}, bf16[8,64,1024]{2,1,0:T(8,128)(2,1)}) custom-call(bf16[8,64,768]{2,1,0:T(8,128)(2,1)} %pad_maximum_fusion.attn, bf16[64,8192]{1,0:T(8,128)(2,1)} %up.1), custom_call_target="tpu_custom_call" | custom-call | bytes 73400320 | tf_op jit(solution)/shard_map/pallas_call | solution.py:549
  44.2 1.1 broadcast_select_fusion.1.out_ref.source
  45.3 62.8 %shard_map.306 = (bf16[8,256,2048]{2,1,0:T(8,128)(2,1)}, f32[8,4,8,128]{3,2,1,0:T(8,128)}, bf16[8,256,2048]{2,1,0:T(8,128)(2,1)}) custom-call(bf16[256,2048]{1,0:T(8,128)(2,1)} %refs_0_.3, f32[8,128]{1,0:T(8,128)} %bitcast_convert_fusion.small_ref, bf16[256,2048]{1,0:T(8,128)(2,1)} %broadcast_select_fusion.1.out_ref.source), custom_call_target="tpu_custom_call" | custom-call | bytes 209715200 | tf_op jit(solution)/shard_map/pallas_call | solution.py:613
  108.1 0.9 copy_bitcast_fusion.6
  112.1 39.9 %shard_map.307 = (bf16[2048,2048]{1,0:T(8,128)(2,1)}, bf16[2048,768]{1,0:T(8,128)(2,1)}, bf16[2048,256]{1,0:T(8,128)(2,1)}, f32[2,8,1024]{2,1,0:T(8,128)}, bf16[8,256,2048]{2,1,0:T(8,128)(2,1)}) custom-call(bf16[2048,2048]{1,0:T(8,128)(2,1)} %bitcast.82, bf16[2048,768]{1,0:T(8,128)(2,1)} %all-gather.7.cloned.1.call-done.w_ref, ...), custom_call_target="tpu_custom_call", output_to_operand_aliasing={{4}: (6, {})} | custom-call | flops 7516192768 | bytes 100000000 | tf_op jit(solution)/shard_map/pallas_call | solution.py:785
  152.0 45.3 %shard_map.308 = (f32[256,2048]{1,0:T(8,128)}, bf16[256,2048]{1,0:T(8,128)(2,1)}) custom-call(bf16[2048,256]{1,0:T(8,128)(2,1)} %get-tuple-element.69.a_ref.mixed_ref, bf16[256,2048]{1,0:T(8,128)(2,1)} %all-gather.5.cloned.1.call-done.w_ref, bf16[256,2048]{1,0:T(8,128)(2,1)} %refs_0_.3, f32[8,2048]{1,0:T(8,128)} %reshape.381.params_ref.refs_1_), custom_call_target="tpu_custom_call" | custom-call | flops 2147483648 | bytes 419430400 | tf_op jit(solution)/shard_map/pallas_call | solution.py:742
  197.4 47.2 %shard_map.309 = (bf16[8,256,2048]{2,1,0:T(8,128)(2,1)}, bf16[2048,1024]{1,0:T(8,128)(2,1)}, bf16[2048,1024]{1,0:T(8,128)(2,1)}) custom-call(bf16[256,2048]{1,0:T(8,128)(2,1)} %get-tuple-element.73.source, bf16[2048,1024]{1,0:T(8,128)(2,1)} %all-gather.9.cloned.1.call-done.up_ref.up, f32[1,1024]{1,0:T(1,128)} %bitcast.81), custom_call_target="tpu_custom_call" | custom-call | flops 8589934592 | bytes 209715200 | tf_op jit(solution)/shard_map/pallas_call | solution.py:921
  244.6 14.3 %convolution_convert_fusion = bf16[1024,2048]{1,0:T(8,128)(2,1)} fusion(bf16[2048,1024]{1,0:T(8,128)(2,1)} %get-tuple-element.74.a, bf16[2048,2048]{1,0:T(8,128)(2,1)} %bitcast.83), kind=kOutput, calls=%fused_computation.1 | convolution fusion | flops 8592031744 | bytes 16777216 | tf_op jit(solution)/shard_map/dot_general | solution.py:29
  258.9 8.5 %all-gather.11.cloned.1.call-done.down.w = bf16[1024,2048]{1,0:T(8,128)(2,1)} async-done(((bf16[256,2048]{1,0:T(8,128)(2,1)}), bf16[1024,2048]{1,0:T(8,128)(2,1)}) %all-gather.11.cloned.1.call-update) | async-done | bytes 4194320 | tf_op jit(solution)/shard_map/all_gather | solution.py:33
  267.5 53.8 %shard_map.310 = (f32[1,1024]{1,0:T(1,128)}, f32[256,2048]{1,0:T(8,128)}, bf16[256,2048]{1,0:T(8,128)(2,1)}, f32[8,2048]{1,0:T(8,128)}, bf16[2048,1024]{1,0:T(8,128)(2,1)}) custom-call(bf16[2048,2048]{1,0:T(8,128)(2,1)} %bitcast.84, bf16[2048,1024]{1,0:T(8,128)(2,1)} %get-tuple-element.76.slope, bf16[1024,2048]{1,0:T(8,128)(2,1)} %all-gather.11.cloned.1.call-done.down.w, ...), custom_call_target="tpu_custom_call" | custom-call | flops 17179869184 | bytes 209715200 | tf_op jit(solution)/shard_map/pallas_call | solution.py:1113
  321.3 26.7 %shard_map.311 = (bf16[1024,256]{1,0:T(8,128)(2,1)}, f32[256,2048]{1,0:T(8,128)}) custom-call(bf16[256,2048]{1,0:T(8,128)(2,1)} %get-tuple-element.79.array, bf16[256,2048]{1,0:T(8,128)(2,1)} %all-gather.5.cloned.1.call-done.w_ref, bf16[2048,256]{1,0:T(8,128)(2,1)} %get-tuple-element.69.a_ref.mixed_ref), custom_call_target="tpu_custom_call" | custom-call | flops 2147483648 | bytes 104857600 | tf_op jit(solution)/shard_map/pallas_call | solution.py:970
  348.3 1.3 copy.51
  349.6 29.1 %shard_map.312 = (bf16[1024,256]{1,0:T(8,128)(2,1)}, bf16[256,2048]{1,0:T(8,128)(2,1)}) custom-call(bf16[256,2048]{1,0:T(8,128)(2,1)} %get-tuple-element.79.array, bf16[256,2048]{1,0:T(8,128)(2,1)} %all-gather.5.cloned.1.call-done.w_ref, bf16[2048,256]{1,0:T(8,128)(2,1)} %get-tuple-element.69.a_ref.mixed_ref, f32[256,2048]{1,0:T(8,128)} %get-tuple-element.81.refs_0_), custom_call_target="tpu_custom_call" | custom-call | flops 2147483648 | bytes 104857600 | tf_op jit(solution)/shard_map/pallas_call | solution.py:970
  378.7 51.1 %shard_map.313 = (bf16[2048,768]{1,0:T(8,128)(2,1)}, f32[256,2048]{1,0:T(8,128)}, f32[1,768]{1,0:T(1,128)}, bf16[2048,768]{1,0:T(8,128)(2,1)}) custom-call(bf16[2048,768]{1,0:T(8,128)(2,1)} %get-tuple-element.71.qkv_ref, bf16[1024,256]{1,0:T(8,128)(2,1)} %get-tuple-element.80.first_ref, bf16[1024,256]{1,0:T(8,128)(2,1)} %get-tuple-element.82.second_ref, ...), custom_call_target="tpu_custom_call" | custom-call | flops 10737418240 | bytes 100000000 | tf_op jit(solution)/shard_map/pallas_call | solution.py:873
  431.0 58.4 %shard_map.314 = (f32[256,2048]{1,0:T(8,128)}, f32[8,2048]{1,0:T(8,128)}, bf16[64,8192]{1,0:T(8,128)(2,1)}, f32[64,1024]{1,0:T(8,128)}) custom-call(bf16[2048,768]{1,0:T(8,128)(2,1)} %get-tuple-element.86.a_ref, bf16[2048,768]{1,0:T(8,128)(2,1)} %all-gather.7.cloned.1.call-done.w_ref, bf16[256,2048]{1,0:T(8,128)(2,1)} %refs_0_.3, ...), custom_call_target="tpu_custom_call" | custom-call | flops 6442450944 | bytes 419430400 | tf_op jit(solution)/shard_map/pallas_call | solution.py:742
  489.5 1.6 convert_element_type.58
  491.0 1.0 slice_reduce_fusion.1
  492.5 2.7 convert_element_type.57
  495.4 4.8 add_convert_fusion
  500.2 1.1 copy-done.3
  501.3 16.1 %shard_map.315 = (f32[8,128]{1,0:T(8,128)S(1)}, bf16[64,2048]{1,0:T(8,128)(2,1)S(1)}, bf16[64,2048]{1,0:T(8,128)(2,1)S(1)}, bf16[64,2048]{1,0:T(8,128)(2,1)S(1)}, f32[64,1024]{1,0:T(8,128)S(1)}) custom-call(f32[8,4,8,128]{3,2,1,0:T(8,128)S(1)} %copy_bitcast_fusion.5.terms, bf16[8,64,768]{2,1,0:T(8,128)(2,1)S(1)} %bitcast.60, bf16[256,2048]{1,0:T(8,128)(2,1)S(1)} %copy-done.2), custom_call_target="tpu_custom_call" | custom-call | bytes 100000000 | tf_op jit(solution)/shard_map/pallas_call | solution.py:1208
  (122 shorter events, 15.5 us)
Async XLA Ops:
  7.2 35.4 %copy-start = (s32[2]{0:T(128)S(1)}, s32[2]{0:T(128)}, u32[]{:S(2)}) copy-start(s32[2]{0:T(128)} %param.34) | copy-start | bytes 28
  7.2 4.8 copy-start.7
  7.2 33.9 %all-gather.5.cloned.1.call-start = ((), (), s32[]{:S(2)}) async-start(), calls=%async_computation.3 | async-start | bytes 1310720 | tf_op jit(solution)/shard_map/all_gather | solution.py:33
  8.0 104.2 %all-gather.7.cloned.1.call-start = ((), (), s32[]{:S(2)}) async-start(), calls=%async_computation.4 | async-start | bytes 3932160 | tf_op jit(solution)/shard_map/all_gather | solution.py:33
  13.1 30.1 %copy-start.12 = (bf16[64]{0:T(256)(128)(2,1)S(1)}, bf16[64]{0:T(256)(128)(2,1)}, u32[]{:S(2)}) copy-start(bf16[64]{0:T(256)(128)(2,1)} %param.19) | copy-start | bytes 388
  13.1 30.1 %copy-start.13 = (bf16[64]{0:T(256)(128)(2,1)S(1)}, bf16[64]{0:T(256)(128)(2,1)}, u32[]{:S(2)}) copy-start(bf16[64]{0:T(256)(128)(2,1)} %param.20) | copy-start | bytes 388
  13.1 30.0 %copy-start.14 = (bf16[64]{0:T(256)(128)(2,1)S(1)}, bf16[64]{0:T(256)(128)(2,1)}, u32[]{:S(2)}) copy-start(bf16[64]{0:T(256)(128)(2,1)} %param.25) | copy-start | bytes 388
  13.2 30.0 %copy-start.15 = (bf16[64]{0:T(256)(128)(2,1)S(1)}, bf16[64]{0:T(256)(128)(2,1)}, u32[]{:S(2)}) copy-start(bf16[64]{0:T(256)(128)(2,1)} %param.26) | copy-start | bytes 388
  13.2 30.0 %copy-start.16 = (bf16[64]{0:T(256)(128)(2,1)S(1)}, bf16[64]{0:T(256)(128)(2,1)}, u32[]{:S(2)}) copy-start(bf16[64]{0:T(256)(128)(2,1)} %param.27) | copy-start | bytes 388
  13.2 30.0 %copy-start.17 = (bf16[64]{0:T(256)(128)(2,1)S(1)}, bf16[64]{0:T(256)(128)(2,1)}, u32[]{:S(2)}) copy-start(bf16[64]{0:T(256)(128)(2,1)} %param.28) | copy-start | bytes 388
  13.2 30.0 %copy-start.18 = (bf16[64]{0:T(256)(128)(2,1)S(1)}, bf16[64]{0:T(256)(128)(2,1)}, u32[]{:S(2)}) copy-start(bf16[64]{0:T(256)(128)(2,1)} %param.29) | copy-start | bytes 388
  13.2 30.0 %copy-start.19 = (bf16[64]{0:T(256)(128)(2,1)S(1)}, bf16[64]{0:T(256)(128)(2,1)}, u32[]{:S(2)}) copy-start(bf16[64]{0:T(256)(128)(2,1)} %param.33) | copy-start | bytes 388
  13.2 30.0 %copy-start.20 = (bf16[256]{0:T(256)(128)(2,1)S(1)}, bf16[256]{0:T(256)(128)(2,1)}, u32[]{:S(2)}) copy-start(bf16[256]{0:T(256)(128)(2,1)} %param.31) | copy-start | bytes 1540
  13.2 30.9 %copy-start.6 = (bf16[256,2048]{1,0:T(8,128)(2,1)S(1)}, bf16[256,2048]{1,0:T(8,128)(2,1)}, u32[]{:S(2)}) copy-start(bf16[256,2048]{1,0:T(8,128)(2,1)} %param.35) | copy-start | bytes 3145732
  41.1 156.2 %all-gather.9.cloned.1.call-start = ((), (), s32[]{:S(2)}) async-start(), calls=%async_computation.5 | async-start | bytes 5242880 | tf_op jit(solution)/shard_map/all_gather | solution.py:33
  41.9 225.6 %all-gather.11.cloned.1.call-start = ((), (), s32[]{:S(2)}) async-start(), calls=%async_computation.6 | async-start | bytes 5242880 | tf_op jit(solution)/shard_map/all_gather | solution.py:33
  42.5 305.5 %reduce-scatter.4.cloned.1.call-start = ((), (), s32[]{:S(2)}) async-start(), calls=%async_computation.7 | async-start | bytes 5242880 | tf_op jit(solution)/shard_map/reduce_scatter | solution.py:37
  258.9 171.0 %reduce-scatter.6.cloned.1.call-start = ((), (), s32[]{:S(2)}) async-start(), calls=%async_computation.8 | async-start | bytes 5242880 | tf_op jit(solution)/shard_map/reduce_scatter | solution.py:37
  348.0 152.1 %reduce-scatter.8.cloned.1.call-start = ((), (), s32[]{:S(2)}) async-start(), calls=%async_computation.9 | async-start | bytes 3932160 | tf_op jit(solution)/shard_map/reduce_scatter | solution.py:37
  431.0 58.4 %copy-start.5 = (bf16[256,2048]{1,0:T(8,128)(2,1)S(1)}, bf16[256,2048]{1,0:T(8,128)(2,1)}, u32[]{:S(2)}) copy-start(bf16[256,2048]{1,0:T(8,128)(2,1)} %reduce-scatter.4.cloned.1.call-done) | copy-start | bytes 3145732
  489.4 5.9 %copy-start.4 = (f32[256,2048]{1,0:T(8,128)S(1)}, f32[256,2048]{1,0:T(8,128)}, u32[]{:S(2)}) copy-start(f32[256,2048]{1,0:T(8,128)} %get-tuple-element.70.attended_ref) | copy-start | bytes 6291460
  495.3 4.8 copy-start.2
  495.3 25.7 %copy-start.8 = (f32[64,1024]{1,0:T(8,128)S(1)}, f32[64,1024]{1,0:T(8,128)}, u32[]{:S(2)}) copy-start(f32[64,1024]{1,0:T(8,128)} %get-tuple-element.103) | copy-start | bytes 786436
  495.3 26.5 %copy-start.1 = (s32[2]{0:T(128)S(1)}, s32[2]{0:T(128)}, u32[]{:S(2)}) copy-start(s32[2]{0:T(128)} %param.34) | copy-start | bytes 28
  (4 other events, 4.4 us)
Sparse Core Ops, SparseCore 0:
  9.6 30.6 all-gather.4
  41.8 63.8 all-gather.6
  107.3 79.4 all-gather.8
  188.2 79.2 all-gather.10
  269.6 75.2 reduce-scatter.3
  348.1 76.3 reduce-scatter.5
  430.0 66.1 reduce-scatter.7

commit v5 on v4

--- a/solution.py
+++ b/solution.py
@@ -199,8 +199,8 @@
         own = self.target.at[self.mine]
         if self.group == 4:
             at_x, at_y, _ = beside(self.inner)
-            self.go(self.to_chip(0, self.source, own, at_x))
-            self.go(self.to_chip(1, self.source, own, at_y))
+            for at, part, inner in ((0, self.low, at_x), (1, self.high, at_y), (2, self.high, at_x), (3, self.low, at_y)):
+                self.go(self.to_chip(at, self.source.at[part], self.block(self.core, self.inner, part), inner))
         else:
             for step in range(1, self.group):
                 self.go(self.to_chip(step, self.source, own, lax.rem(self.inner + step, self.group)))
@@ -222,7 +222,7 @@
             at_x, at_y, across = beside(self.inner)
             for at, part in ((2, self.low), (3, self.high)):
                 block = self.block(self.core, across, part)
-                self.to_chip(at, block, block, at_x).wait_recv()
+                self.to_chip(at + 2, block, block, at_x).wait_recv()
                 self.go(self.to_core(at + 1, block, block))
 
     def run(self, use):
@@ -258,16 +258,15 @@
     def relay(self):
         if self.group == 4:
             at_x, at_y, _ = beside(self.inner)
-            block = self.block(self.core, at_x)
-            self.to_chip(0, block, block, at_x).wait_recv()
-            part = self.block(self.core, at_x, self.low)
-            self.go(self.to_chip(2, part, part, at_y))
-            self.go(self.to_core(1, block, block))
-            block = self.block(self.core, at_y)
-            self.to_chip(1, block, block, at_y).wait_recv()
-            part = self.block(self.core, at_y, self.high)
-            self.go(self.to_chip(3, part, part, at_x))
-            self.go(self.to_core(2, block, block))
+            for at, inner, part, onward in ((0, at_x, self.low, at_y), (1, at_y, self.high, at_x)):
+                block = self.block(self.core, inner, part)
+                self.to_chip(at, block, block, inner).wait_recv()
+                self.go(self.to_chip(at + 4, block, block, onward))
+            for at, inner, part in ((2, at_x, self.high), (3, at_y, self.low)):
+                block = self.block(self.core, inner, part)
+                self.to_chip(at, block, block, inner).wait_recv()
+                block = self.block(self.core, inner)
+                self.go(self.to_core(at - 1, block, block))
         else:
             for step in range(1, self.group):
                 inner = lax.rem(self.inner - step + self.group, self.group)

time: 535 us -> 533 us (level)
  no operation moved by 1% of the time
where the time goes in v5:
time: 533 us; the launch traced here: 527 us
  Pallas kernels  454 us (85%)
  other arithmetic  15.8 us (3%)
  local copies, waits for them, and re-layouts  15.6 us (3%)
  between operations  14.9 us (3%)
  matrix products  14.3 us (3%)
  waiting for transfers between devices  11.9 us (2%)
    pallas_call x2, Pallas kernels, product_sum(): pl.pallas_call(functools.partial(product_sum_kernel, group, planes, flip,...  103 us
    pallas_call x1, Pallas kernels, entry(): pl.pallas_call(functools.partial(entry_kernel, planes, group), out_shape=...  62.1 us
    pallas_call x1, Pallas kernels, back_sum(): pl.pallas_call(functools.partial(back_sum_kernel, group), out_shape=[jax....  53.8 us
    pallas_call x2, Pallas kernels, gather_mixed(): pl.pallas_call(functools.partial(gather_mixed_kernel, group, len(extra)),...  52.8 us
    pallas_call x1, Pallas kernels, attend_back(): pl.pallas_call(functools.partial(attend_back_kernel, block, group), out_s...  50.9 us
    pallas_call x1, Pallas kernels, gather_up(): pl.pallas_call(functools.partial(gather_up_kernel, group), out_shape=[jax...  46.6 us
    pallas_call x1, Pallas kernels, attend(): pl.pallas_call(functools.partial(attend_kernel, block, group), out_shape=...  39.9 us
    pallas_call x1, Pallas kernels, plane_exchange(): pl.pallas_call(functools.partial(swap_kernel, group, unit, repeats), out_...  26.9 us
  transfers between devices with their start and end apart: 7, of which 1 were waited for; matrix products, arithmetic and copies ran while one was open for 7% of the time, Pallas kernels for 83%

profile of v5, /device:TPU:0, one launch (start us, length us, event | category | flops | bytes accessed | tf_op | source)
XLA Modules:
  0.0 526.6 jit_solution(3932380486206459167)
XLA Ops:
  8.0 1.5 reshape.368
  10.0 1.5 reshape.370
  13.2 0.9 pad_maximum_fusion.attn
  14.2 26.9 %shard_map.305 = (bf16[8,64,768]{2,1,0:T(8,128)(2,1)}, bf16[8,64,1024]{2,1,0:T(8,128)(2,1)}) custom-call(bf16[8,64,768]{2,1,0:T(8,128)(2,1)} %pad_maximum_fusion.attn, bf16[64,8192]{1,0:T(8,128)(2,1)} %up.1), custom_call_target="tpu_custom_call" | custom-call | bytes 73400320 | tf_op jit(solution)/shard_map/pallas_call | solution.py:548
  44.2 1.1 broadcast_select_fusion.1.out_ref.source
  45.3 62.1 %shard_map.306 = (bf16[8,256,2048]{2,1,0:T(8,128)(2,1)}, f32[8,4,8,128]{3,2,1,0:T(8,128)}, bf16[8,256,2048]{2,1,0:T(8,128)(2,1)}) custom-call(bf16[256,2048]{1,0:T(8,128)(2,1)} %refs_0_.3, f32[8,128]{1,0:T(8,128)} %bitcast_convert_fusion.small_ref, bf16[256,2048]{1,0:T(8,128)(2,1)} %broadcast_select_fusion.1.out_ref.source), custom_call_target="tpu_custom_call" | custom-call | bytes 209715200 | tf_op jit(solution)/shard_map/pallas_call | solution.py:612
  107.4 0.9 copy_bitcast_fusion.6
  111.4 39.9 %shard_map.307 = (bf16[2048,2048]{1,0:T(8,128)(2,1)}, bf16[2048,768]{1,0:T(8,128)(2,1)}, bf16[2048,256]{1,0:T(8,128)(2,1)}, f32[2,8,1024]{2,1,0:T(8,128)}, bf16[8,256,2048]{2,1,0:T(8,128)(2,1)}) custom-call(bf16[2048,2048]{1,0:T(8,128)(2,1)} %bitcast.82, bf16[2048,768]{1,0:T(8,128)(2,1)} %all-gather.7.cloned.1.call-done.w_ref, ...), custom_call_target="tpu_custom_call", output_to_operand_aliasing={{4}: (6, {})} | custom-call | flops 7516192768 | bytes 100000000 | tf_op jit(solution)/shard_map/pallas_call | solution.py:784
  151.3 45.4 %shard_map.308 = (f32[256,2048]{1,0:T(8,128)}, bf16[256,2048]{1,0:T(8,128)(2,1)}) custom-call(bf16[2048,256]{1,0:T(8,128)(2,1)} %get-tuple-element.69.a_ref.mixed_ref, bf16[256,2048]{1,0:T(8,128)(2,1)} %all-gather.5.cloned.1.call-done.w_ref, bf16[256,2048]{1,0:T(8,128)(2,1)} %refs_0_.3, f32[8,2048]{1,0:T(8,128)} %reshape.381.params_ref.refs_1_), custom_call_target="tpu_custom_call" | custom-call | flops 2147483648 | bytes 419430400 | tf_op jit(solution)/shard_map/pallas_call | solution.py:741
  196.7 46.6 %shard_map.309 = (bf16[8,256,2048]{2,1,0:T(8,128)(2,1)}, bf16[2048,1024]{1,0:T(8,128)(2,1)}, bf16[2048,1024]{1,0:T(8,128)(2,1)}) custom-call(bf16[256,2048]{1,0:T(8,128)(2,1)} %get-tuple-element.73.source, bf16[2048,1024]{1,0:T(8,128)(2,1)} %all-gather.9.cloned.1.call-done.up_ref.up, f32[1,1024]{1,0:T(1,128)} %bitcast.81), custom_call_target="tpu_custom_call" | custom-call | flops 8589934592 | bytes 209715200 | tf_op jit(solution)/shard_map/pallas_call | solution.py:920
  243.3 14.3 %convolution_convert_fusion = bf16[1024,2048]{1,0:T(8,128)(2,1)} fusion(bf16[2048,1024]{1,0:T(8,128)(2,1)} %get-tuple-element.74.a, bf16[2048,2048]{1,0:T(8,128)(2,1)} %bitcast.83), kind=kOutput, calls=%fused_computation.1 | convolution fusion | flops 8592031744 | bytes 16777216 | tf_op jit(solution)/shard_map/dot_general | solution.py:29
  257.6 9.9 %all-gather.11.cloned.1.call-done.down.w = bf16[1024,2048]{1,0:T(8,128)(2,1)} async-done(((bf16[256,2048]{1,0:T(8,128)(2,1)}), bf16[1024,2048]{1,0:T(8,128)(2,1)}) %all-gather.11.cloned.1.call-update) | async-done | bytes 4194320 | tf_op jit(solution)/shard_map/all_gather | solution.py:33
  267.5 53.8 %shard_map.310 = (f32[1,1024]{1,0:T(1,128)}, f32[256,2048]{1,0:T(8,128)}, bf16[256,2048]{1,0:T(8,128)(2,1)}, f32[8,2048]{1,0:T(8,128)}, bf16[2048,1024]{1,0:T(8,128)(2,1)}) custom-call(bf16[2048,2048]{1,0:T(8,128)(2,1)} %bitcast.84, bf16[2048,1024]{1,0:T(8,128)(2,1)} %get-tuple-element.76.slope, bf16[1024,2048]{1,0:T(8,128)(2,1)} %all-gather.11.cloned.1.call-done.down.w, ...), custom_call_target="tpu_custom_call" | custom-call | flops 17179869184 | bytes 209715200 | tf_op jit(solution)/shard_map/pallas_call | solution.py:1112
  321.3 25.9 %shard_map.311 = (bf16[1024,256]{1,0:T(8,128)(2,1)}, f32[256,2048]{1,0:T(8,128)}) custom-call(bf16[256,2048]{1,0:T(8,128)(2,1)} %get-tuple-element.79.array, bf16[256,2048]{1,0:T(8,128)(2,1)} %all-gather.5.cloned.1.call-done.w_ref, bf16[2048,256]{1,0:T(8,128)(2,1)} %get-tuple-element.69.a_ref.mixed_ref), custom_call_target="tpu_custom_call" | custom-call | flops 2147483648 | bytes 104857600 | tf_op jit(solution)/shard_map/pallas_call | solution.py:969
  347.5 1.3 copy.51
  348.8 26.9 %shard_map.312 = (bf16[1024,256]{1,0:T(8,128)(2,1)}, bf16[256,2048]{1,0:T(8,128)(2,1)}) custom-call(bf16[256,2048]{1,0:T(8,128)(2,1)} %get-tuple-element.79.array, bf16[256,2048]{1,0:T(8,128)(2,1)} %all-gather.5.cloned.1.call-done.w_ref, bf16[2048,256]{1,0:T(8,128)(2,1)} %get-tuple-element.69.a_ref.mixed_ref, f32[256,2048]{1,0:T(8,128)} %get-tuple-element.81.refs_0_), custom_call_target="tpu_custom_call" | custom-call | flops 2147483648 | bytes 104857600 | tf_op jit(solution)/shard_map/pallas_call | solution.py:969
  375.7 50.9 %shard_map.313 = (bf16[2048,768]{1,0:T(8,128)(2,1)}, f32[256,2048]{1,0:T(8,128)}, f32[1,768]{1,0:T(1,128)}, bf16[2048,768]{1,0:T(8,128)(2,1)}) custom-call(bf16[2048,768]{1,0:T(8,128)(2,1)} %get-tuple-element.71.qkv_ref, bf16[1024,256]{1,0:T(8,128)(2,1)} %get-tuple-element.80.first_ref, bf16[1024,256]{1,0:T(8,128)(2,1)} %get-tuple-element.82.second_ref, ...), custom_call_target="tpu_custom_call" | custom-call | flops 10737418240 | bytes 100000000 | tf_op jit(solution)/shard_map/pallas_call | solution.py:872
  427.8 57.8 %shard_map.314 = (f32[256,2048]{1,0:T(8,128)}, f32[8,2048]{1,0:T(8,128)}, bf16[64,8192]{1,0:T(8,128)(2,1)}, f32[64,1024]{1,0:T(8,128)}) custom-call(bf16[2048,768]{1,0:T(8,128)(2,1)} %get-tuple-element.86.a_ref, bf16[2048,768]{1,0:T(8,128)(2,1)} %all-gather.7.cloned.1.call-done.w_ref, bf16[256,2048]{1,0:T(8,128)(2,1)} %refs_0_.3, ...), custom_call_target="tpu_custom_call" | custom-call | flops 6442450944 | bytes 419430400 | tf_op jit(solution)/shard_map/pallas_call | solution.py:741
  485.6 1.6 convert_element_type.58
  487.2 1.0 slice_reduce_fusion.1
  488.7 2.7 convert_element_type.57
  491.5 4.7 add_convert_fusion
  496.3 1.1 copy-done.3
  497.4 17.6 %shard_map.315 = (f32[8,128]{1,0:T(8,128)S(1)}, bf16[64,2048]{1,0:T(8,128)(2,1)S(1)}, bf16[64,2048]{1,0:T(8,128)(2,1)S(1)}, bf16[64,2048]{1,0:T(8,128)(2,1)S(1)}, f32[64,1024]{1,0:T(8,128)S(1)}) custom-call(f32[8,4,8,128]{3,2,1,0:T(8,128)S(1)} %copy_bitcast_fusion.5.terms, bf16[8,64,768]{2,1,0:T(8,128)(2,1)S(1)} %bitcast.60, bf16[256,2048]{1,0:T(8,128)(2,1)S(1)} %copy-done.2), custom_call_target="tpu_custom_call" | custom-call | bytes 100000000 | tf_op jit(solution)/shard_map/pallas_call | solution.py:1207
  (122 shorter events, 15.5 us)
Async XLA Ops:
  7.2 35.4 %copy-start = (s32[2]{0:T(128)S(1)}, s32[2]{0:T(128)}, u32[]{:S(2)}) copy-start(s32[2]{0:T(128)} %param.34) | copy-start | bytes 28
  7.2 4.8 copy-start.7
  7.2 33.9 %all-gather.5.cloned.1.call-start = ((), (), s32[]{:S(2)}) async-start(), calls=%async_computation.3 | async-start | bytes 1310720 | tf_op jit(solution)/shard_map/all_gather | solution.py:33
  8.0 103.5 %all-gather.7.cloned.1.call-start = ((), (), s32[]{:S(2)}) async-start(), calls=%async_computation.4 | async-start | bytes 3932160 | tf_op jit(solution)/shard_map/all_gather | solution.py:33
  13.1 30.1 %copy-start.12 = (bf16[64]{0:T(256)(128)(2,1)S(1)}, bf16[64]{0:T(256)(128)(2,1)}, u32[]{:S(2)}) copy-start(bf16[64]{0:T(256)(128)(2,1)} %param.19) | copy-start | bytes 388
  13.1 30.1 %copy-start.13 = (bf16[64]{0:T(256)(128)(2,1)S(1)}, bf16[64]{0:T(256)(128)(2,1)}, u32[]{:S(2)}) copy-start(bf16[64]{0:T(256)(128)(2,1)} %param.20) | copy-start | bytes 388
  13.1 30.0 %copy-start.14 = (bf16[64]{0:T(256)(128)(2,1)S(1)}, bf16[64]{0:T(256)(128)(2,1)}, u32[]{:S(2)}) copy-start(bf16[64]{0:T(256)(128)(2,1)} %param.25) | copy-start | bytes 388
  13.2 30.0 %copy-start.15 = (bf16[64]{0:T(256)(128)(2,1)S(1)}, bf16[64]{0:T(256)(128)(2,1)}, u32[]{:S(2)}) copy-start(bf16[64]{0:T(256)(128)(2,1)} %param.26) | copy-start | bytes 388
  13.2 30.0 %copy-start.16 = (bf16[64]{0:T(256)(128)(2,1)S(1)}, bf16[64]{0:T(256)(128)(2,1)}, u32[]{:S(2)}) copy-start(bf16[64]{0:T(256)(128)(2,1)} %param.27) | copy-start | bytes 388
  13.2 30.0 %copy-start.17 = (bf16[64]{0:T(256)(128)(2,1)S(1)}, bf16[64]{0:T(256)(128)(2,1)}, u32[]{:S(2)}) copy-start(bf16[64]{0:T(256)(128)(2,1)} %param.28) | copy-start | bytes 388
  13.2 30.0 %copy-start.18 = (bf16[64]{0:T(256)(128)(2,1)S(1)}, bf16[64]{0:T(256)(128)(2,1)}, u32[]{:S(2)}) copy-start(bf16[64]{0:T(256)(128)(2,1)} %param.29) | copy-start | bytes 388
  13.2 30.0 %copy-start.19 = (bf16[64]{0:T(256)(128)(2,1)S(1)}, bf16[64]{0:T(256)(128)(2,1)}, u32[]{:S(2)}) copy-start(bf16[64]{0:T(256)(128)(2,1)} %param.33) | copy-start | bytes 388
  13.2 30.0 %copy-start.20 = (bf16[256]{0:T(256)(128)(2,1)S(1)}, bf16[256]{0:T(256)(128)(2,1)}, u32[]{:S(2)}) copy-start(bf16[256]{0:T(256)(128)(2,1)} %param.31) | copy-start | bytes 1540
  13.2 30.9 %copy-start.6 = (bf16[256,2048]{1,0:T(8,128)(2,1)S(1)}, bf16[256,2048]{1,0:T(8,128)(2,1)}, u32[]{:S(2)}) copy-start(bf16[256,2048]{1,0:T(8,128)(2,1)} %param.35) | copy-start | bytes 3145732
  41.1 155.6 %all-gather.9.cloned.1.call-start = ((), (), s32[]{:S(2)}) async-start(), calls=%async_computation.5 | async-start | bytes 5242880 | tf_op jit(solution)/shard_map/all_gather | solution.py:33
  41.9 225.6 %all-gather.11.cloned.1.call-start = ((), (), s32[]{:S(2)}) async-start(), calls=%async_computation.6 | async-start | bytes 5242880 | tf_op jit(solution)/shard_map/all_gather | solution.py:33
  42.5 304.7 %reduce-scatter.4.cloned.1.call-start = ((), (), s32[]{:S(2)}) async-start(), calls=%async_computation.7 | async-start | bytes 5242880 | tf_op jit(solution)/shard_map/reduce_scatter | solution.py:37
  257.6 169.1 %reduce-scatter.6.cloned.1.call-start = ((), (), s32[]{:S(2)}) async-start(), calls=%async_computation.8 | async-start | bytes 5242880 | tf_op jit(solution)/shard_map/reduce_scatter | solution.py:37
  347.2 149.1 %reduce-scatter.8.cloned.1.call-start = ((), (), s32[]{:S(2)}) async-start(), calls=%async_computation.9 | async-start | bytes 3932160 | tf_op jit(solution)/shard_map/reduce_scatter | solution.py:37
  427.8 57.8 %copy-start.5 = (bf16[256,2048]{1,0:T(8,128)(2,1)S(1)}, bf16[256,2048]{1,0:T(8,128)(2,1)}, u32[]{:S(2)}) copy-start(bf16[256,2048]{1,0:T(8,128)(2,1)} %reduce-scatter.4.cloned.1.call-done) | copy-start | bytes 3145732
  485.6 5.9 %copy-start.4 = (f32[256,2048]{1,0:T(8,128)S(1)}, f32[256,2048]{1,0:T(8,128)}, u32[]{:S(2)}) copy-start(f32[256,2048]{1,0:T(8,128)} %get-tuple-element.70.attended_ref) | copy-start | bytes 6291460
  491.5 4.8 copy-start.2
  491.5 27.2 %copy-start.8 = (f32[64,1024]{1,0:T(8,128)S(1)}, f32[64,1024]{1,0:T(8,128)}, u32[]{:S(2)}) copy-start(f32[64,1024]{1,0:T(8,128)} %get-tuple-element.103) | copy-start | bytes 786436
  491.5 28.0 %copy-start.1 = (s32[2]{0:T(128)S(1)}, s32[2]{0:T(128)}, u32[]{:S(2)}) copy-start(s32[2]{0:T(128)} %param.34) | copy-start | bytes 28
  (4 other events, 4.4 us)
Sparse Core Ops, SparseCore 0:
  9.6 30.6 all-gather.4
  41.8 63.8 all-gather.6
  107.3 79.4 all-gather.8
  188.1 79.2 all-gather.10
  269.6 75.2 reduce-scatter.3
  347.3 77.1 reduce-scatter.5
  426.8 68.2 reduce-scatter.7
